TPU v7x, 32 devices: a whole 2x2x4 slice. The times are simulated.
32 devices in a mesh: batch: 16 (over z, y, x), tensor: 2 (over core).
Axes of the slice: x: 2, y: 2, z: 4, core: 2. Of those that a mesh axis runs over, the one named last changes fastest.
Arguments:
- tokens: bfloat16 [32768, 768], P('batch'), may hold values from -6 to 6
- cotangent: bfloat16 [32768, 768], P('batch'), may hold values from -6 to 6
- phase_of: int32 [16], P('batch'), may hold values from 0 to 1
- unit_slot: int32 [144], replicated, may hold values from 0 to 287, as said below
- step_count: int32 [1], replicated, may hold values from 2 to 8
- learn_rates: float32 [5], replicated, as said below
- decay_rates: float32 [3], replicated, may hold values from 0.5 to 0.7
- master: float32 [288, 64, 768], P('batch', None, 'tensor')
- first_moment: float32 [288, 64, 768], P('batch', None, 'tensor')
- second_moment: float32 [288, 64, 768], P('batch', None, 'tensor')
- average: float32 [288, 64, 768], P('batch', None, 'tensor')
- vector_state: float32 [4, 12, 768], replicated
Outputs:
- out: bfloat16 [32768, 768], P('batch')
- input_grad: float32 [32768, 768], P('batch')
- new_master: float32 [288, 64, 768], P('batch', None, 'tensor')
- new_first: float32 [288, 64, 768], P('batch', None, 'tensor')
- new_second: float32 [288, 64, 768], P('batch', None, 'tensor')
- new_average: float32 [288, 64, 768], P('batch', None, 'tensor')
- vector_out: float32 [2, 12, 768], replicated
- vector_grads_out: float32 [2, 12, 768], replicated
- vector_second: float32 [12, 768], replicated
Inputs may be any that keep to these rules, and one draw needn't show every extreme that they name: `unit_slot`: distinct slots; slot s belongs to batch index s // 18; some batch index holds 18 blocks. `phase_of`: 1: the batch index's tokens form sequences of 512 tokens; 0: of 128. `learn_rates`: Positive.
All inputs are finite; a program needn't handle non-finite values.
Results may differ from a plain program's by a relative error of at most 0.012.
The roundings to bfloat16 on the way count: a program that leaves them out, or rounds other values in their place, can miss the bound.
Values may be sent and summed in bfloat16 or wider, within the bound.
No kernel may reach another device: no remote copies, remote signals or barrier semaphores. Data moves between devices by JAX's collectives and lax.ppermute only.
A program may use at most 192 MiB of HBM per device.

v0:
```python
import jax
import jax.numpy as jnp
from jax import lax
from jax.sharding import PartitionSpec as P

HD = 64
FF = 3072
SHORT = 128
LONG = 512


def layer_norm(centre_in, gain_row, shift_row):
    mean_rows = jnp.mean(centre_in, axis=-1, keepdims=True)
    centred = centre_in - mean_rows
    variance = jnp.mean(centred * centred, axis=-1, keepdims=True)
    return centred * lax.rsqrt(variance + 1e-12) * gain_row + shift_row


def gelu_exact(upper_in):
    return jax.nn.gelu(upper_in, approximate=False)


def product(first_mat, second_mat):
    return jnp.dot(first_mat, second_mat, preferred_element_type=jnp.float32)


def contract_rows(first_mat, second_mat):
    return lax.dot_general(
        first_mat, second_mat, (((0,), (0,)), ((), ())), preferred_element_type=jnp.float32
    )


def with_transposed(first_mat, second_mat):
    return lax.dot_general(
        first_mat, second_mat, (((1,), (1,)), ((), ())), preferred_element_type=jnp.float32
    )


def split_seqs(array_in, seq_len):
    return array_in.reshape(LONG // seq_len, seq_len, array_in.shape[1], array_in.shape[2])


def scores_of(query_seqs, key_seqs):
    return jnp.einsum(
        "bqhd,bkhd->bhqk", query_seqs, key_seqs, preferred_element_type=jnp.float32
    ) * HD ** (-0.5)


def attend_forward(queries, keys_in, values, seq_len):
    query_seqs = split_seqs(queries, seq_len)
    key_seqs = split_seqs(keys_in, seq_len)
    value_seqs = split_seqs(values, seq_len)
    scores = scores_of(query_seqs, key_seqs)
    row_max = jnp.max(scores, axis=-1, keepdims=True)
    exp_scores = jnp.exp(scores - row_max)
    row_total = jnp.sum(exp_scores, axis=-1, keepdims=True)
    weights = (exp_scores / row_total).astype(jnp.bfloat16)
    context = jnp.einsum("bhqk,bkhd->bqhd", weights, value_seqs, preferred_element_type=jnp.float32)
    log_total = (row_max + jnp.log(row_total))[..., 0]
    heads_here = queries.shape[1]
    return (
        context.reshape(LONG, heads_here, HD),
        log_total.transpose(1, 0, 2).reshape(heads_here, LONG),
    )


def attend_backward(queries, keys_in, values, log_total, grad_context, seq_len):
    query_seqs = split_seqs(queries, seq_len)
    key_seqs = split_seqs(keys_in, seq_len)
    value_seqs = split_seqs(values, seq_len)
    grad_seqs = split_seqs(grad_context, seq_len)
    heads_here = queries.shape[1]
    log_rows = log_total.reshape(heads_here, LONG // seq_len, seq_len).transpose(1, 0, 2)[..., None]
    probs_f = jnp.exp(scores_of(query_seqs, key_seqs) - log_rows)
    grad_probs = jnp.einsum(
        "bqhd,bkhd->bhqk", grad_seqs, value_seqs, preferred_element_type=jnp.float32
    )
    inner_sum = jnp.sum(probs_f * grad_probs, axis=-1, keepdims=True)
    grad_scores = (probs_f * (grad_probs - inner_sum)).astype(jnp.bfloat16)
    grad_query = jnp.einsum(
        "bhqk,bkhd->bqhd", grad_scores, key_seqs, preferred_element_type=jnp.float32
    ) * HD ** (-0.5)
    grad_key = jnp.einsum(
        "bhqk,bqhd->bkhd", grad_scores, query_seqs, preferred_element_type=jnp.float32
    ) * HD ** (-0.5)
    grad_value = jnp.einsum(
        "bhqk,bqhd->bkhd",
        probs_f.astype(jnp.bfloat16),
        grad_seqs,
        preferred_element_type=jnp.float32,
    )
    return (
        grad_query.reshape(LONG, heads_here, HD).astype(jnp.bfloat16),
        grad_key.reshape(LONG, heads_here, HD).astype(jnp.bfloat16),
        grad_value.reshape(LONG, heads_here, HD).astype(jnp.bfloat16),
    )


def slot_lookup(unit_slot, slot_ids):
    matches = unit_slot[None, :] == slot_ids[:, None]
    unit_ids = jnp.arange(unit_slot.shape[0], dtype=jnp.int32)
    unit_index = jnp.sum(jnp.where(matches, unit_ids[None, :], 0), axis=1)
    return (unit_index, jnp.any(matches, axis=1))


def adamw_update(
    weights_in, moment, square, average_in, gradient, rate_all, decay_rates, step_count
):
    count_f = step_count[0].astype(jnp.float32)
    beta_one = decay_rates[0]
    beta_two = decay_rates[1]
    ema_decay = decay_rates[2]
    moment_new = beta_one * moment + (1.0 - beta_one) * gradient
    square_new = beta_two * square + (1.0 - beta_two) * gradient * gradient
    moment_hat = moment_new / (1.0 - beta_one**count_f)
    square_hat = square_new / (1.0 - beta_two**count_f)
    weights_new = weights_in - rate_all * (
        moment_hat / (jnp.sqrt(square_hat) + 1e-08) + 0.01 * weights_in
    )
    average_new = ema_decay * average_in + (1.0 - ema_decay) * weights_new
    return (weights_new, moment_new, square_new, average_new)


def on_device(
    tokens,
    cotangent,
    phase_of,
    unit_slot,
    step_count,
    learn_rates,
    decay_rates,
    master,
    first_moment,
    second_moment,
    average,
    vector_state,
):
    own_slots, unit_rows, unit_cols = master.shape
    tok_rows, model_width = tokens.shape
    batch_count = lax.axis_size("batch")
    row_blocks = model_width // unit_rows
    col_blocks = FF // model_width
    half_ff = col_blocks * unit_cols
    heads_here = unit_cols // HD
    groups = tok_rows // LONG
    tensor_at = lax.axis_index("tensor")
    batch_at = lax.axis_index("batch")
    low_master = master.astype(jnp.bfloat16)
    every_slot = lax.all_gather(low_master, "batch", axis=0, tiled=True)
    unit_blocks = jnp.take(every_slot, unit_slot, axis=0)

    def narrow(first_unit):
        return unit_blocks[first_unit : first_unit + row_blocks].reshape(model_width, unit_cols)

    def widened(first_unit):
        blocks = unit_blocks[first_unit : first_unit + row_blocks * col_blocks]
        return (
            blocks.reshape(row_blocks, col_blocks, unit_rows, unit_cols)
            .transpose(0, 2, 1, 3)
            .reshape(model_width, half_ff)
        )

    w_query = narrow(0)
    w_key = narrow(row_blocks)
    w_value = narrow(2 * row_blocks)
    w_out = narrow(3 * row_blocks)
    w_up = widened(4 * row_blocks)
    w_down = widened(4 * row_blocks + row_blocks * col_blocks)
    vectors = vector_state[0]
    col_start = tensor_at * unit_cols
    bias_query = lax.dynamic_slice_in_dim(vectors[0], col_start, unit_cols)
    bias_value = lax.dynamic_slice_in_dim(vectors[1], col_start, unit_cols)
    bias_up = lax.dynamic_slice_in_dim(vectors[5:9].reshape(FF), tensor_at * half_ff, half_ff)
    queries = (product(tokens, w_query) + bias_query).astype(jnp.bfloat16)
    keys_all = product(tokens, w_key).astype(jnp.bfloat16)
    values = (product(tokens, w_value) + bias_value).astype(jnp.bfloat16)
    shape_heads = (groups, LONG, heads_here, HD)
    long_phase = phase_of[0] == 1

    def forward_group(operands):
        return lax.cond(
            long_phase,
            lambda: attend_forward(*operands, LONG),
            lambda: attend_forward(*operands, SHORT),
        )

    head_inputs = (
        queries.reshape(shape_heads),
        keys_all.reshape(shape_heads),
        values.reshape(shape_heads),
    )
    context, log_total = lax.map(forward_group, head_inputs)
    context_low = context.reshape(tok_rows, unit_cols).astype(jnp.bfloat16)
    attended = lax.psum(with_transposed(context_low, w_out), "tensor")
    inputs = tokens.astype(jnp.float32)
    hidden_one, norm_one_back = jax.vjp(
        layer_norm, inputs + attended + vectors[2], vectors[3], vectors[4]
    )
    hidden_low = hidden_one.astype(jnp.bfloat16)
    upper_in = product(hidden_low, w_up) + bias_up
    activated, gelu_back = jax.vjp(gelu_exact, upper_in)
    active_low = activated.astype(jnp.bfloat16)
    branch = lax.psum(with_transposed(active_low, w_down), "tensor")
    output_f, norm_two_back = jax.vjp(
        layer_norm, hidden_one + branch + vectors[9], vectors[10], vectors[11]
    )
    grad_two, grad_gain_two, grad_shift_two = norm_two_back(cotangent.astype(jnp.float32))
    grad_branch = grad_two.astype(jnp.bfloat16)
    grad_down = contract_rows(grad_branch, active_low)
    grad_active = product(grad_branch, w_down)
    (grad_upper,) = gelu_back(grad_active)
    upper_low = grad_upper.astype(jnp.bfloat16)
    grad_up = contract_rows(hidden_low, upper_low)
    grad_hidden = grad_two + lax.psum(with_transposed(upper_low, w_up), "tensor")
    grad_one, grad_gain_one, grad_shift_one = norm_one_back(grad_hidden)
    grad_attended = grad_one.astype(jnp.bfloat16)
    grad_out = contract_rows(grad_attended, context_low)
    grad_context = product(grad_attended, w_out).astype(jnp.bfloat16)

    def backward_group(operands):
        return lax.cond(
            long_phase,
            lambda: attend_backward(*operands, LONG),
            lambda: attend_backward(*operands, SHORT),
        )

    grad_heads = lax.map(
        backward_group, head_inputs + (log_total, grad_context.reshape(shape_heads))
    )
    grad_queries = grad_heads[0].reshape(tok_rows, unit_cols)
    grad_keys = grad_heads[1].reshape(tok_rows, unit_cols)
    grad_values = grad_heads[2].reshape(tok_rows, unit_cols)
    grad_wq = contract_rows(tokens, grad_queries)
    grad_wk = contract_rows(tokens, grad_keys)
    grad_wv = contract_rows(tokens, grad_values)
    partial_input = (
        with_transposed(grad_queries, w_query)
        + with_transposed(grad_keys, w_key)
        + with_transposed(grad_values, w_value)
    )
    input_grad = grad_one + lax.psum(partial_input, "tensor")
    head_sums = jnp.stack(
        [
            jnp.sum(grad_queries, axis=0, dtype=jnp.float32),
            jnp.sum(grad_values, axis=0, dtype=jnp.float32),
        ]
    )
    split_rows = lax.dynamic_update_slice_in_dim(
        jnp.zeros((2, model_width), jnp.float32), head_sums, col_start, 1
    )
    up_rows = lax.dynamic_update_slice_in_dim(
        jnp.zeros((FF,), jnp.float32),
        jnp.sum(upper_low, axis=0, dtype=jnp.float32),
        tensor_at * half_ff,
        0,
    )
    shared = 0.5 * jnp.stack([jnp.sum(grad_one, axis=0), grad_gain_one, grad_shift_one])
    tail_rows = 0.5 * jnp.stack([jnp.sum(grad_two, axis=0), grad_gain_two, grad_shift_two])
    partial_vectors = jnp.concatenate(
        [split_rows, shared, up_rows.reshape(FF // model_width, model_width), tail_rows], axis=0
    )
    vector_grads = lax.psum(partial_vectors, ("batch", "tensor"))

    def narrow_back(grad_mat):
        return grad_mat.reshape(row_blocks, unit_rows, unit_cols)

    def wide_back(grad_mat):
        return (
            grad_mat.reshape(row_blocks, unit_rows, col_blocks, unit_cols)
            .transpose(0, 2, 1, 3)
            .reshape(row_blocks * col_blocks, unit_rows, unit_cols)
        )

    unit_grads = jnp.concatenate(
        [
            narrow_back(grad_wq),
            narrow_back(grad_wk),
            narrow_back(grad_wv),
            narrow_back(grad_out),
            wide_back(grad_up),
            wide_back(grad_down),
        ],
        axis=0,
    )
    row_index, row_used = slot_lookup(
        unit_slot, jnp.arange(own_slots * lax.axis_size("batch"), dtype=jnp.int32)
    )
    slot_grads = lax.psum_scatter(
        jnp.where(row_used[:, None, None], jnp.take(unit_grads, row_index, axis=0), 0.0),
        "batch",
        scatter_dimension=0,
        tiled=True,
    )
    my_ids = batch_at * own_slots + jnp.arange(own_slots, dtype=jnp.int32)
    unit_index, occupied = slot_lookup(unit_slot, my_ids)
    kind_sum = (
        (unit_index >= 3 * row_blocks).astype(jnp.int32)
        + (unit_index >= 4 * row_blocks).astype(jnp.int32)
        + (unit_index >= 4 * row_blocks + row_blocks * col_blocks).astype(jnp.int32)
    )
    slot_kinds = jnp.where(occupied, kind_sum, 0)
    kind_ids = jnp.arange(4, dtype=jnp.int32)
    slot_rates = jnp.sum(
        jnp.where(slot_kinds[:, None] == kind_ids[None, :], learn_rates[None, :4], 0.0), axis=1
    )[:, None, None]
    new_master, new_first, new_second, new_average = adamw_update(
        master,
        first_moment,
        second_moment,
        average,
        slot_grads,
        slot_rates,
        decay_rates,
        step_count,
    )
    grads_scaled = vector_grads * float(tok_rows * batch_count) ** (-0.5)
    vec_weights, vec_first, vec_second, vec_average = adamw_update(
        vector_state[0],
        vector_state[1],
        vector_state[2],
        vector_state[3],
        grads_scaled,
        learn_rates[4],
        decay_rates,
        step_count,
    )
    return (
        output_f.astype(jnp.bfloat16),
        input_grad,
        new_master,
        new_first,
        new_second,
        new_average,
        jnp.stack([vec_weights, vec_average]),
        jnp.stack([grads_scaled, vec_first]),
        vec_second,
    )


def solution(mesh):
    return jax.shard_map(
        on_device,
        mesh=mesh,
        in_specs=(
            P("batch", None),
            P("batch", None),
            P("batch"),
            P(),
            P(),
            P(),
            P(),
            P("batch", None, "tensor"),
            P("batch", None, "tensor"),
            P("batch", None, "tensor"),
            P("batch", None, "tensor"),
            P(),
        ),
        out_specs=(
            P("batch", None),
            P("batch", None),
            P("batch", None, "tensor"),
            P("batch", None, "tensor"),
            P("batch", None, "tensor"),
            P("batch", None, "tensor"),
            P(),
            P(),
            P(),
        ),
        check_vma=False,
    )
```

profile of v0, /device:TPU:0, one launch (start us, length us, event | category | flops | bytes accessed | tf_op | source)
XLA Modules:
  0.0 1166.1 jit_solution(7713774288152220641)
XLA Ops:
  13.4 167.6 %all-gather.2.cloned.1.call-done = bf16[288,64,384]{2,1,0:T(8,128)(2,1)} async-done(((bf16[18,64,384]{2,1,0:T(8,128)(2,1)}), bf16[288,64,384]{2,1,0:T(8,128)(2,1)}) %all-gather.2.cloned.1.call-update) | async-done | bytes 14155792 | tf_op jit(solution)/shard_map/all_gather | solution.py:149
  181.0 14.3 %gather_fusion = bf16[144,64,384]{2,1,0:T(8,128)(2,1)} fusion(bf16[288,64,384]{2,1,0:T(8,128)(2,1)} %all-gather.2.cloned.1.call-done, s32[1024]{0:T(1024)S(1)} %pad_clamp_fusion.1), kind=kCustom, calls=%fused_computation | custom fusion | bytes 14156352 | tf_op jit(solution)/shard_map/jit(_take)/gather | solution.py:150
  229.0 43.2 %while.26 = (s32[]{:T(128)}, bf16[4,512,6,64]{1,3,2,0:T(8,128)(2,1)}, f32[4,6,512]{2,1,0:T(8,128)}, pred[]{:T(512)}, bf16[4,512,6,64]{1,3,2,0:T(8,128)(2,1)}, /*...) while((s32[]{:T(128)}, bf16[4,512,6,64]{1,3,2,0:T(8,128)(2,1)}, ...), condition=%wide.region_7.8_spmd, body=%wide.region_0.7_spmd.sunk | while | flops 416805888 | bytes 25293988 | solution.py:192
  292.6 18.8 %all-reduce.5.cloned.1.call-done = f32[2048,768]{1,0:T(8,128)} async-done(((f32[2048,768]{1,0:T(8,128)}), f32[2048,768]{1,0:T(8,128)}) %all-reduce.5.cloned.1.call-update) | async-done | bytes 6291472 | tf_op jit(solution)/shard_map/psum | solution.py:194
  318.6 34.0 %multiply_convert_fusion.2 = (bf16[2048,1536]{1,0:T(8,128)(2,1)S(1)}, f32[2048,1536]{1,0:T(8,128)}, f32[2048,1536]{1,0:T(8,128)}) fusion(f32[1536]{0:T(1024)S(1)} %dynamic_slice.37, bf16[768,1536]{1,0:T(8,128)(2,1)S(1)} %bitcast.296, f32[2048,768]{1,0:T(8,128)S(1)} %get-tuple-element.368, f32[768]{0:T(1024)S(1)} %get-tuple-element.313, ...), kind=kOutput, calls=%fused_computation.68 | convolution fusion | flops 5047320576 | bytes 40136704 | tf_op jit(solution)/shard_map/dot_general | solution.py:24
  355.2 6.9 fusion.94
  362.2 33.3 %all-reduce.7.cloned.1.call-done = f32[2048,768]{1,0:T(8,128)} async-done(((f32[2048,768]{1,0:T(8,128)}), f32[2048,768]{1,0:T(8,128)}) %all-reduce.7.cloned.1.call-update) | async-done | bytes 6291472 | tf_op jit(solution)/shard_map/psum | solution.py:203
  410.8 18.9 %convert_reduce_fusion = (f32[1536]{0:T(1024)}, bf16[2048,1536]{1,0:T(8,128)(2,1)}) fusion(f32[2048,1536]{1,0:T(8,128)} %get-tuple-element.366, bf16[768,1536]{1,0:T(8,128)(2,1)} %bitcast.297, f32[2048,768]{1,0:T(8,128)S(1)} %get-tuple-element.362, f32[2048]{0:T(1024)S(1)} %negate_multiply_fusion.2, f32[2048,1536]{1,0:T(8,128)} %get-tuple-element.405, ...), kind=kOutput, calls=%fused_computation.66 | convolution fusion | flops 4888459776 | bytes 40128512 | tf_op jit(solution)/shard_map/dot_general | solution.py:24
  429.7 9.5 fusion.95
  439.4 33.3 %all-reduce.9.cloned.1.call-done = f32[2048,768]{1,0:T(8,128)} async-done(((f32[2048,768]{1,0:T(8,128)}), f32[2048,768]{1,0:T(8,128)}) %all-reduce.9.cloned.1.call-update) | async-done | bytes 6291472 | tf_op jit(solution)/shard_map/psum | solution.py:214
  472.6 8.9 multiply_reduce_fusion.3
  493.9 86.6 %while.27 = (s32[]{:T(128)}, bf16[4,512,6,64]{1,3,2,0:T(8,128)(2,1)}, bf16[4,512,6,64]{1,3,2,0:T(8,128)(2,1)}, bf16[4,512,6,64]{1,3,2,0:T(8,128)(2,1)}, pred[]{:...) while((s32[]{:T(128)}, ...), condition=%wide.region_24.25_spmd, body=%wide.region_19.24_spmd.sunk | while | flops 1026487296 | bytes 56710844 | solution.py:227
  497.4 16.1 %conditional.5 = (bf16[1,512,6,64]{1,3,2,0:T(8,128)(2,1)S(1)}, bf16[1,512,6,64]{1,3,2,0:T(8,128)(2,1)S(1)}, bf16[1,512,6,64]{1,3,2,0:T(8,128)(2,1)S(1)}) conditional(s32[]{:T(128)} %convert_element_type.324, (bf16[512,6,64]{0,2,1:T(8,128)(2,1)S(1)}, bf16[512,6,64]{0,2,1:T(8,128)(2,1)S(1)}, f32[6,512]{1,0:T(8,128)S(1)}, ...), branch_computations={%region_20.21_spmd, %region_22.23_spmd} | conditional | flops 1026487296 | bytes 51179544 | solution.py:221
  519.0 16.1 %conditional.5 = (bf16[1,512,6,64]{1,3,2,0:T(8,128)(2,1)S(1)}, bf16[1,512,6,64]{1,3,2,0:T(8,128)(2,1)S(1)}, bf16[1,512,6,64]{1,3,2,0:T(8,128)(2,1)S(1)}) conditional(s32[]{:T(128)} %convert_element_type.324, (bf16[512,6,64]{0,2,1:T(8,128)(2,1)S(1)}, bf16[512,6,64]{0,2,1:T(8,128)(2,1)S(1)}, f32[6,512]{1,0:T(8,128)S(1)}, ...), branch_computations={%region_20.21_spmd, %region_22.23_spmd} | conditional | flops 1026487296 | bytes 51179544 | solution.py:221
  540.5 16.0 %conditional.5 = (bf16[1,512,6,64]{1,3,2,0:T(8,128)(2,1)S(1)}, bf16[1,512,6,64]{1,3,2,0:T(8,128)(2,1)S(1)}, bf16[1,512,6,64]{1,3,2,0:T(8,128)(2,1)S(1)}) conditional(s32[]{:T(128)} %convert_element_type.324, (bf16[512,6,64]{0,2,1:T(8,128)(2,1)S(1)}, bf16[512,6,64]{0,2,1:T(8,128)(2,1)S(1)}, f32[6,512]{1,0:T(8,128)S(1)}, ...), branch_computations={%region_20.21_spmd, %region_22.23_spmd} | conditional | flops 1026487296 | bytes 51179544 | solution.py:221
  562.0 16.0 %conditional.5 = (bf16[1,512,6,64]{1,3,2,0:T(8,128)(2,1)S(1)}, bf16[1,512,6,64]{1,3,2,0:T(8,128)(2,1)S(1)}, bf16[1,512,6,64]{1,3,2,0:T(8,128)(2,1)S(1)}) conditional(s32[]{:T(128)} %convert_element_type.324, (bf16[512,6,64]{0,2,1:T(8,128)(2,1)S(1)}, bf16[512,6,64]{0,2,1:T(8,128)(2,1)S(1)}, f32[6,512]{1,0:T(8,128)S(1)}, ...), branch_computations={%region_20.21_spmd, %region_22.23_spmd} | conditional | flops 1026487296 | bytes 51179544 | solution.py:221
  599.7 10.9 fusion.73
  622.8 11.5 fusion.75
  669.0 8.1 add_reduce_fusion
  693.6 31.7 %gather_fusion.1 = f32[288,64,384]{2,1,0:T(8,128)} fusion(f32[144,64,384]{2,1,0:T(8,128)} %constant_dynamic-update-slice_fusion.5, s32[1024]{0:T(1024)S(1)} %pad_clamp_fusion), kind=kCustom, calls=%fused_computation.1 | custom fusion | bytes 56624256 | tf_op jit(solution)/shard_map/jit(_take)/gather | solution.py:289
  725.2 23.1 %select_select_fusion = f32[288,64,384]{2,1,0:T(8,128)} fusion(f32[288,64,384]{2,1,0:T(8,128)} %gather_fusion.1, pred[288]{0:T(512)(128)(4,1)S(1)} %compare_and_fusion, pred[288]{0:T(512)(128)(4,1)S(1)} %fusion.53), kind=kLoop, calls=%fused_computation.63 | loop fusion | flops 14155776 | bytes 56623680 | tf_op jit(solution)/shard_map/jit(_where)/select_n | solution.py:289
  758.6 43.4 %psum.39 = f32[12,768]{1,0:T(8,128)S(1)} all-reduce(f32[12,768]{1,0:T(8,128)S(1)} %pad_maximum_fusion.2), channel_id=1, replica_groups=mesh['batch'=16,'tensor'=2] {'batch','tensor'}, use_global_device_ids=true, to_apply=%region_41.42 | all-reduce | flops 9216 | bytes 73728 | tf_op jit(solution)/shard_map/psum | solution.py:262
  807.4 342.3 %reduce-scatter.2.cloned.1.call-done = f32[18,64,384]{2,1,0:T(8,128)} async-done(((f32[288,64,384]{2,1,0:T(8,128)}), f32[18,64,384]{2,1,0:T(8,128)}) %reduce-scatter.2.cloned.1.call-update) | async-done | bytes 1769488 | tf_op jit(solution)/shard_map/reduce_scatter | solution.py:288
  1149.7 9.1 multiply_add_fusion.1
  (453 shorter events, 344.3 us)
Async XLA Ops:
  7.2 173.8 %all-gather.2.cloned.1.call-start = ((), (), s32[]{:S(2)}) async-start(), calls=%async_computation.1 | async-start | bytes 15040512 | tf_op jit(solution)/shard_map/all_gather | solution.py:149
  9.8 301.6 %all-reduce.5.cloned.1.call-start = ((), (), s32[]{:S(2)}) async-start(), calls=%async_computation.2 | async-start | bytes 12582912 | tf_op jit(solution)/shard_map/psum | solution.py:194
  12.0 383.6 %copy-start.55 = (f32[768]{0:T(1024)}, f32[768]{0:T(1024)S(1)}, u32[]{:S(2)}) copy-start(f32[768]{0:T(1024)S(1)} %get-tuple-element.313) | copy-start | bytes 9220
  12.0 469.6 %copy-start.44 = (f32[768]{0:T(1024)}, f32[768]{0:T(1024)S(1)}, u32[]{:S(2)}) copy-start(f32[768]{0:T(1024)S(1)} %get-tuple-element.314) | copy-start | bytes 9220
  195.3 8.9 copy-start.24
  203.4 16.8 %copy-start.31 = (bf16[12,64,384]{2,1,0:T(8,128)(2,1)}, bf16[12,64,384]{2,1,0:T(8,128)(2,1)S(1)}, u32[]{:S(2)}) copy-start(bf16[12,64,384]{2,1,0:T(8,128)(2,1)S(1)} %get-tuple-element.387) | copy-start | bytes 1769476
  281.1 114.5 %all-reduce.7.cloned.1.call-start = ((), (), s32[]{:S(2)}) async-start(), calls=%async_computation.3 | async-start | bytes 12582912 | tf_op jit(solution)/shard_map/psum | solution.py:203
  287.1 24.3 %copy-start.25 = (bf16[2048,768]{1,0:T(8,128)(2,1)S(1)}, bf16[2048,768]{1,0:T(8,128)(2,1)}, u32[]{:S(2)}) copy-start(bf16[2048,768]{1,0:T(8,128)(2,1)} %param.20) | copy-start | bytes 9437188
  315.1 37.4 %copy-start.1 = (f32[2048,768]{1,0:T(8,128)}, f32[2048,768]{1,0:T(8,128)S(1)}, u32[]{:S(2)}) copy-start(f32[2048,768]{1,0:T(8,128)S(1)} %get-tuple-element.368) | copy-start | bytes 18874372
  315.1 166.5 %copy-start.38 = (f32[2048]{0:T(1024)}, f32[2048]{0:T(1024)S(1)}, u32[]{:S(2)}) copy-start(f32[2048]{0:T(1024)S(1)} %broadcast_multiply_fusion.1) | copy-start | bytes 24580
  316.0 165.6 %copy-start.40 = (f32[2048]{0:T(1024)}, f32[2048]{0:T(1024)S(1)}, u32[]{:S(2)}) copy-start(f32[2048]{0:T(1024)S(1)} %fusion.67) | copy-start | bytes 24580
  318.5 36.7 %copy-start.36 = (bf16[96,8,4,384]{3,1,2,0:T(8,128)(2,1)S(1)}, bf16[96,8,4,384]{3,1,2,0:T(8,128)(2,1)}, u32[]{:S(2)}) copy-start(bf16[96,8,4,384]{3,1,2,0:T(8,128)(2,1)} %copy.261) | copy-start | bytes 7077892
  362.1 33.4 %copy-start.57 = (f32[768]{0:T(1024)S(1)}, f32[768]{0:T(1024)}, u32[]{:S(2)}) copy-start(f32[768]{0:T(1024)} %get-tuple-element.312) | copy-start | bytes 9220
  362.2 110.5 %all-reduce.9.cloned.1.call-start = ((), (), s32[]{:S(2)}) async-start(), calls=%async_computation.4 | async-start | bytes 12582912 | tf_op jit(solution)/shard_map/psum | solution.py:214
  410.8 18.9 %copy-start.8 = (f32[2048,768]{1,0:T(8,128)}, f32[2048,768]{1,0:T(8,128)S(1)}, u32[]{:S(2)}) copy-start(f32[2048,768]{1,0:T(8,128)S(1)} %get-tuple-element.362) | copy-start | bytes 18874372
  410.8 61.8 %copy-start.49 = (f32[2048]{0:T(1024)}, f32[2048]{0:T(1024)S(1)}, u32[]{:S(2)}) copy-start(f32[2048]{0:T(1024)S(1)} %negate_multiply_fusion.2) | copy-start | bytes 24580
  439.3 229.7 %all-reduce.11.cloned.1.call-start = ((), (), s32[]{:S(2)}) async-start(), calls=%async_computation.5 | async-start | bytes 12582912 | tf_op jit(solution)/shard_map/psum | solution.py:241
  439.4 42.2 %copy-start.43 = (f32[2048]{0:T(1024)S(1)}, f32[2048]{0:T(1024)}, u32[]{:S(2)}) copy-start(f32[2048]{0:T(1024)} %copy-done.42) | copy-start | bytes 24580
  598.8 550.9 %reduce-scatter.2.cloned.1.call-start = ((), (), s32[]{:S(2)}) async-start(), calls=%async_computation.6 | async-start | bytes 30081024 | tf_op jit(solution)/shard_map/reduce_scatter | solution.py:288
  610.7 12.1 %slice-start = ((s8[6291456]{0:T(1024)(128)(4,1)}), s8[2097152]{0:T(1024)(128)(4,1)S(1)}, s32[]{:S(2)}) async-start(s8[6291456]{0:T(1024)(128)(4,1)} %bitcast.251), calls=%async_computation.7 | async-start | bytes 4194304
  648.5 9.8 copy-start.19
  655.6 8.7 copy-start.23
  677.0 9.8 slice-start.4
  748.5 401.2 %copy-start.17 = (f32[18,64,384]{2,1,0:T(8,128)S(1)}, f32[18,64,384]{2,1,0:T(8,128)}, u32[]{:S(2)}) copy-start(f32[18,64,384]{2,1,0:T(8,128)} %param.27) | copy-start | bytes 5308420
  (66 other events, 260.2 us)
Sparse Core Ops, SparseCore 0:
  11.4 169.5 all-gather.1
  281.2 30.1 all-reduce.4
  362.3 33.2 all-reduce.6
  439.4 33.2 all-reduce.8
  598.9 33.2 all-reduce.10
  748.6 401.0 reduce-scatter.1
where the time goes:
time: 1180 us; the launch traced here: 1170 us
  waiting for transfers between devices  595 us (50%)
  local copies, waits for them, and re-layouts  247 us (21%)
  matrix products  168 us (14%)
  other arithmetic  89.6 us (8%)
  blocking collectives  43.4 us (4%)
  between operations  20.2 us (2%)
    reduce_scatter x1, waiting for transfers between devices, on_device(): lax.psum_scatter(jnp.where(row_used[:, None, None], jnp.take(unit_grads,...  342 us
    all_gather x1, waiting for transfers between devices, on_device(): every_slot = lax.all_gather(low_master, 'batch', axis=0, tiled=True)  168 us
    dot_general x6, matrix products, product(): return jnp.dot(first_mat, second_mat, preferred_element_type=jnp.float32)  66.4 us
    psum x1, blocking collectives, on_device(): vector_grads = lax.psum(partial_vectors, ('batch', 'tensor'))  43.4 us
    dot_general x6, matrix products, contract_rows(): lax.dot_general(first_mat, second_mat, (((0,), (0,)), ((), ())), preferre...  38.3 us
    unnamed x140, local copies, waits for them, and re-layouts  33.3 us
    psum x1, waiting for transfers between devices, on_device(): branch = lax.psum(with_transposed(active_low, w_down), 'tensor')  33.3 us
    psum x1, waiting for transfers between devices, on_device(): lax.psum(with_transposed(upper_low, w_up), 'tensor')  33.3 us
  transfers between devices with their start and end apart: 6, of which 5 were waited for; matrix products, arithmetic and copies ran while one was open for 8% of the time, Pallas kernels for 0%

commit v1 on v0

v1 whole, which is shorter than its diff:
```python
import functools

import jax
import jax.numpy as jnp
from jax import lax
from jax.experimental import pallas as pl
from jax.experimental.pallas import tpu as pltpu
from jax.sharding import PartitionSpec as P

HD = 64
FF = 3072
SHORT = 128
LONG = 512
EPS = 1e-12
BF = jnp.bfloat16
F32 = jnp.float32
VMEM_BYTES = 60 * 2**20
BOTH = ("batch", "tensor")
ANY = pl.BlockSpec(memory_space=pl.ANY)
PLANES = 4
FAST_BATCH = 16


def dot(first_mat, second_mat):
    return lax.dot_general(
        first_mat, second_mat, (((1,), (0,)), ((), ())), preferred_element_type=F32
    )


def dot_nt(first_mat, second_mat):
    return lax.dot_general(
        first_mat, second_mat, (((1,), (1,)), ((), ())), preferred_element_type=F32
    )


def normalized(rows):
    centred = rows - jnp.mean(rows, axis=-1, keepdims=True)
    inverse = lax.rsqrt(jnp.mean(centred * centred, axis=-1, keepdims=True) + EPS)
    return centred * inverse, inverse


def norm_back(grad_scaled, normal, inverse):
    mean_grad = jnp.mean(grad_scaled, axis=-1, keepdims=True)
    mean_both = jnp.mean(grad_scaled * normal, axis=-1, keepdims=True)
    return inverse * (grad_scaled - mean_grad - normal * mean_both)


def row_sum(array_in):
    return jnp.sum(array_in, axis=0, keepdims=True)


def load_blocks(mine_ref, theirs_ref, blocks, weight_ref, sem_ref):
    cols = mine_ref.shape[2]
    copies = []
    for spot, (half, block) in enumerate(blocks):
        source = (mine_ref, theirs_ref)[half]
        copies.append(
            pltpu.make_async_copy(
                source.at[block],
                weight_ref.at[:, pl.ds(spot * cols, cols)],
                sem_ref.at[spot],
            )
        )
    return copies


PAIRED = [(half, block) for block in range(4) for half in range(2)]
HALVED = [(half, block) for half in range(2) for block in range(4)]


def call(kernel, grid, in_specs, out_specs, out_shape, scratch, prefetch, flops, moved, exps=0):
    return pl.pallas_call(
        kernel,
        out_shape=out_shape,
        grid_spec=pltpu.PrefetchScalarGridSpec(
            num_scalar_prefetch=prefetch,
            grid=grid,
            in_specs=in_specs,
            out_specs=out_specs,
            scratch_shapes=scratch,
        ),
        compiler_params=pltpu.CompilerParams(vmem_limit_bytes=VMEM_BYTES),
        cost_estimate=pl.CostEstimate(
            flops=flops, bytes_accessed=moved, transcendentals=exps
        ),
    )


def struct(shape, kind):
    return jax.ShapeDtypeStruct(shape, kind)


def spread_kernel(base, row_step, block_step, cap, rows, info_ref, slot_ref, master_ref, *outs):
    block = pl.program_id(0)
    for out_ref, half in zip(outs, (1 - info_ref[0], info_ref[0])):
        count = out_ref.shape[1] // rows
        for step in range(count):
            unit = base + (half * count + step) * row_step + block * block_step
            local = slot_ref[unit] - info_ref[1]
            own = (local >= 0) & (local < cap)
            spot = pl.ds(step * rows, rows)

            @pl.when(own)
            def _():
                out_ref[0, spot, :] = master_ref[local].astype(BF)

            @pl.when(jnp.logical_not(own))
            def _():
                out_ref[0, spot, :] = jnp.zeros((rows, out_ref.shape[2]), BF)


def spread(master, unit_slot, info, chunk):
    cap, rows, cols = master.shape
    base, row_step, block_step = chunk
    half_rows = 6 * rows
    shape = struct((4, half_rows, cols), BF)
    block = pl.BlockSpec((1, half_rows, cols), lambda i, *_: (i, 0, 0))
    return call(
        functools.partial(spread_kernel, base, row_step, block_step, cap, rows),
        (4,),
        [pl.BlockSpec((cap, rows, cols), lambda i, *_: (0, 0, 0))],
        [block, block],
        [shape, shape],
        [],
        2,
        0,
        8 * 2**20,
    )(info, unit_slot, master)


def swap_pairs(orient, stage):
    pairs = []
    for place in range(FAST_BATCH):
        for core in range(2):
            first_bit = 2 if (core + orient) % 2 == 0 else 1
            bit = first_bit if stage == 1 else 3 - first_bit
            pairs.append((place * 2 + core, (place ^ bit) * 2 + core))
    return pairs


def plane_pairs(step):
    return [
        (place * 2 + core, (place + 4 * step) % FAST_BATCH * 2 + core)
        for place in range(FAST_BATCH)
        for core in range(2)
    ]


def cut(array_in, start, size):
    return lax.dynamic_slice_in_dim(array_in, start, size, 1)


def total(*terms):
    result = terms[0].astype(F32)
    for term in terms[1:]:
        result = result + term.astype(F32)
    return result.astype(BF)


def packed(parts):
    if len(parts) == 1:
        return parts[0]
    return jnp.concatenate([part.reshape(-1, part.shape[2]) for part in parts], axis=0)


def unpacked(array_in, likes):
    if len(likes) == 1:
        return [array_in]
    at, parts = 0, []
    for like in likes:
        count = like.shape[0] * like.shape[1]
        parts.append(array_in[at : at + count].reshape(like.shape))
        at += count
    return parts


def send(parts, pairs):
    return unpacked(lax.ppermute(packed(parts), BOTH, pairs), parts)


def reduce_parts(sends, keeps, orient, where):
    first_at, second_at, plane = where
    got_one = send(sends, swap_pairs(orient, 1))
    halves = [keep.shape[1] // 2 for keep in keeps]
    outgoing = [
        total(cut(keep, (1 - second_at) * half, half), cut(one, (1 - second_at) * half, half))
        for keep, one, half in zip(keeps, got_one, halves)
    ]
    got_two = send(outgoing, swap_pairs(orient, 2))

    def local(which):
        return [
            (
                cut(keep, second_at * half + which * (half // PLANES), half // PLANES),
                cut(one, second_at * half + which * (half // PLANES), half // PLANES),
                cut(two, which * (half // PLANES), half // PLANES),
            )
            for keep, one, two, half in zip(keeps, got_one, got_two, halves)
        ]

    arrived = []
    for step in range(1, PLANES):
        pieces = [total(*terms) for terms in local((plane + step) % PLANES)]
        arrived.append(send(pieces, plane_pairs(step)))
    return [
        total(*terms, *[pieces[at] for pieces in arrived])
        for at, terms in enumerate(local(plane))
    ]


def join(flag, here, there):
    low_first = flag == 0
    return jnp.concatenate(
        [jnp.where(low_first, here, there), jnp.where(low_first, there, here)], axis=1
    )


def gather_parts(owned, orient, where):
    first_at, second_at, plane = where
    pieces = [owned] + [send(owned, plane_pairs(step)) for step in range(1, PLANES)]
    level = []
    for at in range(len(owned)):
        choices = [piece[at] for piece in pieces]
        level.append(
            jnp.concatenate(
                [
                    lax.select_n((plane - row) % PLANES, *choices)
                    for row in range(PLANES)
                ],
                axis=1,
            )
        )
    level = [
        join(second_at, here, there)
        for here, there in zip(level, send(level, swap_pairs(orient, 2)))
    ]
    return [
        join(first_at, here, there)
        for here, there in zip(level, send(level, swap_pairs(orient, 1)))
    ]


def core_swap(array_in):
    return lax.ppermute(array_in, "tensor", [(0, 1), (1, 0)])


def seen_mask():
    key_at = lax.broadcasted_iota(jnp.int32, (LONG, LONG), 0) // SHORT
    query_at = lax.broadcasted_iota(jnp.int32, (LONG, LONG), 1) // SHORT
    return key_at == query_at


def low_lanes(rows):
    return lax.broadcasted_iota(jnp.int32, (rows, 2 * HD), 1) < HD


def pair_lanes(pair):
    return pl.ds(pl.multiple_of(pair * 2 * HD, 2 * HD), 2 * HD)


def head_part(array_in, head):
    lanes = low_lanes(array_in.shape[0])
    keep = lanes if head == 0 else jnp.logical_not(lanes)
    return jnp.where(keep, array_in, jnp.zeros_like(array_in))


def attend_pair(pair, short, q_ref, k_ref, v_ref, ctx_ref, lse_ref):
    lanes = pair_lanes(pair)
    queries = q_ref[:, lanes] * BF(HD**-0.5)
    keys_here = k_ref[:, lanes]
    values_t = v_ref[:, lanes].T
    outs = []
    for head in range(2):
        scores = dot_nt(head_part(keys_here, head), queries)
        if short:
            scores = jnp.where(seen_mask(), scores, -1e30)
        top = jnp.max(scores, axis=0, keepdims=True)
        weights = jnp.exp(scores - top)
        norm = jnp.sum(weights, axis=0, keepdims=True)
        probs = (weights * (1.0 / norm)).astype(BF)
        outs.append(dot(values_t[head * HD : (head + 1) * HD], probs))
        lse_ref[0, pl.ds(pair * 2 + head, 1), :] = top + jnp.log(norm)
    ctx_ref[:, lanes] = jnp.concatenate(outs, axis=0).T.astype(BF)


def forward_kernel(
    info_ref, x_ref, rows_ref, mine_ref, theirs_ref,
    q_ref, k_ref, v_ref, ctx_ref, lse_ref, z_ref, xt_ref, w_ref, sem_ref,
):
    width = x_ref.shape[1]

    @pl.when(pl.program_id(0) == 0)
    def _():
        copies = load_blocks(mine_ref, theirs_ref, PAIRED, w_ref, sem_ref)
        for copy in copies:
            copy.start()
        for copy in copies:
            copy.wait()

    tokens = x_ref[...]
    q_ref[...] = (dot(tokens, w_ref[:, :width]) + rows_ref[0:1]).astype(BF)
    k_ref[...] = dot(tokens, w_ref[:, width : 2 * width]).astype(BF)
    v_ref[...] = (dot(tokens, w_ref[:, 2 * width : 3 * width]) + rows_ref[1:2]).astype(BF)
    xt_ref[...] = tokens.T
    pairs = width // (2 * HD)

    def all_pairs(short):
        @pl.loop(0, pairs)
        def _(pair):
            attend_pair(pair, short, q_ref, k_ref, v_ref, ctx_ref, lse_ref)

    @pl.when(info_ref[0] == 1)
    def _():
        all_pairs(False)

    @pl.when(info_ref[0] != 1)
    def _():
        all_pairs(True)

    attended = dot_nt(ctx_ref[...], w_ref[:, 3 * width :])
    z_ref[...] = tokens.astype(F32) + attended + rows_ref[2:3]


def forward(info, tokens, rows, mine, theirs):
    tok = tokens.shape[0] // 2
    width = tokens.shape[1]
    groups = tok // LONG
    tile = pl.BlockSpec((LONG, width), lambda i, *_: (i, 0))
    low = struct((tok, width), BF)
    return call(
        forward_kernel,
        (groups,),
        [
            pl.BlockSpec((LONG, width), lambda i, info: (info[1] * groups + i, 0)),
            pl.BlockSpec((8, width), lambda i, *_: (0, 0)),
            ANY,
            ANY,
        ],
        [
            tile, tile, tile, tile,
            pl.BlockSpec((1, 16, LONG), lambda i, *_: (i, 0, 0)),
            tile,
            pl.BlockSpec((width, LONG), lambda i, *_: (0, i)),
        ],
        [
            low, low, low, low,
            struct((groups, 16, LONG), F32),
            struct((tok, width), F32),
            struct((width, tok), BF),
        ],
        [pltpu.VMEM((width, 4 * width), BF), pltpu.SemaphoreType.DMA((8,))],
        1,
        2 * tok * width * (4 * width + 2 * LONG) * 2,
        20 * 2**20,
        tok * LONG * 12,
    )(info, tokens, rows, mine, theirs)


def up_kernel(z_ref, rows_ref, bias_ref, mine_ref, theirs_ref, act_ref, slope_ref, ht_ref, w_ref, sem_ref):
    width = z_ref.shape[1]

    @pl.when(pl.program_id(0) == 0)
    def _():
        copies = load_blocks(mine_ref, theirs_ref, HALVED, w_ref, sem_ref)
        for copy in copies:
            copy.start()
        for copy in copies:
            copy.wait()

    normal, _ = normalized(z_ref[...])
    low = (normal * rows_ref[3:4] + rows_ref[4:5]).astype(BF)
    ht_ref[...] = low.T
    for part in range(FF // width):
        spot = slice(part * width, (part + 1) * width)
        upper = dot(low, w_ref[:, spot]) + bias_ref[part : part + 1]
        phi_sum = 0.5 + 0.5 * lax.erf(upper * (0.5**0.5))
        density = jnp.exp(-0.5 * upper * upper) * 0.3989422804014327
        act_ref[:, spot] = (upper * phi_sum).astype(BF)
        slope_ref[:, spot] = (phi_sum + upper * density).astype(BF)


TILE = 256


def feed_up(first, rows, bias, mine, theirs):
    tok, width = first.shape
    wide = struct((tok, FF), BF)
    return call(
        up_kernel,
        (tok // TILE,),
        [
            pl.BlockSpec((TILE, width), lambda i: (i, 0)),
            pl.BlockSpec((8, width), lambda i: (0, 0)),
            pl.BlockSpec((4, width), lambda i: (0, 0)),
            ANY,
            ANY,
        ],
        [
            pl.BlockSpec((TILE, FF), lambda i: (i, 0)),
            pl.BlockSpec((TILE, FF), lambda i: (i, 0)),
            pl.BlockSpec((width, TILE), lambda i: (0, i)),
        ],
        [wide, wide, struct((width, tok), BF)],
        [pltpu.VMEM((width, FF), BF), pltpu.SemaphoreType.DMA((8,))],
        0,
        2 * tok * width * FF,
        20 * 2**20,
        tok * FF * 2,
    )(first, rows, bias, mine, theirs)


def split_grad(grad, width, mine_ref, theirs_ref):
    cols = mine_ref.shape[2]
    for ref in (mine_ref, theirs_ref):
        for block in range(ref.shape[0]):
            ref[block] = grad[:, block * cols : (block + 1) * cols].astype(BF)


def down_kernel(
    info_ref, z_ref, act_ref, cot_ref, rows_ref, mine_ref, theirs_ref,
    out_ref, dz_ref, gm_ref, gt_ref, sum_ref, w_ref, dyt_ref, sem_ref,
):
    step = pl.program_id(0)
    width = z_ref.shape[1]
    tiles = act_ref.shape[0] // TILE

    @pl.when(step == 0)
    def _():
        copies = load_blocks(mine_ref, theirs_ref, HALVED, w_ref, sem_ref)
        for copy in copies:
            copy.start()
        sum_ref[...] = jnp.zeros_like(sum_ref)
        for copy in copies:
            copy.wait()

    @pl.when(step < tiles)
    def _():
        spot = pl.ds(pl.multiple_of(step * TILE, TILE), TILE)
        branch = dot_nt(act_ref[spot, :], w_ref[...])
        normal, _ = normalized(z_ref[...])
        hidden = normal * rows_ref[3:4] + rows_ref[4:5]
        normal_two, inverse = normalized(hidden + branch + rows_ref[5:6])
        out_ref[...] = (normal_two * rows_ref[6:7] + rows_ref[7:8]).astype(BF)
        cot = cot_ref[...].astype(F32)
        grad = norm_back(cot * rows_ref[6:7], normal_two, inverse)
        dz_ref[...] = grad
        dyt_ref[:, spot] = grad.astype(BF).T
        sum_ref[0:1] += row_sum(grad)
        sum_ref[1:2] += row_sum(cot * normal_two)
        sum_ref[2:3] += row_sum(cot)

    for part in range(4):
        @pl.when(step == tiles + part)
        def _():
            spot = slice((part ^ 2) * width, ((part ^ 2) + 1) * width)
            grad = dot(dyt_ref[...], act_ref[:, spot])
            ref = gt_ref if part < 2 else gm_ref
            cols = ref.shape[2]
            for block in range(2):
                ref[block] = grad[:, block * cols : (block + 1) * cols].astype(BF)


def grad_specs(tiles, width):
    cols = width // 2
    mine = pl.BlockSpec((2, width, cols), lambda i, *_: (jnp.clip(i - tiles - 2, 0, 1), 0, 0))
    theirs = pl.BlockSpec((2, width, cols), lambda i, *_: (jnp.clip(i - tiles, 0, 1), 0, 0))
    return [mine, theirs]


def feed_down(info, first, act, cot, rows, mine, theirs):
    tok, width = first.shape
    tiles = tok // TILE
    last = tiles - 1
    row_tile = pl.BlockSpec((TILE, width), lambda i, *_: (jnp.minimum(i, last), 0))
    grads = struct((4, width, width // 2), BF)
    return call(
        down_kernel,
        (tiles + 4,),
        [
            row_tile,
            pl.BlockSpec((tok, FF), lambda i, *_: (0, 0)),
            pl.BlockSpec(
                (TILE, width), lambda i, info: (info[1] * tiles + jnp.minimum(i, last), 0)
            ),
            pl.BlockSpec((8, width), lambda i, *_: (0, 0)),
            ANY,
            ANY,
        ],
        [row_tile, row_tile]
        + grad_specs(tiles, width)
        + [pl.BlockSpec((8, width), lambda i, *_: (0, 0))],
        [struct((tok, width), BF), struct((tok, width), F32), grads, grads, struct((8, width), F32)],
        [
            pltpu.VMEM((width, FF), BF),
            pltpu.VMEM((width, tok), BF),
            pltpu.SemaphoreType.DMA((8,)),
        ],
        1,
        4 * tok * width * FF,
        30 * 2**20,
    )(info, first, act, cot, rows, mine, theirs)


def back_kernel(
    z_ref, dz2_ref, slope_ref, ht_ref, rows_ref, dm_ref, dt_ref, um_ref, ut_ref, om_ref, ot_ref,
    dz1_ref, dctx_ref, dtt_ref, gm_ref, gt_ref, sum_ref,
    wd_ref, wu_ref, wo_ref, da_ref, dsem_ref, usem_ref, osem_ref,
):
    step = pl.program_id(0)
    width = z_ref.shape[1]
    tiles = da_ref.shape[0] // TILE

    @pl.when(step == 0)
    def _():
        copies = load_blocks(dm_ref, dt_ref, HALVED, wd_ref, dsem_ref)
        copies += load_blocks(um_ref, ut_ref, HALVED, wu_ref, usem_ref)
        copies += load_blocks(om_ref, ot_ref, [(0, 3), (1, 3)], wo_ref, osem_ref)
        for copy in copies:
            copy.start()
        sum_ref[...] = jnp.zeros_like(sum_ref)
        for copy in copies:
            copy.wait()

    @pl.when(step < tiles)
    def _():
        spot = pl.ds(pl.multiple_of(step * TILE, TILE), TILE)
        grad_two = dz2_ref[...]
        low_two = grad_two.astype(BF)
        grad_hidden = grad_two
        for part in range(FF // width):
            lanes = slice(part * width, (part + 1) * width)
            grad_act = dot(low_two, wd_ref[:, lanes])
            grad_up = (grad_act * slope_ref[:, lanes].astype(F32)).astype(BF)
            da_ref[spot, lanes] = grad_up
            sum_ref[4 + part : 5 + part] += row_sum(grad_up.astype(F32))
            grad_hidden = grad_hidden + dot_nt(grad_up, wu_ref[:, lanes])
        normal, inverse = normalized(z_ref[...])
        grad_one = norm_back(grad_hidden * rows_ref[3:4], normal, inverse)
        sum_ref[0:1] += row_sum(grad_one)
        sum_ref[1:2] += row_sum(grad_hidden * normal)
        sum_ref[2:3] += row_sum(grad_hidden)
        dz1_ref[...] = grad_one
        low_one = grad_one.astype(BF)
        dtt_ref[...] = low_one.T
        dctx_ref[...] = dot(low_one, wo_ref[...]).astype(BF)

    for part in range(4):
        @pl.when(step == tiles + part)
        def _():
            spot = slice((part ^ 2) * width, ((part ^ 2) + 1) * width)
            grad = dot(ht_ref[...], da_ref[:, spot])
            ref = gt_ref if part < 2 else gm_ref
            cols = ref.shape[2]
            for block in range(2):
                ref[block] = grad[:, block * cols : (block + 1) * cols].astype(BF)


def feed_back(first, dz2, slope, hidden_t, rows, down, upper, other):
    tok, width = first.shape
    tiles = tok // TILE
    last = tiles - 1
    row_tile = pl.BlockSpec((TILE, width), lambda i: (jnp.minimum(i, last), 0))
    grads = struct((4, width, width // 2), BF)
    return call(
        back_kernel,
        (tiles + 4,),
        [
            row_tile,
            row_tile,
            pl.BlockSpec((TILE, FF), lambda i: (jnp.minimum(i, last), 0)),
            pl.BlockSpec((width, tok), lambda i: (0, 0)),
            pl.BlockSpec((8, width), lambda i: (0, 0)),
        ]
        + [ANY] * 6,
        [row_tile, row_tile, pl.BlockSpec((width, TILE), lambda i: (0, jnp.minimum(i, last)))]
        + grad_specs(tiles, width)
        + [pl.BlockSpec((8, width), lambda i: (0, 0))],
        [
            struct((tok, width), F32),
            struct((tok, width), BF),
            struct((width, tok), BF),
            grads,
            grads,
            struct((8, width), F32),
        ],
        [
            pltpu.VMEM((width, FF), BF),
            pltpu.VMEM((width, FF), BF),
            pltpu.VMEM((width, width), BF),
            pltpu.VMEM((tok, FF), BF),
            pltpu.SemaphoreType.DMA((8,)),
            pltpu.SemaphoreType.DMA((8,)),
            pltpu.SemaphoreType.DMA((2,)),
        ],
        0,
        6 * tok * width * FF,
        40 * 2**20,
    )(first, dz2, slope, hidden_t, rows, *down, *upper, *other)


def attend_pair_back(pair, short, base, q_ref, k_ref, v_ref, dctx_ref, lse_ref, dqkv_ref):
    width = q_ref.shape[1]
    lanes = pair_lanes(pair)
    queries = q_ref[:, lanes] * BF(HD**-0.5)
    keys_here = k_ref[:, lanes]
    values = v_ref[:, lanes]
    grads = dctx_ref[:, lanes]
    keys_t = keys_here.T
    grad_q, grad_k, grad_v = [], [], []
    for head in range(2):
        scores = dot_nt(head_part(keys_here, head), queries)
        if short:
            scores = jnp.where(seen_mask(), scores, -1e30)
        probs = jnp.exp(scores - lse_ref[0, pl.ds(pair * 2 + head, 1), :])
        grad_probs = dot_nt(head_part(values, head), grads)
        inner = jnp.sum(probs * grad_probs, axis=0, keepdims=True)
        grad_scores = (probs * (grad_probs - inner)).astype(BF)
        grad_k.append(dot(grad_scores, queries))
        grad_v.append(dot(probs.astype(BF), grads))
        grad_q.append(dot(keys_t[head * HD : (head + 1) * HD], grad_scores))
    low = low_lanes(LONG)
    rows = pl.ds(pl.multiple_of(base, LONG), LONG)

    def store(part, values_in):
        spot = pl.ds(pl.multiple_of(part * width + pair * 2 * HD, 2 * HD), 2 * HD)
        dqkv_ref[rows, spot] = values_in.astype(BF)

    store(0, jnp.concatenate(grad_q, axis=0).T * HD**-0.5)
    store(1, jnp.where(low, grad_k[0], grad_k[1]))
    store(2, jnp.where(low, grad_v[0], grad_v[1]))


def attend_back_kernel(
    info_ref, q_ref, k_ref, v_ref, dctx_ref, lse_ref, dz_ref, xt_ref, dtt_ref, ctx_ref,
    mine_ref, theirs_ref, gm_ref, gt_ref, gx_ref, sum_ref, w_ref, dqkv_ref, sem_ref,
):
    step = pl.program_id(0)
    width = q_ref.shape[1]
    groups = dqkv_ref.shape[0] // LONG
    cols = gm_ref.shape[2]

    @pl.when(step == 0)
    def _():
        copies = load_blocks(mine_ref, theirs_ref, PAIRED[:6], w_ref, sem_ref)
        for copy in copies:
            copy.start()
        sum_ref[...] = jnp.zeros_like(sum_ref)
        for copy in copies:
            copy.wait()

    def all_pairs(short):
        @pl.loop(0, width // (2 * HD))
        def _(pair):
            attend_pair_back(
                pair, short, step * LONG, q_ref, k_ref, v_ref, dctx_ref, lse_ref, dqkv_ref
            )

    @pl.when((step < groups) & (info_ref[0] == 1))
    def _():
        all_pairs(False)

    @pl.when((step < groups) & (info_ref[0] != 1))
    def _():
        all_pairs(True)

    @pl.when(step < groups)
    def _():
        rows = pl.ds(pl.multiple_of(step * LONG, LONG), LONG)
        grads = dqkv_ref[rows, :]
        gx_ref[...] = (dz_ref[...] + dot_nt(grads, w_ref[...])).astype(BF)
        sum_ref[0:1] += row_sum(dqkv_ref[rows, :width].astype(F32))
        sum_ref[1:2] += row_sum(dqkv_ref[rows, 2 * width :].astype(F32))

    def put(grad):
        gm_ref[0] = grad[:, :cols].astype(BF)
        gt_ref[0] = grad[:, cols:].astype(BF)

    for part in range(3):
        @pl.when(step == groups + part)
        def _():
            put(dot(xt_ref[...], dqkv_ref[:, part * width : (part + 1) * width]))

    @pl.when(step == groups + 3)
    def _():
        put(dot(dtt_ref[...], ctx_ref[...]))


def attend_back(info, q, k, v, dctx, lse, dz, x_t, dt_t, ctx, mine, theirs):
    tok, width = q.shape
    groups = tok // LONG
    last = groups - 1
    tile = pl.BlockSpec((LONG, width), lambda i, *_: (jnp.minimum(i, last), 0))
    whole = pl.BlockSpec((width, tok), lambda i, *_: (0, 0))
    block = pl.BlockSpec((1, width, width // 2), lambda i, *_: (jnp.clip(i - groups, 0, 3), 0, 0))
    grads = struct((4, width, width // 2), BF)
    return call(
        attend_back_kernel,
        (groups + 4,),
        [
            tile, tile, tile, tile,
            pl.BlockSpec((1, 16, LONG), lambda i, *_: (jnp.minimum(i, last), 0, 0)),
            tile, whole, whole,
            pl.BlockSpec((tok, width), lambda i, *_: (0, 0)),
            ANY, ANY,
        ],
        [block, block, tile, pl.BlockSpec((8, width), lambda i, *_: (0, 0))],
        [grads, grads, struct((tok, width), BF), struct((8, width), F32)],
        [
            pltpu.VMEM((width, 3 * width), BF),
            pltpu.VMEM((tok, 3 * width), BF),
            pltpu.SemaphoreType.DMA((6,)),
        ],
        1,
        2 * tok * width * (7 * width + 5 * LONG),
        30 * 2**20,
        tok * LONG * 12,
    )(info, q, k, v, dctx, lse, dz, x_t, dt_t, ctx, mine, theirs)


def adamw_update(weights_in, moment, square, average_in, gradient, rate, scalars):
    beta_one, beta_two, ema_decay, scale_one, scale_two = scalars
    moment_new = beta_one * moment + (1.0 - beta_one) * gradient
    square_new = beta_two * square + (1.0 - beta_two) * gradient * gradient
    moment_hat = moment_new * scale_one
    square_hat = square_new * scale_two
    weights_new = weights_in - rate * (
        moment_hat / (jnp.sqrt(square_hat) + 1e-08) + 0.01 * weights_in
    )
    average_new = ema_decay * average_in + (1.0 - ema_decay) * weights_new
    return weights_new, moment_new, square_new, average_new


def adamw_kernel(table_ref, scale_ref, w_ref, m_ref, s_ref, a_ref, *refs):
    slot = pl.program_id(0)
    grads, outs = refs[:3], refs[3:]
    chunk = table_ref[0, slot]
    gradient = jnp.zeros(w_ref.shape[1:], F32)
    for at, ref in enumerate(grads):
        gradient = gradient + ref[0].astype(F32) * jnp.where(chunk == at, 1.0, 0.0)
    results = adamw_update(
        w_ref[0], m_ref[0], s_ref[0], a_ref[0], gradient,
        scale_ref[8 + slot], [scale_ref[at] for at in range(5)],
    )
    for ref, value in zip(outs, results):
        ref[0] = value


def adamw_slots(table, scales, states, grads):
    cap, rows, cols = states[0].shape
    own = pl.BlockSpec((1, rows, cols), lambda i, *_: (i, 0, 0))

    def chosen(at):
        def index(i, table, scales):
            here = table[0, i] == at
            return jnp.where(here, table[1, i], 0), jnp.where(here, table[2, i], 0), 0

        return pl.BlockSpec((1, rows, cols), index)

    return call(
        adamw_kernel,
        (cap,),
        [own] * 4 + [chosen(at) for at in range(3)],
        [own] * 4,
        [struct(states[0].shape, F32)] * 4,
        [],
        2,
        20 * cap * rows * cols,
        40 * cap * rows * cols,
    )(table, scales, *states, *grads)


def on_device(
    tokens,
    cotangent,
    phase_of,
    unit_slot,
    step_count,
    learn_rates,
    decay_rates,
    master,
    first_moment,
    second_moment,
    average,
    vector_state,
):
    cap, unit_rows, cols = master.shape
    tok_rows, width = tokens.shape
    batch_count = lax.axis_size("batch")
    row_blocks = width // unit_rows
    col_blocks = FF // width
    core = lax.axis_index("tensor")
    place = lax.axis_index("batch")
    fast = batch_count == FAST_BATCH
    plane, y_at, x_at = place // 4, (place // 2) % 2, place % 2
    up_base = 4 * row_blocks
    down_base = up_base + row_blocks * col_blocks
    chunks = [(0, 1, row_blocks), (up_base, col_blocks, 1), (down_base, col_blocks, 1)]
    orients = [0, 1, 0]

    def coords(orient):
        y_first = (core + orient) % 2 == 0
        return jnp.where(y_first, y_at, x_at), jnp.where(y_first, x_at, y_at), plane

    def chunk_units(chunk):
        base, row_step, block_step = chunk
        return base + jnp.arange(4)[:, None] * block_step + jnp.arange(row_blocks)[None] * row_step

    def weights_of(at):
        chunk, orient = chunks[at], orients[at]
        if fast:
            where = coords(orient)
            info = jnp.stack([where[0], place * cap]).astype(jnp.int32)
            going, kept = spread(master, unit_slot, info, chunk)
            owned = reduce_parts([going], [kept], orient, where)
            mine = gather_parts(owned, orient, where)[0]
        else:
            local = unit_slot[chunk_units(chunk)] - place * cap
            own = (local >= 0) & (local < cap)
            blocks = jnp.take(master, jnp.clip(local, 0, cap - 1), axis=0)
            blocks = jnp.where(own[..., None, None], blocks, 0.0).astype(BF)
            mine = lax.psum(blocks.reshape(4, width, cols), "batch")
        return mine, core_swap(mine)

    def grads_of(at, mine, theirs, vec_mine=None, vec_theirs=None):
        orient = orients[at]
        grad = total(mine, core_swap(theirs))
        parts = [grad]
        if vec_mine is not None:
            parts.append(total(vec_mine, core_swap(vec_theirs))[None])
        if not fast:
            return [lax.psum(part, "batch") for part in parts]
        where = coords(orient)
        halves = [part.shape[1] // 2 for part in parts]
        going = [cut(part, (1 - where[0]) * half, half) for part, half in zip(parts, halves)]
        kept = [cut(part, where[0] * half, half) for part, half in zip(parts, halves)]
        return gather_parts(reduce_parts(going, kept, orient, where), orient, where)

    def halves_of(array_in):
        other = lax.dynamic_slice_in_dim(array_in, (1 - core) * cols, cols, array_in.ndim - 1)
        return lax.dynamic_slice_in_dim(array_in, core * cols, cols, array_in.ndim - 1), other

    def swapped(array_in):
        return jnp.concatenate(halves_of(array_in), axis=-1)

    info = jnp.stack([phase_of[0], core]).astype(jnp.int32)
    vectors = vector_state[0]
    rows = jnp.concatenate(
        [swapped(vectors[0:2]), vectors[2:5], vectors[9:12]], axis=0
    )
    upper = vectors[5:9].reshape(2, FF // 2)
    bias_up = jnp.where(core == 0, upper, upper[::-1]).reshape(4, width)

    weights_io = weights_of(0)
    weights_up = weights_of(1)
    weights_down = weights_of(2)
    q, k, v, ctx, lse, first, x_t = forward(info, tokens, rows, *weights_io)
    act, slope, hidden_t = feed_up(first, rows, bias_up, *weights_up)
    out_half, dz2, down_mine, down_theirs, sums_two = feed_down(
        info, first, act, cotangent, rows, *weights_down
    )
    (grad_down,) = grads_of(2, down_mine, down_theirs)
    out_other = core_swap(out_half)
    dz1, dctx, dt_t, up_mine, up_theirs, sums_one = feed_back(
        first, dz2, slope, hidden_t, rows, weights_down, weights_up, weights_io
    )
    (grad_up,) = grads_of(1, up_mine, up_theirs)
    io_mine, io_theirs, grad_x, sums_zero = attend_back(
        info, q, k, v, dctx, lse, dz1, x_t, dt_t, ctx, *weights_io
    )
    grad_x_other = core_swap(grad_x)

    full_mine, full_theirs = halves_of(jnp.concatenate([sums_one[0:3], sums_two[0:3]], axis=0))
    up_rows = sums_one[4:8].reshape(2, 4, cols)

    def vec_rows(at, full):
        head_rows = sums_zero[0:2, at * cols : (at + 1) * cols]
        pad = jnp.zeros((4, cols), F32)
        return jnp.concatenate([head_rows, full[0:3], up_rows[at], full[3:6], pad], axis=0)

    grad_io, vec_half = grads_of(
        0, io_mine, io_theirs, vec_rows(0, full_mine), vec_rows(1, full_theirs)
    )
    vec_here = vec_half[0].astype(F32)
    vec_there = core_swap(vec_half[0]).astype(F32)
    left = jnp.where(core == 0, vec_here, vec_there)
    right = jnp.where(core == 0, vec_there, vec_here)
    wide_rows = jnp.concatenate([left, right], axis=1)
    vector_grads = jnp.concatenate(
        [
            wide_rows[0:5],
            left[5:9].reshape(2, width),
            right[5:9].reshape(2, width),
            wide_rows[9:12],
        ],
        axis=0,
    )

    count_f = step_count[0].astype(F32)
    scalars = [
        decay_rates[0],
        decay_rates[1],
        decay_rates[2],
        1.0 / (1.0 - decay_rates[0] ** count_f),
        1.0 / (1.0 - decay_rates[1] ** count_f),
    ]
    my_ids = place * cap + jnp.arange(cap, dtype=jnp.int32)
    matches = unit_slot[None, :] == my_ids[:, None]
    unit_ids = jnp.arange(unit_slot.shape[0], dtype=jnp.int32)
    unit = jnp.sum(jnp.where(matches, unit_ids[None, :], 0), axis=1)
    occupied = jnp.any(matches, axis=1)
    is_up = (unit >= up_base) & (unit < down_base)
    is_down = unit >= down_base
    chunk_at = jnp.where(is_down, 2, jnp.where(is_up, 1, 0))
    local = unit - jnp.where(is_down, down_base, up_base)
    block_at = jnp.where(chunk_at == 0, unit // row_blocks, local % col_blocks)
    row_at = jnp.where(chunk_at == 0, unit % row_blocks, local // col_blocks)
    kind = jnp.where(
        occupied,
        (unit >= 3 * row_blocks).astype(jnp.int32) + is_up.astype(jnp.int32) + 2 * is_down,
        0,
    )
    rates = jnp.sum(
        jnp.where(kind[:, None] == jnp.arange(4)[None, :], learn_rates[None, :4], 0.0), axis=1
    )
    table = jnp.stack([jnp.where(occupied, chunk_at, 3), block_at, row_at]).astype(jnp.int32)
    scales = jnp.concatenate([jnp.stack(scalars), jnp.zeros((3,), F32), rates])
    new_states = adamw_slots(
        table,
        scales,
        (master, first_moment, second_moment, average),
        (grad_io, grad_up, grad_down),
    )
    grads_scaled = vector_grads * float(tok_rows * batch_count) ** (-0.5)
    vec_weights, vec_first, vec_second, vec_average = adamw_update(
        vector_state[0], vector_state[1], vector_state[2], vector_state[3],
        grads_scaled, learn_rates[4], scalars,
    )

    def both(here, there):
        low_first = core == 0
        return jnp.concatenate(
            [jnp.where(low_first, here, there), jnp.where(low_first, there, here)], axis=0
        )

    return (
        both(out_half, out_other),
        both(grad_x, grad_x_other).astype(F32),
        *new_states,
        jnp.stack([vec_weights, vec_average]),
        jnp.stack([grads_scaled, vec_first]),
        vec_second,
    )


def solution(mesh):
    return jax.shard_map(
        on_device,
        mesh=mesh,
        in_specs=(
            P("batch", None),
            P("batch", None),
            P("batch"),
            P(),
            P(),
            P(),
            P(),
            P("batch", None, "tensor"),
            P("batch", None, "tensor"),
            P("batch", None, "tensor"),
            P("batch", None, "tensor"),
            P(),
        ),
        out_specs=(
            P("batch", None),
            P("batch", None),
            P("batch", None, "tensor"),
            P("batch", None, "tensor"),
            P("batch", None, "tensor"),
            P("batch", None, "tensor"),
            P(),
            P(),
            P(),
        ),
        check_vma=False,
    )
```

time: 1180 us -> 562 us (0.48)
  waiting for transfers between devices: 595 us -> 171 us
  local copies, waits for them, and re-layouts: 247 us -> 25.7 us
  matrix products: 168 us -> 0 us
  Pallas kernels: 0 us -> 166 us
  starting transfers between devices: 0.65 us -> 121 us
  blocking collectives: 43.4 us -> 0 us
  other arithmetic: 89.6 us -> 62.2 us
  between operations: 20.2 us -> 6.46 us
    reduce_scatter x1 -> x0, waiting for transfers between devices: 342 us -> none  [on_device(): lax.psum_scatter(jnp.where(row_used[:, None, None], jnp.take(unit_grads,...]
    ppermute x0 -> x70, waiting for transfers between devices: none -> 171 us  [the longest x60 169 us: send(): return unpacked(lax.ppermute(packed(parts), BOTH, pairs), parts)]
    dot_general x46 -> x0, matrix products: 168 us -> none  [the longest x6 66.4 us: product(): return jnp.dot(first_mat, second_mat, preferred_element_type=jnp.float32)]
    all_gather x1 -> x0, waiting for transfers between devices: 168 us -> none  [on_device(): every_slot = lax.all_gather(low_master, 'batch', axis=0, tiled=True)]
    pallas_call x0 -> x9, Pallas kernels: none -> 166 us  [the longest x1 43.1 us: attend_back(): call(attend_back_kernel, (groups + 4,), [tile, tile, tile, tile, pl.Block...]
    ppermute x0 -> x70, starting transfers between devices: none -> 121 us  [the longest x60 118 us: send(): return unpacked(lax.ppermute(packed(parts), BOTH, pairs), parts)]
    psum x4 -> x0, waiting for transfers between devices: 85.4 us -> none  [the longest x1 33.3 us: on_device(): branch = lax.psum(with_transposed(active_low, w_down), 'tensor')]
    reshape x27 -> x5, local copies, waits for them, and re-layouts: 49.8 us -> 1.38 us  [the longest x1 0.73 us: on_device(): upper = vectors[5:9].reshape(2, FF // 2)]
  transfers between devices with their start and end apart: 6 -> 70, of which waited for: 5 -> 26; matrix products, arithmetic and copies ran while one was open for 8% -> 14% of each run, Pallas kernels for 0% -> 25%
where the time goes in v1:
time: 562 us; the launch traced here: 552 us
  waiting for transfers between devices  171 us (30%)
  Pallas kernels  166 us (30%)
  starting transfers between devices  121 us (22%)
  other arithmetic  62.2 us (11%)
  local copies, waits for them, and re-layouts  25.7 us (5%)
  between operations  6.46 us (1%)
    ppermute x60, waiting for transfers between devices, send(): return unpacked(lax.ppermute(packed(parts), BOTH, pairs), parts)  169 us
    ppermute x60, starting transfers between devices, send(): return unpacked(lax.ppermute(packed(parts), BOTH, pairs), parts)  118 us
    pallas_call x1, Pallas kernels, attend_back(): call(attend_back_kernel, (groups + 4,), [tile, tile, tile, tile, pl.Block...  43.1 us
    pallas_call x1, Pallas kernels, feed_back(): call(back_kernel, (tiles + 4,), [row_tile, row_tile, pl.BlockSpec((TILE,...  29.9 us
    convert_element_type x25, other arithmetic, total(): return result.astype(BF)  27.4 us
    pallas_call x1, Pallas kernels, forward(): call(forward_kernel, (groups,), [pl.BlockSpec((LONG, width), lambda i, in...  26.1 us
    pallas_call x1, Pallas kernels, feed_down(): call(down_kernel, (tiles + 4,), [row_tile, pl.BlockSpec((tok, FF), lambda...  22.9 us
    pallas_call x1, Pallas kernels, feed_up(): call(up_kernel, (tok // TILE,), [pl.BlockSpec((TILE, width), lambda i: (i...  16.8 us
  transfers between devices with their start and end apart: 70, of which 26 were waited for; matrix products, arithmetic and copies ran while one was open for 14% of the time, Pallas kernels for 25%

profile of v1, /device:TPU:0, one launch (start us, length us, event | category | flops | bytes accessed | tf_op | source)
XLA Modules:
  0.0 552.3 jit_solution(460937892117233292)
XLA Ops:
  30.6 20.7 %collective-permute-done.22 = bf16[4,384,384]{2,1,0:T(8,128)(2,1)S(1)} collective-permute-done((bf16[4,384,384]{2,1,0:T(8,128)(2,1)}, bf16[4,384,384]{2,1,0:T(8,128)(2,1)S(1)}, u32[]{:S(2)}, u32[]{:S(2)}) %collective-permute-start.22) | collective-permute-done | bytes 1179680 | tf_op jit(solution)/shard_map/ppermute | solution.py:178
  79.7 10.2 %collective-permute-done.3 = bf16[4,48,384]{2,1,0:T(8,128)(2,1)S(1)} collective-permute-done((bf16[4,48,384]{2,1,0:T(8,128)(2,1)S(1)}, bf16[4,48,384]{2,1,0:T(8,128)(2,1)S(1)}, u32[]{:S(2)}, u32[]{:S(2)}) %collective-permute-start.3) | collective-permute-done | bytes 147488 | tf_op jit(solution)/shard_map/ppermute | solution.py:178
  91.3 8.7 %collective-permute-start.5 = (bf16[4,48,384]{2,1,0:T(8,128)(2,1)S(1)}, bf16[4,48,384]{2,1,0:T(8,128)(2,1)S(1)}, u32[]{:S(2)}, u32[]{:S(2)}) collective-permute-start(bf16[4,48,384]{2,1,0:T(8,128)(2,1)S(1)} %add_convert_fusion.28), channel_id=1, source_target_pairs={{0,8},{1,9},{2,10},{3,11},{4,12},{5,13},{6,14},{7,15},{8,16},{9,17... | collective-permute-start | bytes 442376 | tf_op jit(solution)/shard_map/ppermute | solution.py:178
  100.0 5.7 %collective-permute-done.14 = bf16[4,48,384]{2,1,0:T(8,128)(2,1)S(1)} collective-permute-done((bf16[4,48,384]{2,1,0:T(8,128)(2,1)S(1)}, bf16[4,48,384]{2,1,0:T(8,128)(2,1)S(1)}, u32[]{:S(2)}, u32[]{:S(2)}) %collective-permute-start.14) | collective-permute-done | bytes 147488 | tf_op jit(solution)/shard_map/ppermute | solution.py:178
  111.3 7.0 %collective-permute-done.6 = bf16[4,48,384]{2,1,0:T(8,128)(2,1)S(1)} collective-permute-done((bf16[4,48,384]{2,1,0:T(8,128)(2,1)S(1)}, bf16[4,48,384]{2,1,0:T(8,128)(2,1)S(1)}, u32[]{:S(2)}, u32[]{:S(2)}) %collective-permute-start.6) | collective-permute-done | bytes 147488 | tf_op jit(solution)/shard_map/ppermute | solution.py:178
  131.3 5.8 %collective-permute-done.17 = bf16[4,48,384]{2,1,0:T(8,128)(2,1)S(1)} collective-permute-done((bf16[4,48,384]{2,1,0:T(8,128)(2,1)S(1)}, bf16[4,48,384]{2,1,0:T(8,128)(2,1)S(1)}, u32[]{:S(2)}, u32[]{:S(2)}) %collective-permute-start.17) | collective-permute-done | bytes 147488 | tf_op jit(solution)/shard_map/ppermute | solution.py:178
  144.0 13.0 %collective-permute-done.19 = bf16[4,192,384]{2,1,0:T(8,128)(2,1)S(1)} collective-permute-done((bf16[4,192,384]{2,1,0:T(8,128)(2,1)S(1)}, bf16[4,192,384]{2,1,0:T(8,128)(2,1)S(1)}, u32[]{:S(2)}, u32[]{:S(2)}) %collective-permute-start.19) | collective-permute-done | bytes 589856 | tf_op jit(solution)/shard_map/ppermute | solution.py:178
  161.6 13.9 %collective-permute-done.9 = bf16[4,384,384]{2,1,0:T(8,128)(2,1)S(1)} collective-permute-done((bf16[4,384,384]{2,1,0:T(8,128)(2,1)S(1)}, bf16[4,384,384]{2,1,0:T(8,128)(2,1)S(1)}, u32[]{:S(2)}, u32[]{:S(2)}) %collective-permute-start.9) | collective-permute-done | bytes 1179680 | tf_op jit(solution)/shard_map/ppermute | solution.py:178
  176.8 8.8 %collective-permute-done.20 = bf16[4,384,384]{2,1,0:T(8,128)(2,1)S(1)} collective-permute-done((bf16[4,384,384]{2,1,0:T(8,128)(2,1)S(1)}, bf16[4,384,384]{2,1,0:T(8,128)(2,1)S(1)}, u32[]{:S(2)}, u32[]{:S(2)}) %collective-permute-start.20) | collective-permute-done | bytes 1179680 | tf_op jit(solution)/shard_map/ppermute | solution.py:178
  194.2 26.1 %shard_map.188 = (bf16[1024,768]{1,0:T(8,128)(2,1)}, bf16[1024,768]{1,0:T(8,128)(2,1)}, bf16[1024,768]{1,0:T(8,128)(2,1)}, bf16[1024,768]{1,0:T(8,128)(2,1)}, f3...) custom-call(s32[2]{0:T(128)} %pad_add_fusion.1.info_ref, bf16[2048,768]{1,0:T(8,128)(2,1)} %x_ref.1, ...), custom_call_target="tpu_custom_call" | custom-call | flops 12884901888 | bytes 20971520 | tf_op jit(solution)/shard_map/pallas_call | solution.py:330
  220.4 16.8 %shard_map.190 = (bf16[1024,3072]{1,0:T(8,128)(2,1)}, bf16[1024,3072]{1,0:T(8,128)(2,1)}, bf16[768,1024]{1,0:T(8,128)(2,1)}) custom-call(f32[1024,768]{1,0:T(8,128)} %get-tuple-element.46.z_ref, f32[8,768]{1,0:T(8,128)} %pad_maximum_fusion.31.rows_ref, f32[4,768]{1,0:T(4,128)} %reshape.920.bias_ref, bf16[4,768,384]{2,1,0:T(8,128)(2,1)} %pad_maximum_fusion.2.mine_ref.um_ref, ...), custom_call_target="tpu_custom_call" | custom-call | flops 4831838208 | bytes 20971520 | tf_op jit(solution)/shard_map/pallas_call | solution.py:388
  237.2 22.9 %shard_map.192 = (bf16[1024,768]{1,0:T(8,128)(2,1)}, f32[1024,768]{1,0:T(8,128)}, bf16[4,768,384]{2,1,0:T(8,128)(2,1)}, bf16[4,768,384]{2,1,0:T(8,128)(2,1)}, f32[8,768]{1,0:T(8,128)}) custom-call(s32[2]{0:T(128)} %pad_add_fusion.1.info_ref, f32[1024,768]{1,0:T(8,128)} %get-tuple-element.46.z_ref, bf16[1024,3072]{1,0:T(8,128)(2,1)} %get-tuple-element.49.act_ref, ...), custom_call_target="tpu_custom_call" | custom-call | flops 9663676416 | bytes 31457280 | tf_op jit(solution)/shard_map/pallas_call | solution.py:476
  260.5 29.9 %shard_map.193 = (f32[1024,768]{1,0:T(8,128)}, bf16[1024,768]{1,0:T(8,128)(2,1)}, bf16[768,1024]{1,0:T(8,128)(2,1)}, bf16[4,768,384]{2,1,0:T(8,128)(2,1)}, bf16[...) custom-call(f32[1024,768]{1,0:T(8,128)} %get-tuple-element.46.z_ref, f32[1024,768]{1,0:T(8,128)} %get-tuple-element.56.dz2_ref, ...), custom_call_target="tpu_custom_call" | custom-call | flops 14495514624 | bytes 41943040 | tf_op jit(solution)/shard_map/pallas_call | solution.py:564
  290.6 43.1 %shard_map.194 = (bf16[4,768,384]{2,1,0:T(8,128)(2,1)}, bf16[4,768,384]{2,1,0:T(8,128)(2,1)}, bf16[1024,768]{1,0:T(8,128)(2,1)}, f32[8,768]{1,0:T(8,128)}) custom-call(s32[2]{0:T(128)} %pad_add_fusion.1.info_ref, bf16[1024,768]{1,0:T(8,128)(2,1)} %get-tuple-element.53.q_ref, bf16[1024,768]{1,0:T(8,128)(2,1)} %get-tuple-element.54.k_ref, ...), custom_call_target="tpu_custom_call" | custom-call | flops 12482248704 | bytes 31457280 | tf_op jit(solution)/shard_map/pallas_call | solution.py:696
  371.7 6.2 %collective-permute-done.48 = bf16[4,384,384]{2,1,0:T(8,128)(2,1)} collective-permute-done((bf16[4,384,384]{2,1,0:T(8,128)(2,1)}, bf16[4,384,384]{2,1,0:T(8,128)(2,1)}, u32[]{:S(2)}, u32[]{:S(2)}) %collective-permute-start.48) | collective-permute-done | bytes 1179680 | tf_op jit(solution)/shard_map/ppermute | solution.py:178
  380.5 11.2 %collective-permute-done.37 = bf16[1544,384]{1,0:T(8,128)(2,1)} collective-permute-done((bf16[1544,384]{1,0:T(8,128)(2,1)S(1)}, bf16[1544,384]{1,0:T(8,128)(2,1)}, u32[]{:S(2)}, u32[]{:S(2)}) %collective-permute-start.37) | collective-permute-done | bytes 1185824 | tf_op jit(solution)/shard_map/ppermute | solution.py:178
  398.3 5.9 %collective-permute-start.61 = (bf16[4,48,384]{2,1,0:T(8,128)(2,1)S(1)}, bf16[4,48,384]{2,1,0:T(8,128)(2,1)S(1)}, u32[]{:S(2)}, u32[]{:S(2)}) collective-permute-start(bf16[4,48,384]{2,1,0:T(8,128)(2,1)S(1)} %get-tuple-element.108), channel_id=1, source_target_pairs={{0,8},{1,9},{2,10},{3,11},{4,12},{5,13},{6,14},{7,15},{8,16},{9,17... | collective-permute-start | bytes 442376 | tf_op jit(solution)/shard_map/ppermute | solution.py:178
  413.1 7.3 %collective-permute-done.62 = bf16[4,48,384]{2,1,0:T(8,128)(2,1)S(1)} collective-permute-done((bf16[4,48,384]{2,1,0:T(8,128)(2,1)S(1)}, bf16[4,48,384]{2,1,0:T(8,128)(2,1)S(1)}, u32[]{:S(2)}, u32[]{:S(2)}) %collective-permute-start.62) | collective-permute-done | bytes 147488 | tf_op jit(solution)/shard_map/ppermute | solution.py:178
  453.9 5.6 %collective-permute-done.65 = bf16[4,48,384]{2,1,0:T(8,128)(2,1)S(1)} collective-permute-done((bf16[4,48,384]{2,1,0:T(8,128)(2,1)S(1)}, bf16[4,48,384]{2,1,0:T(8,128)(2,1)S(1)}, u32[]{:S(2)}, u32[]{:S(2)}) %collective-permute-start.65) | collective-permute-done | bytes 147488 | tf_op jit(solution)/shard_map/ppermute | solution.py:178
  459.5 9.3 %collective-permute-start.44 = (bf16[193,384]{1,0:T(8,128)(2,1)S(1)}, bf16[193,384]{1,0:T(8,128)(2,1)S(1)}, u32[]{:S(2)}, u32[]{:S(2)}) collective-permute-start(bf16[193,384]{1,0:T(8,128)(2,1)S(1)} %pad_maximum_fusion.26), channel_id=1, source_target_pairs={{0,24},{1,25},{2,26},{3,27},{4,28},{5,29},{6,30},{7,31},{8,0},{9,1... | collective-permute-start | bytes 444680 | tf_op jit(solution)/shard_map/ppermute | solution.py:178
  488.2 10.6 %collective-permute-done.45 = bf16[772,384]{1,0:T(8,128)(2,1)S(1)} collective-permute-done((bf16[772,384]{1,0:T(8,128)(2,1)S(1)}, bf16[772,384]{1,0:T(8,128)(2,1)S(1)}, u32[]{:S(2)}, u32[]{:S(2)}) %collective-permute-start.45) | collective-permute-done | bytes 592928 | tf_op jit(solution)/shard_map/ppermute | solution.py:178
  502.7 12.7 %collective-permute-done.68 = bf16[4,384,384]{2,1,0:T(8,128)(2,1)S(1)} collective-permute-done((bf16[4,384,384]{2,1,0:T(8,128)(2,1)S(1)}, bf16[4,384,384]{2,1,0:T(8,128)(2,1)S(1)}, u32[]{:S(2)}, u32[]{:S(2)}) %collective-permute-start.68) | collective-permute-done | bytes 1179680 | tf_op jit(solution)/shard_map/ppermute | solution.py:178
  517.6 6.5 %collective-permute-done.57 = bf16[4,384,384]{2,1,0:T(8,128)(2,1)S(1)} collective-permute-done((bf16[4,384,384]{2,1,0:T(8,128)(2,1)S(1)}, bf16[4,384,384]{2,1,0:T(8,128)(2,1)S(1)}, u32[]{:S(2)}, u32[]{:S(2)}) %collective-permute-start.57) | collective-permute-done | bytes 1179680 | tf_op jit(solution)/shard_map/ppermute | solution.py:178
  532.3 13.8 %shard_map.195 = (f32[18,64,384]{2,1,0:T(8,128)}, f32[18,64,384]{2,1,0:T(8,128)}, f32[18,64,384]{2,1,0:T(8,128)}, f32[18,64,384]{2,1,0:T(8,128)}) custom-call(s32[3,18]{1,0:T(4,128)} %pad_add_fusion.table_ref, f32[26]{0:T(128)} %concatenate.175.scale_ref, f32[18,64,384]{2,1,0:T(8,128)} %w_ref.1, f32[18,64,384]{2,1,0:T(8,128)} %m_ref.1, ...), custom_call_target="tpu_custom_call" | custom-call | flops 8847360 | bytes 17694720 | tf_op jit(solution)/shard_map/pallas_call | solution.py:759
  (339 shorter events, 224.1 us)
Async XLA Ops:
  13.0 38.4 %collective-permute-start.22 = (bf16[4,384,384]{2,1,0:T(8,128)(2,1)}, bf16[4,384,384]{2,1,0:T(8,128)(2,1)S(1)}, u32[]{:S(2)}, u32[]{:S(2)}) collective-permute-start(bf16[4,384,384]{2,1,0:T(8,128)(2,1)} %get-tuple-element.51), channel_id=1, source_target_pairs={{0,4},{1,3},{2,6},{3,1},{4,0},{5,7},{6,2},{7,5},{8,12},{9,11},{10,... | collective-permute-start | bytes 3538952 | tf_op jit(solution)/shard_map/ppermute | solution.py:178
  17.5 37.2 %collective-permute-start.11 = (bf16[4,384,384]{2,1,0:T(8,128)(2,1)}, bf16[4,384,384]{2,1,0:T(8,128)(2,1)}, u32[]{:S(2)}, u32[]{:S(2)}) collective-permute-start(bf16[4,384,384]{2,1,0:T(8,128)(2,1)} %get-tuple-element.48), channel_id=1, source_target_pairs={{0,2},{1,5},{2,0},{3,7},{4,6},{5,1},{6,4},{7,3},{8,10},{9,13},{10,... | collective-permute-start | bytes 3538952 | tf_op jit(solution)/shard_map/ppermute | solution.py:178
  28.2 37.1 %collective-permute-start.1 = (bf16[4,192,384]{2,1,0:T(8,128)(2,1)}, bf16[4,192,384]{2,1,0:T(8,128)(2,1)}, u32[]{:S(2)}, u32[]{:S(2)}) collective-permute-start(bf16[4,192,384]{2,1,0:T(8,128)(2,1)} %add_convert_fusion.8), channel_id=1, source_target_pairs={{0,2},{1,5},{2,0},{3,7},{4,6},{5,1},{6,4},{7,3},{8,10},{9,13},{10,... | collective-permute-start | bytes 1769480 | tf_op jit(solution)/shard_map/ppermute | solution.py:178
  73.7 51.7 %collective-permute-start.24 = (bf16[4,48,384]{2,1,0:T(8,128)(2,1)S(1)}, bf16[4,48,384]{2,1,0:T(8,128)(2,1)S(1)}, u32[]{:S(2)}, u32[]{:S(2)}) collective-permute-start(bf16[4,48,384]{2,1,0:T(8,128)(2,1)S(1)} %get-tuple-element.121), channel_id=1, source_target_pairs={{0,8},{1,9},{2,10},{3,11},{4,12},{5,13},{6,14},{7,15},{8,16},{9,17... | collective-permute-start | bytes 442376 | tf_op jit(solution)/shard_map/ppermute | solution.py:178
  74.5 51.5 %collective-permute-start.25 = (bf16[4,48,384]{2,1,0:T(8,128)(2,1)S(1)}, bf16[4,48,384]{2,1,0:T(8,128)(2,1)S(1)}, u32[]{:S(2)}, u32[]{:S(2)}) collective-permute-start(bf16[4,48,384]{2,1,0:T(8,128)(2,1)S(1)} %get-tuple-element.123), channel_id=1, source_target_pairs={{0,16},{1,17},{2,18},{3,19},{4,20},{5,21},{6,22},{7,23},{8,24},{9,... | collective-permute-start | bytes 442376 | tf_op jit(solution)/shard_map/ppermute | solution.py:178
  142.6 33.0 %collective-permute-start.9 = (bf16[4,384,384]{2,1,0:T(8,128)(2,1)S(1)}, bf16[4,384,384]{2,1,0:T(8,128)(2,1)S(1)}, u32[]{:S(2)}, u32[]{:S(2)}) collective-permute-start(bf16[4,384,384]{2,1,0:T(8,128)(2,1)S(1)} %pad_maximum_fusion.9), channel_id=1, source_target_pairs={{0,4},{1,3},{2,6},{3,1},{4,0},{5,7},{6,2},{7,5},{8,12},{9,11},{10,... | collective-permute-start | bytes 3538952 | tf_op jit(solution)/shard_map/ppermute | solution.py:178
  157.4 28.2 %collective-permute-start.20 = (bf16[4,384,384]{2,1,0:T(8,128)(2,1)S(1)}, bf16[4,384,384]{2,1,0:T(8,128)(2,1)S(1)}, u32[]{:S(2)}, u32[]{:S(2)}) collective-permute-start(bf16[4,384,384]{2,1,0:T(8,128)(2,1)S(1)} %pad_maximum_fusion.10), channel_id=1, source_target_pairs={{0,2},{1,5},{2,0},{3,7},{4,6},{5,1},{6,4},{7,3},{8,10},{9,13},{10,... | collective-permute-start | bytes 3538952 | tf_op jit(solution)/shard_map/ppermute | solution.py:178
  160.1 28.1 %collective-permute-start.31 = (bf16[4,384,384]{2,1,0:T(8,128)(2,1)S(1)}, bf16[4,384,384]{2,1,0:T(8,128)(2,1)S(1)}, u32[]{:S(2)}, u32[]{:S(2)}) collective-permute-start(bf16[4,384,384]{2,1,0:T(8,128)(2,1)S(1)} %pad_maximum_fusion.11), channel_id=1, source_target_pairs={{0,4},{1,3},{2,6},{3,1},{4,0},{5,7},{6,2},{7,5},{8,12},{9,11},{10,... | collective-permute-start | bytes 3538952 | tf_op jit(solution)/shard_map/ppermute | solution.py:178
  187.8 32.6 %collective-permute-start.21 = (bf16[4,768,384]{2,1,0:T(8,128)(2,1)}, bf16[4,768,384]{2,1,0:T(8,128)(2,1)}, u32[]{:S(2)}, u32[]{:S(2)}) collective-permute-start(bf16[4,768,384]{2,1,0:T(8,128)(2,1)} %pad_maximum_fusion.2.mine_ref.um_ref), channel_id=1, source_target_pairs={{0,1},{1,0},{2,3},{3,2},{4,5},{5,4},{6,7},{7,6},{8,9},{9,8},{10,11... | collective-permute-start | bytes 7077896 | tf_op jit(solution)/shard_map/ppermute | solution.py:244
  190.3 46.9 %collective-permute-start.32 = (bf16[4,768,384]{2,1,0:T(8,128)(2,1)}, bf16[4,768,384]{2,1,0:T(8,128)(2,1)}, u32[]{:S(2)}, u32[]{:S(2)}) collective-permute-start(bf16[4,768,384]{2,1,0:T(8,128)(2,1)} %pad_maximum_fusion.3.mine_ref.dm_ref), channel_id=1, source_target_pairs={{0,1},{1,0},{2,3},{3,2},{4,5},{5,4},{6,7},{7,6},{8,9},{9,8},{10,11... | collective-permute-start | bytes 7077896 | tf_op jit(solution)/shard_map/ppermute | solution.py:244
  260.1 78.8 %collective-permute-start.58 = (bf16[4,768,384]{2,1,0:T(8,128)(2,1)}, bf16[4,768,384]{2,1,0:T(8,128)(2,1)}, u32[]{:S(2)}, u32[]{:S(2)}) collective-permute-start(bf16[4,768,384]{2,1,0:T(8,128)(2,1)} %get-tuple-element.74), channel_id=1, source_target_pairs={{0,1},{1,0},{2,3},{3,2},{4,5},{5,4},{6,7},{7,6},{8,9},{9,8},{10,11... | collective-permute-start | bytes 7077896 | tf_op jit(solution)/shard_map/ppermute | solution.py:244
  290.4 53.5 %collective-permute-start.47 = (bf16[4,768,384]{2,1,0:T(8,128)(2,1)}, bf16[4,768,384]{2,1,0:T(8,128)(2,1)}, u32[]{:S(2)}, u32[]{:S(2)}) collective-permute-start(bf16[4,768,384]{2,1,0:T(8,128)(2,1)} %get-tuple-element.72), channel_id=1, source_target_pairs={{0,1},{1,0},{2,3},{3,2},{4,5},{5,4},{6,7},{7,6},{8,9},{9,8},{10,11... | collective-permute-start | bytes 7077896 | tf_op jit(solution)/shard_map/ppermute | solution.py:244
  335.4 28.1 %collective-permute-start.34 = (bf16[1024,768]{1,0:T(8,128)(2,1)}, bf16[1024,768]{1,0:T(8,128)(2,1)}, u32[]{:S(2)}, u32[]{:S(2)}) collective-permute-start(bf16[1024,768]{1,0:T(8,128)(2,1)} %get-tuple-element.65), channel_id=1, source_target_pairs={{0,1},{1,0},{2,3},{3,2},{4,5},{5,4},{6,7},{7,6},{8,9},{9,8},{10,11... | collective-permute-start | bytes 4718600 | tf_op jit(solution)/shard_map/ppermute | solution.py:244
  338.4 56.9 %collective-permute-start.33 = (bf16[1024,768]{1,0:T(8,128)(2,1)}, bf16[1024,768]{1,0:T(8,128)(2,1)}, u32[]{:S(2)}, u32[]{:S(2)}) collective-permute-start(bf16[1024,768]{1,0:T(8,128)(2,1)} %get-tuple-element.52), channel_id=1, source_target_pairs={{0,1},{1,0},{2,3},{3,2},{4,5},{5,4},{6,7},{7,6},{8,9},{9,8},{10,11... | collective-permute-start | bytes 4718600 | tf_op jit(solution)/shard_map/ppermute | solution.py:244
  343.5 25.8 %collective-permute-start.59 = (bf16[4,384,384]{2,1,0:T(8,128)(2,1)}, bf16[4,384,384]{2,1,0:T(8,128)(2,1)}, u32[]{:S(2)}, u32[]{:S(2)}) collective-permute-start(bf16[4,384,384]{2,1,0:T(8,128)(2,1)} %constant_dynamic-slice_fusion.2), channel_id=1, source_target_pairs={{0,4},{1,3},{2,6},{3,1},{4,0},{5,7},{6,2},{7,5},{8,12},{9,11},{10,... | collective-permute-start | bytes 3538952 | tf_op jit(solution)/shard_map/ppermute | solution.py:178
  348.7 29.3 %collective-permute-start.48 = (bf16[4,384,384]{2,1,0:T(8,128)(2,1)}, bf16[4,384,384]{2,1,0:T(8,128)(2,1)}, u32[]{:S(2)}, u32[]{:S(2)}) collective-permute-start(bf16[4,384,384]{2,1,0:T(8,128)(2,1)} %constant_dynamic-slice_fusion.13), channel_id=1, source_target_pairs={{0,2},{1,5},{2,0},{3,7},{4,6},{5,1},{6,4},{7,3},{8,10},{9,13},{10,... | collective-permute-start | bytes 3538952 | tf_op jit(solution)/shard_map/ppermute | solution.py:178
  353.3 38.4 %collective-permute-start.37 = (bf16[1544,384]{1,0:T(8,128)(2,1)S(1)}, bf16[1544,384]{1,0:T(8,128)(2,1)}, u32[]{:S(2)}, u32[]{:S(2)}) collective-permute-start(bf16[1544,384]{1,0:T(8,128)(2,1)S(1)} %pad_maximum_fusion.7), channel_id=1, source_target_pairs={{0,4},{1,3},{2,6},{3,1},{4,0},{5,7},{6,2},{7,5},{8,12},{9,11},{10,... | collective-permute-start | bytes 3557384 | tf_op jit(solution)/shard_map/ppermute | solution.py:178
  370.6 26.4 %collective-permute-start.60 = (bf16[4,192,384]{2,1,0:T(8,128)(2,1)S(1)}, bf16[4,192,384]{2,1,0:T(8,128)(2,1)S(1)}, u32[]{:S(2)}, u32[]{:S(2)}) collective-permute-start(bf16[4,192,384]{2,1,0:T(8,128)(2,1)S(1)} %add_convert_fusion.3), channel_id=1, source_target_pairs={{0,2},{1,5},{2,0},{3,7},{4,6},{5,1},{6,4},{7,3},{8,10},{9,13},{10,... | collective-permute-start | bytes 1769480 | tf_op jit(solution)/shard_map/ppermute | solution.py:178
  379.3 27.4 %collective-permute-start.49 = (bf16[4,192,384]{2,1,0:T(8,128)(2,1)S(1)}, bf16[4,192,384]{2,1,0:T(8,128)(2,1)S(1)}, u32[]{:S(2)}, u32[]{:S(2)}) collective-permute-start(bf16[4,192,384]{2,1,0:T(8,128)(2,1)S(1)} %add_convert_fusion.4), channel_id=1, source_target_pairs={{0,4},{1,3},{2,6},{3,1},{4,0},{5,7},{6,2},{7,5},{8,12},{9,11},{10,... | collective-permute-start | bytes 1769480 | tf_op jit(solution)/shard_map/ppermute | solution.py:178
  411.1 25.8 %collective-permute-start.52 = (bf16[4,48,384]{2,1,0:T(8,128)(2,1)S(1)}, bf16[4,48,384]{2,1,0:T(8,128)(2,1)S(1)}, u32[]{:S(2)}, u32[]{:S(2)}) collective-permute-start(bf16[4,48,384]{2,1,0:T(8,128)(2,1)S(1)} %get-tuple-element.112), channel_id=1, source_target_pairs={{0,24},{1,25},{2,26},{3,27},{4,28},{5,29},{6,30},{7,31},{8,0},{9,1... | collective-permute-start | bytes 442376 | tf_op jit(solution)/shard_map/ppermute | solution.py:178
  420.3 26.6 %collective-permute-start.40 = (bf16[193,384]{1,0:T(8,128)(2,1)S(1)}, bf16[193,384]{1,0:T(8,128)(2,1)S(1)}, u32[]{:S(2)}, u32[]{:S(2)}) collective-permute-start(bf16[193,384]{1,0:T(8,128)(2,1)S(1)} %pad_maximum_fusion.24), channel_id=1, source_target_pairs={{0,16},{1,17},{2,18},{3,19},{4,20},{5,21},{6,22},{7,23},{8,24},{9,... | collective-permute-start | bytes 444680 | tf_op jit(solution)/shard_map/ppermute | solution.py:178
  486.4 29.0 %collective-permute-start.68 = (bf16[4,384,384]{2,1,0:T(8,128)(2,1)S(1)}, bf16[4,384,384]{2,1,0:T(8,128)(2,1)S(1)}, u32[]{:S(2)}, u32[]{:S(2)}) collective-permute-start(bf16[4,384,384]{2,1,0:T(8,128)(2,1)S(1)} %pad_maximum_fusion.14), channel_id=1, source_target_pairs={{0,4},{1,3},{2,6},{3,1},{4,0},{5,7},{6,2},{7,5},{8,12},{9,11},{10,... | collective-permute-start | bytes 3538952 | tf_op jit(solution)/shard_map/ppermute | solution.py:178
  488.1 35.9 %collective-permute-start.57 = (bf16[4,384,384]{2,1,0:T(8,128)(2,1)S(1)}, bf16[4,384,384]{2,1,0:T(8,128)(2,1)S(1)}, u32[]{:S(2)}, u32[]{:S(2)}) collective-permute-start(bf16[4,384,384]{2,1,0:T(8,128)(2,1)S(1)} %pad_maximum_fusion.13), channel_id=1, source_target_pairs={{0,2},{1,5},{2,0},{3,7},{4,6},{5,1},{6,4},{7,3},{8,10},{9,13},{10,... | collective-permute-start | bytes 3538952 | tf_op jit(solution)/shard_map/ppermute | solution.py:178
  499.4 29.0 %collective-permute-start.46 = (bf16[1544,384]{1,0:T(8,128)(2,1)S(1)}, bf16[1544,384]{1,0:T(8,128)(2,1)S(1)}, u32[]{:S(2)}, u32[]{:S(2)}) collective-permute-start(bf16[1544,384]{1,0:T(8,128)(2,1)S(1)} %pad_maximum_fusion.8), channel_id=1, source_target_pairs={{0,4},{1,3},{2,6},{3,1},{4,0},{5,7},{6,2},{7,5},{8,12},{9,11},{10,... | collective-permute-start | bytes 3557384 | tf_op jit(solution)/shard_map/ppermute | solution.py:178
  (79 other events, 1252.2 us)

commit v2 on v0

v2 whole, which is shorter than its diff:
```python
import functools

import jax
import jax.numpy as jnp
from jax import lax
from jax.experimental import pallas as pl
from jax.experimental.pallas import tpu as pltpu
from jax.sharding import PartitionSpec as P

HD = 64
FF = 3072
SHORT = 128
LONG = 512
EPS = 1e-12
BF = jnp.bfloat16
F32 = jnp.float32
VMEM_BYTES = 60 * 2**20
BOTH = ("batch", "tensor")
ANY = pl.BlockSpec(memory_space=pl.ANY)
PLANES = 4
FAST_BATCH = 16


def dot(first_mat, second_mat):
    return lax.dot_general(
        first_mat, second_mat, (((1,), (0,)), ((), ())), preferred_element_type=F32
    )


def dot_nt(first_mat, second_mat):
    return lax.dot_general(
        first_mat, second_mat, (((1,), (1,)), ((), ())), preferred_element_type=F32
    )


def normalized(rows):
    centred = rows - jnp.mean(rows, axis=-1, keepdims=True)
    inverse = lax.rsqrt(jnp.mean(centred * centred, axis=-1, keepdims=True) + EPS)
    return centred * inverse, inverse


def norm_back(grad_scaled, normal, inverse):
    mean_grad = jnp.mean(grad_scaled, axis=-1, keepdims=True)
    mean_both = jnp.mean(grad_scaled * normal, axis=-1, keepdims=True)
    return inverse * (grad_scaled - mean_grad - normal * mean_both)


def row_sum(array_in):
    return jnp.sum(array_in, axis=0, keepdims=True)


def load_blocks(info_ref, parts, blocks, weight_ref, sem_ref):
    _, half_rows, cols = parts[0].shape
    copies = []
    for spot, (half, block) in enumerate(blocks):
        first = info_ref[2 + half]
        pair = []
        for at in range(2):
            start = pl.multiple_of((first if at == 0 else 1 - first) * half_rows, half_rows)
            pair.append(
                pltpu.make_async_copy(
                    parts[2 * half + at].at[block],
                    weight_ref.at[pl.ds(start, half_rows), pl.ds(spot * cols, cols)],
                    sem_ref.at[2 * spot + at],
                )
            )
        copies.append(pair)
    return copies


def after(array_in, *others):
    return lax.optimization_barrier((array_in, others))[0]


def first_time(copies):
    @pl.when(pl.program_id(0) == 0)
    def _():
        for pair in copies:
            for copy in pair:
                copy.wait()


def start_first(copies):
    @pl.when(pl.program_id(0) == 0)
    def _():
        for pair in copies:
            for copy in pair:
                copy.start()


PAIRED = [(half, block) for block in range(4) for half in range(2)]
SHARES = [(half, block) for half in range(2) for block in range(3)]
HALVED = [(half, block) for half in range(2) for block in range(4)]


def call(
    kernel, grid, in_specs, out_specs, out_shape, scratch, prefetch, flops, moved, exps=0, kept=None
):
    aliases = {}
    if kept is not None:
        given = prefetch + len(in_specs)
        count = len(kept)
        in_specs = in_specs + [ANY] * count
        aliases = {given + at: at for at in range(count)}
        inner = kernel

        def kernel(*refs):
            inner(*refs[:given], *refs[given + count :])

    return pl.pallas_call(
        kernel,
        input_output_aliases=aliases,
        out_shape=out_shape,
        grid_spec=pltpu.PrefetchScalarGridSpec(
            num_scalar_prefetch=prefetch,
            grid=grid,
            in_specs=in_specs,
            out_specs=out_specs,
            scratch_shapes=scratch,
        ),
        compiler_params=pltpu.CompilerParams(vmem_limit_bytes=VMEM_BYTES),
        cost_estimate=pl.CostEstimate(
            flops=30 * flops, bytes_accessed=moved, transcendentals=exps
        ),
    )


def struct(shape, kind):
    return jax.ShapeDtypeStruct(shape, kind)


def spread_kernel(
    base, row_step, block_step, cap, rows, info_ref, slot_ref, *refs
):
    sources, outs, (held_ref, quarter_ref, sem_ref) = refs[:4], refs[4:8], refs[8:]
    block = pl.program_id(0)
    quarter, plane, place = info_ref[0], info_ref[1], info_ref[2]
    copies = [
        [
            pltpu.make_async_copy(
                ref, held_ref.at[pl.ds(info_ref[3 + at] * cap, cap)], sem_ref.at[at]
            )
        ]
        for at, ref in enumerate(sources)
    ]
    start_first(copies)
    first_time(copies)
    total_slots = PLANES * cap
    for step in range(3):
        unit = base + (quarter * 3 + step) * row_step + block * block_step
        local = slot_ref[unit] - plane * total_slots
        here = (local >= 0) & (local < total_slots)
        spot = slice(step * rows, (step + 1) * rows)

        @pl.when(here)
        def _():
            quarter_ref[spot, :] = held_ref[local]

        @pl.when(jnp.logical_not(here))
        def _():
            quarter_ref[spot, :] = jnp.zeros((rows, quarter_ref.shape[1]), BF)

    for ahead, out_ref in enumerate(outs):
        size = out_ref.shape[1]
        start = pl.multiple_of(lax.rem(plane + ahead, PLANES) * size, size)
        out_ref[0] = quarter_ref[pl.ds(start, size), :]


def spread(sources, unit_slot, info, chunk):
    cap, rows, cols = sources[0].shape
    base, row_step, block_step = chunk
    size = 3 * rows // PLANES
    block = pl.BlockSpec((1, size, cols), lambda i, *_: (i, 0, 0))
    return call(
        functools.partial(spread_kernel, base, row_step, block_step, cap, rows),
        (4,),
        [ANY] * 4,
        [block] * 4,
        [struct((4, size, cols), BF)] * 4,
        [
            pltpu.VMEM((PLANES * cap, rows, cols), BF),
            pltpu.VMEM((3 * rows, cols), BF),
            pltpu.SemaphoreType.DMA((4,)),
        ],
        2,
        0,
        5 * 2**20,
    )(info, unit_slot, *sources)


def swap_pairs(orient, stage):
    pairs = []
    for place in range(FAST_BATCH):
        for core in range(2):
            first_bit = 2 if (core + orient) % 2 == 0 else 1
            bit = first_bit if stage == 1 else 3 - first_bit
            pairs.append((place * 2 + core, (place ^ bit) * 2 + core))
    return pairs


def flip_pairs(bit):
    return [
        (place * 2 + core, (place ^ bit) * 2 + core)
        for place in range(FAST_BATCH)
        for core in range(2)
    ]


def plane_pairs(step):
    return [
        (place * 2 + core, (place + 4 * step) % FAST_BATCH * 2 + core)
        for place in range(FAST_BATCH)
        for core in range(2)
    ]


def total(*terms):
    result = terms[0].astype(F32)
    for term in terms[1:]:
        result = result + term.astype(F32)
    return result.astype(BF)


def send(array_in, pairs):
    return lax.ppermute(array_in, BOTH, pairs)


def cut(array_in, start, size):
    return lax.dynamic_slice_in_dim(array_in, start, size, 1)


def first_split(info, mine, other):
    half = mine.shape[1] // 2
    return [
        total(cut(mine, at * half, half), cut(other, at * half, half))
        for at in (1 - info[0], info[0])
    ]


def second_split(info, kept, got):
    half = kept.shape[1] // 2
    start = (1 - info[1]) * half
    return total(cut(kept, start, half), cut(got, start, half))


def third_split(info, kept, one, two):
    half = two.shape[1]
    size = half // PLANES
    pieces = []
    for ahead in range(PLANES):
        start = (info[2] + ahead) % PLANES * size
        pieces.append(
            total(
                cut(kept, info[1] * half + start, size),
                cut(one, info[1] * half + start, size),
                cut(two, start, size),
            )
        )
    return pieces


def plane_join(info, pieces):
    return jnp.concatenate(
        [lax.select_n((info[2] - row) % PLANES, *pieces) for row in range(PLANES)], axis=1
    )


def half_join(info, here, there):
    low_first = info[1] == 0
    return jnp.concatenate(
        [jnp.where(low_first, here, there), jnp.where(low_first, there, here)], axis=1
    )


def exchange(going, kept, orient, info):
    (one,) = yield [(going, swap_pairs(orient, 1))]
    outgoing = second_split(info, kept, one)
    (two,) = yield [(outgoing, swap_pairs(orient, 2))]
    own, *pieces = third_split(info, kept, one, two)
    return (yield from spreading([own] + pieces, orient, info))


def spreading(pieces, orient, info):
    arrived = yield [(pieces[step], plane_pairs(step)) for step in range(1, PLANES)]
    owned = total(pieces[0], *arrived)
    others = yield [(owned, plane_pairs(step)) for step in range(1, PLANES)]
    level = plane_join(info, [owned] + others)
    (there,) = yield [(level, swap_pairs(orient, 2))]
    level = half_join(info, level, there)
    (there,) = yield [(level, swap_pairs(orient, 1))]
    return level, there


def quarters(info, mine, other):
    size = mine.shape[1] // 4
    at = info[0]
    return [
        total(cut(mine, (at ^ away) * size, size), cut(other, (at ^ away) * size, size))
        for away in range(4)
    ]


def plane_exchange(pieces, info):
    own, *going = pieces
    got = yield [(piece, flip_pairs(away)) for away, piece in zip((1, 2, 3), going)]
    size = own.shape[1] // PLANES
    parts = []
    for ahead in range(PLANES):
        start = (info[2] + ahead) % PLANES * size
        parts.append(total(*[cut(piece, start, size) for piece in [own] + got]))
    arrived = yield [(parts[step], plane_pairs(step)) for step in range(1, PLANES)]
    owned = total(parts[0], *arrived)
    others = yield [(owned, plane_pairs(step)) for step in range(1, PLANES)]
    level = plane_join(info, [owned] + others)
    there = yield [(level, flip_pairs(away)) for away in (1, 2, 3)]
    return [level] + there


def doubling(array_in):
    cores = [(at, at ^ 1) for at in range(2 * FAST_BATCH)]
    for pairs in [cores] + [flip_pairs(bit) for bit in (1, 2, 4, 8)]:
        (other,) = yield [(array_in, pairs)]
        array_in = array_in + other
    return array_in


class Chain:
    def __init__(self, steps):
        self.steps = steps
        self.result = None
        self.pending = next(steps)

    @property
    def ready(self):
        return [parts for parts, _ in self.pending]

    def take(self, arrived):
        try:
            self.pending = self.steps.send(arrived)
        except StopIteration as stop:
            self.pending, self.result = [], stop.value


def phase(chains=(), swaps=(), work=None):
    ready, swaps = lax.optimization_barrier(([chain.ready for chain in chains], list(swaps)))
    arrived = [
        [send(parts, pairs) for parts, (_, pairs) in zip(given, chain.pending)]
        for given, chain in zip(ready, chains)
    ]
    swapped = [core_swap(array) for array in swaps]
    done = None if work is None else work((ready, swaps))
    arrived, swapped, done = lax.optimization_barrier((arrived, swapped, done))
    for chain, parts in zip(chains, arrived):
        chain.take(parts)
    return swapped, done


def core_swap(array_in):
    return lax.ppermute(array_in, "tensor", [(0, 1), (1, 0)])


def seen_mask():
    key_at = lax.broadcasted_iota(jnp.int32, (2 * LONG, LONG), 0) % LONG // SHORT
    query_at = lax.broadcasted_iota(jnp.int32, (2 * LONG, LONG), 1) // SHORT
    return key_at == query_at


def low_lanes(rows):
    return lax.broadcasted_iota(jnp.int32, (rows, 2 * HD), 1) < HD


def pair_lanes(pair):
    return pl.ds(pl.multiple_of(pair * 2 * HD, 2 * HD), 2 * HD)


def both_heads(array_in):
    low = low_lanes(array_in.shape[0])
    none = jnp.zeros_like(array_in)
    return jnp.concatenate(
        [jnp.where(low, array_in, none), jnp.where(low, none, array_in)], axis=0
    )


def by_head(array_in):
    return array_in.reshape(2, LONG, array_in.shape[1])


def pair_columns(array_in):
    return jnp.where(low_lanes(LONG), array_in[:LONG], array_in[LONG:])


FORWARD_PAIRS = 2
BACKWARD_PAIRS = 1


def attend_pairs(first, short, q_ref, k_ref, v_ref, ctx_ref, lse_ref):
    pairs = range(FORWARD_PAIRS)
    lanes = [pair_lanes(first + pair) for pair in pairs]
    queries = [q_ref[:, at] * BF(HD**-0.5) for at in lanes]
    keys_here = [both_heads(k_ref[:, at]) for at in lanes]
    values_t = [v_ref[:, at].T for at in lanes]
    scores = [dot_nt(keys_here[pair], queries[pair]) for pair in pairs]
    if short:
        scores = [jnp.where(seen_mask(), score, -1e30) for score in scores]
    scores = [by_head(score) for score in scores]
    tops = [jnp.max(score, axis=1, keepdims=True) for score in scores]
    weights = [jnp.exp(score - top) for score, top in zip(scores, tops)]
    norms = [jnp.sum(weight, axis=1, keepdims=True) for weight in weights]
    probs = [(weight * (1.0 / norm)).astype(BF) for weight, norm in zip(weights, norms)]
    for pair in pairs:
        outs = [
            dot(values_t[pair][head * HD : (head + 1) * HD], probs[pair][head])
            for head in range(2)
        ]
        ctx_ref[:, lanes[pair]] = jnp.concatenate(outs, axis=0).T.astype(BF)
        for head in range(2):
            spot = pl.ds((first + pair) * 2 + head, 1)
            lse_ref[0, spot, :] = tops[pair][head] + jnp.log(norms[pair][head])


def forward_kernel(
    info_ref, x_ref, rows_ref, w0_ref, w1_ref, w2_ref, w3_ref,
    q_ref, k_ref, v_ref, ctx_ref, lse_ref, z_ref, xt_ref, w_ref, sem_ref,
):
    width = x_ref.shape[1]
    parts = (w0_ref, w1_ref, w2_ref, w3_ref)
    copies = load_blocks(info_ref, parts, PAIRED, w_ref, sem_ref)
    start_first(copies)
    tokens = x_ref[...]
    xt_ref[...] = tokens.T
    first_time(copies[:2])
    q_ref[...] = (dot(tokens, w_ref[:, :width]) + rows_ref[0:1]).astype(BF)
    first_time(copies[2:4])
    k_ref[...] = dot(tokens, w_ref[:, width : 2 * width]).astype(BF)
    first_time(copies[4:6])
    v_ref[...] = (dot(tokens, w_ref[:, 2 * width : 3 * width]) + rows_ref[1:2]).astype(BF)
    pairs = width // (2 * HD)

    def all_pairs(short):
        @pl.loop(0, pairs, step=FORWARD_PAIRS)
        def _(first):
            attend_pairs(first, short, q_ref, k_ref, v_ref, ctx_ref, lse_ref)

    @pl.when(info_ref[0] == 1)
    def _():
        all_pairs(False)

    @pl.when(info_ref[0] != 1)
    def _():
        all_pairs(True)

    first_time(copies[6:8])
    attended = dot_nt(ctx_ref[...], w_ref[:, 3 * width :])
    z_ref[...] = tokens.astype(F32) + attended + rows_ref[2:3]


def forward(group, info, tokens, rows, weights, kept=None):
    tok = tokens.shape[0] // 2
    width = tokens.shape[1]
    groups = tok // LONG
    tile = pl.BlockSpec((LONG, width), lambda i, *_: (group, 0))
    low = struct((tok, width), BF)
    return call(
        forward_kernel,
        (1,),
        [
            pl.BlockSpec((LONG, width), lambda i, info: (info[1] * groups + group, 0)),
            pl.BlockSpec((8, width), lambda i, *_: (0, 0)),
        ]
        + [ANY] * 4,
        [
            tile, tile, tile, tile,
            pl.BlockSpec((1, 16, LONG), lambda i, *_: (group, 0, 0)),
            tile,
            pl.BlockSpec((width, LONG), lambda i, *_: (0, group)),
        ],
        [
            low, low, low, low,
            struct((groups, 16, LONG), F32),
            struct((tok, width), F32),
            struct((width, tok), BF),
        ],
        [pltpu.VMEM((width, 4 * width), BF), pltpu.SemaphoreType.DMA((16,))],
        1,
        2 * LONG * width * (4 * width + 2 * LONG) * 2,
        12 * 2**20,
        LONG * LONG * 12,
        kept,
    )(info, tokens, rows, *weights, *(kept or ()))


def up_kernel(
    info_ref, z_ref, rows_ref, bias_ref, w0_ref, w1_ref, w2_ref, w3_ref,
    act_ref, slope_ref, ht_ref, hidden_ref, w_ref, sem_ref,
):
    width = z_ref.shape[1]
    parts = (w0_ref, w1_ref, w2_ref, w3_ref)
    copies = load_blocks(info_ref, parts, HALVED, w_ref, sem_ref)
    start_first(copies)
    normal, _ = normalized(z_ref[...])
    hidden = normal * rows_ref[3:4] + rows_ref[4:5]
    hidden_ref[...] = hidden
    low = hidden.astype(BF)
    ht_ref[...] = low.T
    for part in range(FF // width):
        spot = slice(part * width, (part + 1) * width)
        first_time(copies[2 * part : 2 * part + 2])
        upper = dot(low, w_ref[:, spot]) + bias_ref[part : part + 1]
        phi_sum = 0.5 + 0.5 * lax.erf(upper * (0.5**0.5))
        density = jnp.exp(-0.5 * upper * upper) * 0.3989422804014327
        act_ref[:, spot] = (upper * phi_sum).astype(BF)
        slope_ref[:, spot] = (phi_sum + upper * density).astype(BF)


TILE = 512
ROWS, COLUMNS, NORM_ROWS = 256, 256, 64
UP_TILE = 256


def feed_up(info, first, rows, bias, weights):
    tok, width = first.shape
    wide = struct((tok, FF), BF)
    return call(
        up_kernel,
        (tok // UP_TILE,),
        [
            pl.BlockSpec((UP_TILE, width), lambda i, *_: (i, 0)),
            pl.BlockSpec((8, width), lambda i, *_: (0, 0)),
            pl.BlockSpec((4, width), lambda i, *_: (0, 0)),
        ]
        + [ANY] * 4,
        [
            pl.BlockSpec((UP_TILE, FF), lambda i, *_: (i, 0)),
            pl.BlockSpec((UP_TILE, FF), lambda i, *_: (i, 0)),
            pl.BlockSpec((width, UP_TILE), lambda i, *_: (0, i)),
            pl.BlockSpec((UP_TILE, width), lambda i, *_: (i, 0)),
        ],
        [wide, wide, struct((width, tok), BF), struct((tok, width), F32)],
        [pltpu.VMEM((width, FF), BF), pltpu.SemaphoreType.DMA((16,))],
        1,
        2 * tok * width * FF,
        20 * 2**20,
        tok * FF * 2,
    )(info, first, rows, bias, *weights)


def down_kernel(
    info_ref, h_ref, act_ref, cot_ref, rows_ref, w0_ref, w1_ref, w2_ref, w3_ref,
    out_ref, dz_ref, gt_ref, dyt_ref, sum_ref, w_ref, branch_ref, low_ref, sem_ref,
):
    step = pl.program_id(0)
    width = h_ref.shape[1]
    tiles = act_ref.shape[0] // TILE

    parts = (w0_ref, w1_ref, w2_ref, w3_ref)
    copies = load_blocks(info_ref, parts, HALVED, w_ref, sem_ref)
    start_first(copies)

    @pl.when(step == 0)
    def _():
        sum_ref[...] = jnp.zeros_like(sum_ref)

    first_time(copies)

    @pl.when(step < tiles)
    def _():
        base = pl.multiple_of(step * TILE, TILE)
        for row in range(0, TILE, ROWS):
            spot = slice(row, row + ROWS)
            branch_ref[spot, :] = dot_nt(act_ref[pl.ds(base + row, ROWS), :], w_ref[...])
        gains = rows_ref[6:7]
        sums = [0.0, 0.0, 0.0]
        for row in range(0, TILE, NORM_ROWS):
            spot = slice(row, row + NORM_ROWS)
            normal, inverse = normalized(h_ref[spot, :] + branch_ref[spot, :] + rows_ref[5:6])
            out_ref[spot, :] = (normal * gains + rows_ref[7:8]).astype(BF)
            cot = cot_ref[spot, :].astype(F32)
            grad = norm_back(cot * gains, normal, inverse)
            dz_ref[spot, :] = grad
            low_ref[spot, :] = grad.astype(BF)
            for at, value in enumerate((grad, cot * normal, cot)):
                sums[at] = sums[at] + row_sum(value)
        dyt_ref[:, pl.ds(base, TILE)] = low_ref[...].T
        for at in range(3):
            sum_ref[at : at + 1] += sums[at]

    for part in range(2):
        @pl.when(step == tiles + part)
        def _():
            grad = dot(dyt_ref[...], act_ref[:, (part + 2) * width : (part + 3) * width])
            put_blocks(gt_ref, grad)


def put_blocks(ref, grad):
    cols = ref.shape[2]
    for block in range(ref.shape[0]):
        ref[block] = grad[:, block * cols : (block + 1) * cols].astype(BF)


def feed_down(info, hidden, act, cot, rows, weights):
    tok, width = hidden.shape
    tiles = tok // TILE
    last = tiles - 1
    row_tile = pl.BlockSpec((TILE, width), lambda i, *_: (jnp.minimum(i, last), 0))
    grads = struct((4, width, width // 2), BF)
    return call(
        down_kernel,
        (tiles + 2,),
        [
            row_tile,
            pl.BlockSpec((tok, FF), lambda i, *_: (0, 0)),
            pl.BlockSpec(
                (TILE, width), lambda i, info: (info[1] * tiles + jnp.minimum(i, last), 0)
            ),
            pl.BlockSpec((8, width), lambda i, *_: (0, 0)),
        ]
        + [ANY] * 4,
        [
            row_tile,
            row_tile,
            pl.BlockSpec((2, width, width // 2), lambda i, *_: (jnp.clip(i - tiles, 0, 1), 0, 0)),
            pl.BlockSpec((width, tok), lambda i, *_: (0, 0)),
            pl.BlockSpec((8, width), lambda i, *_: (0, 0)),
        ],
        [
            struct((tok, width), BF),
            struct((tok, width), F32),
            grads,
            struct((width, tok), BF),
            struct((8, width), F32),
        ],
        [
            pltpu.VMEM((width, FF), BF),
            pltpu.VMEM((TILE, width), F32),
            pltpu.VMEM((TILE, width), BF),
            pltpu.SemaphoreType.DMA((16,)),
        ],
        1,
        3 * tok * width * FF,
        30 * 2**20,
    )(info, hidden, act, cot, rows, *weights)


def back_kernel(info_ref, z_ref, dz2_ref, slope_ref, rows_ref, *refs):
    down, upper, other = refs[:4], refs[4:8], refs[8:12]
    dz1_ref, dctx_ref, dtt_ref, da_ref, sum_ref = refs[12:17]
    wd_ref, wu_ref, wo_ref, hidden_ref, low_ref, dsem_ref, usem_ref, osem_ref = refs[17:]
    width = z_ref.shape[1]
    downs = load_blocks(info_ref, down, HALVED, wd_ref, dsem_ref)
    ups = load_blocks(info_ref, upper, HALVED, wu_ref, usem_ref)
    outs = load_blocks(info_ref, other, [(0, 3), (1, 3)], wo_ref, osem_ref)
    for at in range(0, 8, 2):
        start_first(downs[at : at + 2] + ups[at : at + 2])
    start_first(outs)

    @pl.when(pl.program_id(0) == 0)
    def _():
        sum_ref[...] = jnp.zeros_like(sum_ref)

    tile = z_ref.shape[0]
    low_two = dz2_ref[...].astype(BF)
    for part in range(FF // width):
        first_time(downs[2 * part : 2 * part + 2])
        place = 4 + (part ^ (2 * info_ref[1]))
        for start in range(0, width, COLUMNS):
            lanes = slice(part * width + start, part * width + start + COLUMNS)
            grad_sum = 0.0
            for row in range(0, tile, ROWS):
                spot = slice(row, row + ROWS)
                grad_act = dot(low_two[spot], wd_ref[:, lanes])
                grad_up = (grad_act * slope_ref[spot, lanes].astype(F32)).astype(BF)
                da_ref[spot, lanes] = grad_up
                grad_sum = grad_sum + row_sum(grad_up.astype(F32))
            sum_ref[pl.ds(place, 1), start : start + COLUMNS] += grad_sum
    first_time(ups)
    for row in range(0, tile, ROWS):
        spot = slice(row, row + ROWS)
        hidden_ref[spot, :] = dz2_ref[spot, :] + dot_nt(da_ref[spot, :], wu_ref[...])
    gains = rows_ref[3:4]
    sums = [0.0, 0.0, 0.0]
    for row in range(0, tile, NORM_ROWS):
        spot = slice(row, row + NORM_ROWS)
        grad_hidden = hidden_ref[spot, :]
        normal, inverse = normalized(z_ref[spot, :])
        grad_one = norm_back(grad_hidden * gains, normal, inverse)
        sums[0] = sums[0] + row_sum(grad_one)
        sums[1] = sums[1] + row_sum(grad_hidden * normal)
        sums[2] = sums[2] + row_sum(grad_hidden)
        dz1_ref[spot, :] = grad_one
        low_ref[spot, :] = grad_one.astype(BF)
    for at in range(3):
        sum_ref[at : at + 1] += sums[at]
    dtt_ref[...] = low_ref[...].T
    first_time(outs)
    dctx_ref[...] = dot(low_ref[...], wo_ref[...]).astype(BF)


def feed_back(info, first, dz2, slope, rows, down, upper, other):
    tok, width = first.shape
    row_tile = pl.BlockSpec((TILE, width), lambda i, *_: (i, 0))
    wide_tile = pl.BlockSpec((TILE, FF), lambda i, *_: (i, 0))
    fixed = pl.BlockSpec((8, width), lambda i, *_: (0, 0))
    return call(
        back_kernel,
        (tok // TILE,),
        [row_tile, row_tile, wide_tile, fixed] + [ANY] * 12,
        [row_tile, row_tile, pl.BlockSpec((width, TILE), lambda i, *_: (0, i)), wide_tile, fixed],
        [
            struct((tok, width), F32),
            struct((tok, width), BF),
            struct((width, tok), BF),
            struct((tok, FF), BF),
            struct((8, width), F32),
        ],
        [
            pltpu.VMEM((width, FF), BF),
            pltpu.VMEM((width, FF), BF),
            pltpu.VMEM((width, width), BF),
            pltpu.VMEM((TILE, width), F32),
            pltpu.VMEM((TILE, width), BF),
            pltpu.SemaphoreType.DMA((16,)),
            pltpu.SemaphoreType.DMA((16,)),
            pltpu.SemaphoreType.DMA((4,)),
        ],
        1,
        4 * tok * width * FF,
        30 * 2**20,
    )(info, first, dz2, slope, rows, *down, *upper, *other)


def product_kernel(left_ref, right_ref, *outs):
    grad = dot(left_ref[...], right_ref[...])
    step = pl.program_id(0)
    for at, ref in enumerate(outs):
        @pl.when(step // 2 == at)
        def _():
            put_blocks(ref, grad)


def wide_grad(left_t, right, halves, blocks=4):
    width, tok = left_t.shape
    first = halves[0]
    spec = [
        pl.BlockSpec(
            (2, width, width // 2), lambda i, at=at: (jnp.clip(i - 2 * at, 0, 1), 0, 0)
        )
        for at in range(len(halves))
    ]
    return call(
        product_kernel,
        (2 * len(halves),),
        [
            pl.BlockSpec((width, tok), lambda i: (0, 0)),
            pl.BlockSpec((tok, width), lambda i: (0, (i + 2 * first) % 4)),
        ],
        spec,
        [struct((blocks, width, width // 2), BF)] * len(halves),
        [],
        0,
        tok * width * FF * len(halves),
        10 * 2**20 * len(halves),
    )(left_t, right)


def square_kernel(left_ref, right_ref, gm_ref, gt_ref):
    grad = dot(left_ref[...], right_ref[...])
    cols = gm_ref.shape[2]
    gm_ref[0] = grad[:, :cols].astype(BF)
    gt_ref[0] = grad[:, cols:].astype(BF)


def share_kernel(left_ref, right_ref, out_ref):
    put_blocks(out_ref, dot(left_ref[...], right_ref[...]))


def share_grad(left_t, right, half):
    width, tok = left_t.shape
    cols = right.shape[1] // 2
    shape = (3, width, cols // 3)
    return call(
        share_kernel,
        (1,),
        [
            pl.BlockSpec((width, tok), lambda i: (0, 0)),
            pl.BlockSpec((tok, cols), lambda i: (0, half)),
        ],
        [pl.BlockSpec(shape, lambda i: (0, 0, 0))],
        [struct(shape, BF)],
        [],
        0,
        2 * tok * width * cols,
        6 * 2**20,
    )(left_t, right)[0]


def square_grad(left_t, right, first=0, kept=None):
    width, tok = left_t.shape
    count = right.shape[1] // width
    block = pl.BlockSpec((1, width, width // 2), lambda i: (first + i, 0, 0))
    return call(
        square_kernel,
        (count,),
        [
            pl.BlockSpec((width, tok), lambda i: (0, 0)),
            pl.BlockSpec((tok, width), lambda i: (0, i)),
        ],
        [block, block],
        [struct((first + count, width, width // 2), BF)] * 2,
        [],
        0,
        2 * tok * width * width * count,
        4 * 2**20 * count,
        0,
        kept,
    )(left_t, right, *(kept or ()))


def attend_pairs_back(first, short, q_ref, k_ref, v_ref, dctx_ref, lse_ref, dqkv_ref):
    width = q_ref.shape[1]
    pairs = range(BACKWARD_PAIRS)
    lanes = [pair_lanes(first + pair) for pair in pairs]
    queries = [q_ref[:, at] * BF(HD**-0.5) for at in lanes]
    keys_here = [k_ref[:, at] for at in lanes]
    grads = [dctx_ref[:, at] for at in lanes]
    keys_t = [keys.T for keys in keys_here]
    scores = [dot_nt(both_heads(keys_here[pair]), queries[pair]) for pair in pairs]
    grad_probs = [
        by_head(dot_nt(both_heads(v_ref[:, lanes[pair]]), grads[pair])) for pair in pairs
    ]
    if short:
        scores = [jnp.where(seen_mask(), score, -1e30) for score in scores]
    probs = [
        jnp.exp(
            by_head(scores[pair])
            - jnp.stack(
                [lse_ref[0, pl.ds((first + pair) * 2 + head, 1), :] for head in range(2)]
            )
        )
        for pair in pairs
    ]
    grad_v = [
        dot(prob.astype(BF).reshape(2 * LONG, LONG), grads[pair])
        for pair, prob in enumerate(probs)
    ]
    inners = [
        jnp.sum(prob * grad, axis=1, keepdims=True) for prob, grad in zip(probs, grad_probs)
    ]
    grad_scores = [
        (prob * (grad - inner)).astype(BF)
        for prob, grad, inner in zip(probs, grad_probs, inners)
    ]
    grad_k = [
        dot(grad.reshape(2 * LONG, LONG), queries[pair]) for pair, grad in enumerate(grad_scores)
    ]
    for pair in pairs:
        grad_q = [
            dot(keys_t[pair][head * HD : (head + 1) * HD], grad_scores[pair][head])
            for head in range(2)
        ]

        def store(part, values_in):
            at = first + pair
            half = at // 3
            start = half * (3 * width // 2) + part * (width // 2) + (at - 3 * half) * 2 * HD
            dqkv_ref[:, pl.ds(pl.multiple_of(start, 2 * HD), 2 * HD)] = values_in.astype(BF)

        store(0, jnp.concatenate(grad_q, axis=0).T * HD**-0.5)
        store(1, pair_columns(grad_k[pair]))
        store(2, pair_columns(grad_v[pair]))


def attend_back_kernel(
    info_ref, q_ref, k_ref, v_ref, dctx_ref, lse_ref, dz_ref, w0_ref, w1_ref, w2_ref, w3_ref,
    dqkv_ref, gx_ref, sum_ref, w_ref, sem_ref,
):
    width = q_ref.shape[1]
    parts = (w0_ref, w1_ref, w2_ref, w3_ref)
    copies = load_blocks(info_ref, parts, SHARES, w_ref, sem_ref)
    start_first(copies)

    def all_pairs(short):
        @pl.loop(0, width // (2 * HD), step=BACKWARD_PAIRS)
        def _(first):
            attend_pairs_back(first, short, q_ref, k_ref, v_ref, dctx_ref, lse_ref, dqkv_ref)

    @pl.when(info_ref[0] == 1)
    def _():
        all_pairs(False)

    @pl.when(info_ref[0] != 1)
    def _():
        all_pairs(True)

    sum_ref[...] = jnp.zeros_like(sum_ref)
    cols = width // 2
    for half in range(2):
        core = info_ref[1] if half == 0 else 1 - info_ref[1]
        spot = pl.ds(pl.multiple_of(core * cols, cols), cols)
        for row, part in enumerate((0, 2)):
            start = (3 * half + part) * cols
            sum_ref[row : row + 1, spot] = row_sum(dqkv_ref[:, start : start + cols].astype(F32))
    first_time(copies)
    gx_ref[...] = (dz_ref[...] + dot_nt(dqkv_ref[...], w_ref[...])).astype(BF)


def attend_back(group, info, q, k, v, dctx, lse, dz, weights, kept=None):
    tok, width = q.shape
    tile = pl.BlockSpec((LONG, width), lambda i, *_: (group, 0))
    *results, sums = call(
        attend_back_kernel,
        (1,),
        [
            tile, tile, tile, tile,
            pl.BlockSpec((1, 16, LONG), lambda i, *_: (group, 0, 0)),
            tile,
        ]
        + [ANY] * 4,
        [
            pl.BlockSpec((LONG, 3 * width), lambda i, *_: (group, 0)),
            tile,
            pl.BlockSpec((8, width), lambda i, *_: (0, 0)),
        ],
        [struct((tok, 3 * width), BF), struct((tok, width), BF), struct((8, width), F32)],
        [pltpu.VMEM((width, 3 * width), BF), pltpu.SemaphoreType.DMA((12,))],
        1,
        2 * LONG * width * (3 * width + 10 * LONG),
        15 * 2**20,
        LONG * LONG * 12,
        kept,
    )(info, q, k, v, dctx, lse, dz, *weights, *(kept or ()))
    return results, sums


def adamw_update(weights_in, moment, square, average_in, gradient, rate, scalars):
    beta_one, beta_two, ema_decay, scale_one, scale_two = scalars
    moment_new = beta_one * moment + (1.0 - beta_one) * gradient
    square_new = beta_two * square + (1.0 - beta_two) * gradient * gradient
    moment_hat = moment_new * scale_one
    square_hat = square_new * scale_two
    weights_new = weights_in - rate * (
        moment_hat / (jnp.sqrt(square_hat) + 1e-08) + 0.01 * weights_in
    )
    average_new = ema_decay * average_in + (1.0 - ema_decay) * weights_new
    return weights_new, moment_new, square_new, average_new


SLOT_STEPS = 3
LATE = 4


def fetch_gradient(ref, table_ref, slot, held_ref, sem_ref, rows):
    spot = pl.ds(pl.multiple_of(table_ref[2, slot] * rows, rows), rows)
    return pltpu.make_async_copy(
        ref.at[table_ref[1, slot], spot], held_ref.at[slot], sem_ref.at[slot]
    )


def adamw_kernel(table_ref, scale_ref, w_ref, m_ref, s_ref, a_ref, *refs):
    grads, outs, (held_ref, sem_ref) = refs[:4], refs[4:8], refs[8:]
    step = pl.program_id(0)
    count, rows, _ = w_ref.shape

    @pl.when(step == 0)
    def _():
        @pl.loop(0, held_ref.shape[0])
        def _(slot):
            for at, ref in enumerate(grads):
                chosen = table_ref[0, slot] == at + LATE
                if at == 0:
                    chosen = table_ref[0, slot] <= LATE

                @pl.when(chosen)
                def _():
                    fetch_gradient(ref, table_ref, slot, held_ref, sem_ref, rows).start()

    scalars = [scale_ref[at] for at in range(5)]

    @pl.loop(0, count)
    def _(at):
        slot = step * count + at
        fetch_gradient(grads[0], table_ref, slot, held_ref, sem_ref, rows).wait()
        gradient = held_ref[slot].astype(F32) * scale_ref[8 + 2 * slot]
        results = adamw_update(
            w_ref[at], m_ref[at], s_ref[at], a_ref[at], gradient,
            scale_ref[9 + 2 * slot], scalars,
        )
        for ref, value in zip(outs, results):
            ref[at] = value


def adamw_slots(table, scales, states, grads):
    cap, rows, cols = states[0].shape
    steps = SLOT_STEPS if cap % SLOT_STEPS == 0 else 1
    own = pl.BlockSpec((cap // steps, rows, cols), lambda i, *_: (i, 0, 0))
    return call(
        adamw_kernel,
        (steps,),
        [own] * 4 + [ANY] * 4,
        [own] * 4,
        [struct(states[0].shape, F32)] * 4,
        [pltpu.VMEM((cap, rows, cols), BF), pltpu.SemaphoreType.DMA((cap,))],
        2,
        20 * cap * rows * cols,
        40 * cap * rows * cols,
    )(table, scales, *states, *grads)


def late_kernel(table_ref, scale_ref, *refs):
    states, grads, outs, scratch = refs[:4], refs[4:8], refs[8:12], refs[12:]
    state_ref, result_ref, held_ref, sem_ref, state_sem_ref, out_sem_ref = scratch
    cap, rows, _ = held_ref.shape
    scalars = [scale_ref[at] for at in range(5)]

    def loads(slot):
        return [
            pltpu.make_async_copy(ref.at[slot], state_ref.at[slot, at], state_sem_ref.at[slot, at])
            for at, ref in enumerate(states)
        ]

    def stores(slot):
        return [
            pltpu.make_async_copy(result_ref.at[slot, at], ref.at[slot], out_sem_ref.at[slot, at])
            for at, ref in enumerate(outs)
        ]

    def each(work):
        @pl.loop(0, cap)
        def _(slot):
            @pl.when(table_ref[0, slot] < LATE)
            def _():
                work(slot)

    def begin(slot):
        for at, ref in enumerate(grads):
            @pl.when(table_ref[0, slot] == at)
            def _():
                fetch_gradient(ref, table_ref, slot, held_ref, sem_ref, rows).start()
        for copy in loads(slot):
            copy.start()

    def update(slot):
        fetch_gradient(grads[0], table_ref, slot, held_ref, sem_ref, rows).wait()
        for copy in loads(slot):
            copy.wait()
        gradient = held_ref[slot].astype(F32) * scale_ref[8 + 2 * slot]
        results = adamw_update(
            *[state_ref[slot, at] for at in range(4)], gradient, scale_ref[9 + 2 * slot], scalars
        )
        for at, value in enumerate(results):
            result_ref[slot, at] = value
        for copy in stores(slot):
            copy.start()

    def finish(slot):
        for copy in stores(slot):
            copy.wait()

    each(begin)
    each(update)
    each(finish)


def adamw_late(table, scales, states, grads, kept):
    cap, rows, cols = states[0].shape
    return call(
        late_kernel,
        (1,),
        [ANY] * 8,
        [ANY] * 4,
        [struct(states[0].shape, F32)] * 4,
        [
            pltpu.VMEM((cap, 4, rows, cols), F32),
            pltpu.VMEM((cap, 4, rows, cols), F32),
            pltpu.VMEM((cap, rows, cols), BF),
            pltpu.SemaphoreType.DMA((cap,)),
            pltpu.SemaphoreType.DMA((cap, 4)),
            pltpu.SemaphoreType.DMA((cap, 4)),
        ],
        2,
        20 * cap * rows * cols,
        40 * cap * rows * cols,
        0,
        kept,
    )(table, scales, *states, *grads, *kept)


def on_device(
    tokens,
    cotangent,
    phase_of,
    unit_slot,
    step_count,
    learn_rates,
    decay_rates,
    master,
    first_moment,
    second_moment,
    average,
    vector_state,
):
    cap, unit_rows, cols = master.shape
    tok_rows, width = tokens.shape
    batch_count = lax.axis_size("batch")
    row_blocks = width // unit_rows
    col_blocks = FF // width
    core = lax.axis_index("tensor")
    place = lax.axis_index("batch")
    fast = batch_count == FAST_BATCH
    plane, y_at, x_at = place // 4, (place // 2) % 2, place % 2
    up_base = 4 * row_blocks
    down_base = up_base + row_blocks * col_blocks
    chunks = [(0, 1, row_blocks), (up_base, col_blocks, 1), (down_base, col_blocks, 1)]
    corner = jnp.stack([place % 4, place % 4, plane]).astype(jnp.int32)

    def coords(orient):
        y_first = (core + orient) % 2 == 0
        first = jnp.where(y_first, y_at, x_at)
        second = jnp.where(y_first, x_at, y_at)
        return jnp.stack([first, second, plane]).astype(jnp.int32)

    places = [coords(orient) for orient in range(2)]

    def chunk_units(chunk):
        base, row_step, block_step = chunk
        return base + jnp.arange(4)[:, None] * block_step + jnp.arange(row_blocks)[None] * row_step

    def spreads(sources, which):
        first_bit = jnp.where(core == 0, 2, 1)
        inner = place % 4
        numbers = jnp.stack(
            [
                places[0][0] * 2 + places[0][1], plane, place,
                inner, inner ^ first_bit, inner ^ (3 - first_bit), inner ^ 3,
            ]
        ).astype(jnp.int32)
        return [spread(sources, unit_slot, numbers, chunks[at]) for at in which]

    def weights_chain(pieces):
        return Chain(spreading(pieces, 0, places[0]))

    def weights_plain(at):
        local = unit_slot[chunk_units(chunks[at])] - place * cap
        own = (local >= 0) & (local < cap)
        blocks = jnp.take(master, jnp.clip(local, 0, cap - 1), axis=0)
        blocks = jnp.where(own[..., None, None], blocks, 0.0).astype(BF)
        return lax.psum(blocks.reshape(4, width, cols), "batch")

    def grads_chain(mine, other):
        going, kept = first_split(places[0], mine, other)
        return Chain(exchange(going, kept, 0, places[0]))

    def shared(array_in):
        half = array_in.shape[1] // 2
        parts = [array_in[:, :half], array_in[:, half:]]
        return parts + [core_swap(part) for part in parts]

    def halves_of(array_in):
        other = lax.dynamic_slice_in_dim(array_in, (1 - core) * cols, cols, array_in.ndim - 1)
        return lax.dynamic_slice_in_dim(array_in, core * cols, cols, array_in.ndim - 1), other

    def swapped(array_in):
        return jnp.concatenate(halves_of(array_in), axis=-1)

    def both(here, there):
        low_first = core == 0
        return jnp.concatenate(
            [jnp.where(low_first, here, there), jnp.where(low_first, there, here)], axis=0
        )

    count_f = step_count[0].astype(F32)
    scalars = [
        decay_rates[0],
        decay_rates[1],
        decay_rates[2],
        1.0 / (1.0 - decay_rates[0] ** count_f),
        1.0 / (1.0 - decay_rates[1] ** count_f),
    ]

    def vec_update(sums):
        vector_grads = jnp.concatenate(
            [sums[0:2], sums[8:11], sums[12:16], sums[16:19]], axis=0
        )
        grads_scaled = vector_grads * float(tok_rows * batch_count) ** (-0.5)
        vec_weights, vec_first, vec_second, vec_average = adamw_update(
            vector_state[0], vector_state[1], vector_state[2], vector_state[3],
            grads_scaled, learn_rates[4], scalars,
        )
        return (
            jnp.stack([vec_weights, vec_average]),
            jnp.stack([grads_scaled, vec_first]),
            vec_second,
        )

    my_ids = place * cap + jnp.arange(cap, dtype=jnp.int32)
    matches = unit_slot[None, :] == my_ids[:, None]
    unit_ids = jnp.arange(unit_slot.shape[0], dtype=jnp.int32)
    unit = jnp.sum(jnp.where(matches, unit_ids[None, :], 0), axis=1)
    occupied = jnp.any(matches, axis=1)
    is_up = (unit >= up_base) & (unit < down_base)
    is_down = unit >= down_base
    is_other = (unit >= 3 * row_blocks) & (unit < up_base)
    is_wide = is_up | is_down
    chunk_at = jnp.where(is_down, 2, jnp.where(is_up | is_other, 1, 0))
    local = unit - jnp.where(is_down, down_base, up_base)
    block_at = jnp.where(
        is_wide, local % col_blocks, jnp.where(is_other, col_blocks, unit // row_blocks)
    )
    row_at = jnp.where(is_wide, local // col_blocks, unit % row_blocks)
    kind = jnp.where(
        occupied,
        (unit >= 3 * row_blocks).astype(jnp.int32) + is_up.astype(jnp.int32) + 2 * is_down,
        0,
    )
    rates = jnp.sum(
        jnp.where(kind[:, None] == jnp.arange(4)[None, :], learn_rates[None, :4], 0.0), axis=1
    )
    quarter_rows, half_rows = row_blocks // 4, row_blocks // 2
    first_quarter, first_half = (corner[0], places[0][0]) if fast else (0, 0)
    array_at = jnp.where(
        chunk_at == 0,
        (row_at // quarter_rows) ^ first_quarter,
        2 + 2 * chunk_at + ((row_at // half_rows) ^ first_half),
    )
    row_at = jnp.where(chunk_at == 0, row_at % quarter_rows, row_at % half_rows)
    table = jnp.stack([array_at, block_at, row_at]).astype(jnp.int32)
    states = (master, first_moment, second_moment, average)
    scales = jnp.concatenate(
        [
            jnp.stack(scalars),
            jnp.zeros((3,), F32),
            jnp.stack([occupied.astype(F32), rates], axis=1).reshape(-1),
        ]
    )
    firsts = [places[0][0], places[1][0]] if fast else [0, 0]
    info = jnp.stack([phase_of[0], core, *firsts]).astype(jnp.int32)
    vectors = vector_state[0]
    rows = jnp.concatenate(
        [swapped(vectors[0:2]), vectors[2:5], vectors[9:12]], axis=0
    )
    upper = vectors[5:9].reshape(2, FF // 2)
    turned = jnp.concatenate([upper[1:], upper[:1]], axis=0)
    bias_up = jnp.where(core == 0, upper, turned).reshape(4, width)

    if fast:
        low_master = master.astype(BF)
        beside = lax.ppermute(low_master, BOTH, swap_pairs(0, 1))
        across = lax.ppermute(low_master, BOTH, swap_pairs(0, 2))
        diagonal = lax.ppermute(beside, BOTH, swap_pairs(0, 2))
        sources = (low_master, beside, across, diagonal)
        io = weights_chain(spreads(sources, (0,))[0])
        _, (up, down) = phase([io], work=lambda _: spreads(sources, (1, 2)))
        up, down = weights_chain(up), weights_chain(down)
        phase([io])
        phase([io, up])
        theirs_first, _ = phase([io, up], io.ready)
        theirs_last, _ = phase([up, down], io.result[1:])
        weights_io = [*io.result, *theirs_first, *theirs_last]
        theirs_first, stage = phase(
            [up, down],
            up.ready,
            lambda late: forward(0, after(info, late), tokens, rows, weights_io),
        )
        theirs_last, stage = phase(
            [down],
            up.result[1:],
            lambda late: forward(1, after(info, late), tokens, rows, weights_io, kept=stage),
        )
        weights_up = [*up.result, *theirs_first, *theirs_last]
        q, k, v, ctx, lse, first, x_t = stage
        theirs_first, (act, slope, hidden_t, hidden) = phase(
            [down],
            down.ready,
            lambda late: feed_up(after(info, late), first, rows, bias_up, weights_up),
        )
        theirs_last, _ = phase(swaps=down.result[1:])
        weights_down = [*down.result, *theirs_first, *theirs_last]
    else:
        weights_io, weights_up, weights_down = [shared(weights_plain(at)) for at in range(3)]
        stage = None
        for group in range(tok_rows // 2 // LONG):
            stage = forward(group, info, tokens, rows, weights_io, kept=stage)
        q, k, v, ctx, lse, first, x_t = stage
        act, slope, hidden_t, hidden = feed_up(info, first, rows, bias_up, weights_up)

    out_half, dz2, down_theirs, grad_two_t, sums_two = feed_down(
        info, hidden, act, cotangent, rows, weights_down
    )
    heads = (q, k, v)

    def back(info):
        return feed_back(
            info, first, dz2, slope, rows, weights_down, weights_up, weights_io
        )

    def heads_back(group, info, dctx, dz1, kept=None):
        return attend_back(group, info, *heads, dctx, lse, dz1, weights_io, kept=kept)

    if fast:
        (other,), (down_mine,) = phase(
            swaps=[down_theirs], work=lambda late: wide_grad(after(grad_two_t, late), act, (0,))
        )
        down = grads_chain(down_mine, other)
        (out_other,), (dz1, dctx, dt_t, grad_up, sums_one) = phase(
            [down], [out_half], lambda late: back(after(info, late))
        )
        _, (up_mine, up_theirs) = phase(
            [down],
            work=lambda late: square_grad(
                dt_t, ctx, 4, wide_grad(after(hidden_t, late), grad_up, (0, 1), 5)
            ),
        )
        (other,), (kept, sums_zero) = phase(
            [down], [up_theirs], lambda late: heads_back(0, after(info, late), dctx, dz1)
        )
        up = grads_chain(up_mine, other)
        _, (kept, sums_extra) = phase(
            [down, up],
            work=lambda late: heads_back(1, after(info, late), dctx, dz1, kept),
        )
        dqkv, grad_x = kept
        vec = Chain(doubling(jnp.concatenate([sums_zero + sums_extra, sums_one, sums_two])))
        _, io_theirs = phase(
            [down, up, vec], work=lambda late: share_grad(after(x_t, late), dqkv, 1)
        )
        (other,), io_mine = phase(
            [down, up, vec], [io_theirs], lambda late: share_grad(after(x_t, late), dqkv, 0)
        )
        io = Chain(plane_exchange(quarters(corner, io_mine, other), corner))
        (grad_x_other,), out = phase(
            [io, up, vec], [grad_x], lambda late: both(after(out_half, late), out_other)
        )
        _, input_grad = phase(
            [io, up, vec],
            work=lambda late: both(after(grad_x, late), grad_x_other).astype(F32),
        )
        phase([io, up, vec])
        _, (new_states, vec_outs) = phase(
            [io],
            work=lambda late: (
                adamw_slots(after(table, late), scales, states, [*up.result, *down.result]),
                vec_update(after(vec.result, late)),
            ),
        )
        grads = io.result
    else:
        dz1, dctx, dt_t, grad_up, sums_one = back(info)
        kept, sums_zero = None, 0.0
        for group in range(tok_rows // 2 // LONG):
            kept, sums_extra = heads_back(group, info, dctx, dz1, kept)
            sums_zero = sums_zero + sums_extra
        dqkv, grad_x = kept
        up_mine, up_theirs = square_grad(
            dt_t, ctx, 4, wide_grad(hidden_t, grad_up, (0, 1), 5)
        )
        (down_mine,) = wide_grad(grad_two_t, act, (0,))
        grads = []
        for mine, theirs, parts in (
            (share_grad(x_t, dqkv, 0), share_grad(x_t, dqkv, 1), 4),
            (up_mine, up_theirs, 2),
            (down_mine, down_theirs, 2),
        ):
            grad = lax.psum(total(mine, core_swap(theirs)), "batch")
            grads += jnp.split(grad, parts, axis=1)
        new_states = adamw_slots(table, scales, states, grads[4:])
        grads = grads[:4]
        vec_outs = vec_update(
            lax.psum(jnp.concatenate([sums_zero, sums_one, sums_two]), BOTH)
        )
        out = both(out_half, core_swap(out_half))
        input_grad = both(grad_x, core_swap(grad_x)).astype(F32)

    new_states = adamw_late(table, scales, states, grads, new_states)
    return (out, input_grad, *new_states, *vec_outs)


def solution(mesh):
    return jax.shard_map(
        on_device,
        mesh=mesh,
        in_specs=(
            P("batch", None),
            P("batch", None),
            P("batch"),
            P(),
            P(),
            P(),
            P(),
            P("batch", None, "tensor"),
            P("batch", None, "tensor"),
            P("batch", None, "tensor"),
            P("batch", None, "tensor"),
            P(),
        ),
        out_specs=(
            P("batch", None),
            P("batch", None),
            P("batch", None, "tensor"),
            P("batch", None, "tensor"),
            P("batch", None, "tensor"),
            P("batch", None, "tensor"),
            P(),
            P(),
            P(),
        ),
        check_vma=False,
    )
```

time: 1180 us -> 470 us (0.40)
  waiting for transfers between devices: 595 us -> 112 us
  local copies, waits for them, and re-layouts: 247 us -> 10.2 us
  Pallas kernels: 0 us -> 185 us
  matrix products: 168 us -> 0 us
  starting transfers between devices: 0.65 us -> 94.2 us
  blocking collectives: 43.4 us -> 0 us
  other arithmetic: 89.6 us -> 54.5 us
  between operations: 20.2 us -> 6.9 us
    reduce_scatter x1 -> x0, waiting for transfers between devices: 342 us -> none  [on_device(): lax.psum_scatter(jnp.where(row_used[:, None, None], jnp.take(unit_grads,...]
    pallas_call x0 -> x17, Pallas kernels: none -> 185 us  [the longest x2 33.3 us: attend_back(): call(attend_back_kernel, (1,), [tile, tile, tile, tile, pl.BlockSpec((1,...]
    dot_general x46 -> x0, matrix products: 168 us -> none  [the longest x6 66.4 us: product(): return jnp.dot(first_mat, second_mat, preferred_element_type=jnp.float32)]
    all_gather x1 -> x0, waiting for transfers between devices: 168 us -> none  [on_device(): every_slot = lax.all_gather(low_master, 'batch', axis=0, tiled=True)]
    ppermute x0 -> x75, waiting for transfers between devices: none -> 112 us  [the longest x61 79.5 us: send(): return lax.ppermute(array_in, BOTH, pairs)]
    ppermute x0 -> x75, starting transfers between devices: none -> 94.2 us  [the longest x61 86.6 us: send(): return lax.ppermute(array_in, BOTH, pairs)]
    psum x4 -> x0, waiting for transfers between devices: 85.4 us -> none  [the longest x1 33.3 us: on_device(): branch = lax.psum(with_transposed(active_low, w_down), 'tensor')]
    reshape x27 -> x1, local copies, waits for them, and re-layouts: 49.8 us -> 0.09 us  [on_device(): jnp.stack([occupied.astype(F32), rates], axis=1).reshape(-1)]
  transfers between devices with their start and end apart: 6 -> 75, of which waited for: 5 -> 21; matrix products, arithmetic and copies ran while one was open for 8% -> 5% of each run, Pallas kernels for 0% -> 33%
where the time goes in v2:
time: 470 us; the launch traced here: 463 us
  Pallas kernels  185 us (39%)
  waiting for transfers between devices  112 us (24%)
  starting transfers between devices  94.2 us (20%)
  other arithmetic  54.5 us (12%)
  local copies, waits for them, and re-layouts  10.2 us (2%)
  between operations  6.9 us (1%)
    ppermute x61, starting transfers between devices, send(): return lax.ppermute(array_in, BOTH, pairs)  86.6 us
    ppermute x61, waiting for transfers between devices, send(): return lax.ppermute(array_in, BOTH, pairs)  79.5 us
    pallas_call x2, Pallas kernels, attend_back(): call(attend_back_kernel, (1,), [tile, tile, tile, tile, pl.BlockSpec((1,...  33.3 us
    pallas_call x2, Pallas kernels, forward(): call(forward_kernel, (1,), [pl.BlockSpec((LONG, width), lambda i, info: (...  28.7 us
    pallas_call x1, Pallas kernels, feed_back(): call(back_kernel, (tok // TILE,), [row_tile, row_tile, wide_tile, fixed]...  24.3 us
    convert_element_type x14, other arithmetic, total(): return result.astype(BF)  23.8 us
    pallas_call x1, Pallas kernels, feed_down(): call(down_kernel, (tiles + 2,), [row_tile, pl.BlockSpec((tok, FF), lambda...  19.7 us
    ppermute x1, waiting for transfers between devices, on_device(): beside = lax.ppermute(low_master, BOTH, swap_pairs(0, 1))  18.5 us
  transfers between devices with their start and end apart: 75, of which 21 were waited for; matrix products, arithmetic and copies ran while one was open for 5% of the time, Pallas kernels for 33%

profile of v2, /device:TPU:0, one launch (start us, length us, event | category | flops | bytes accessed | tf_op | source)
XLA Modules:
  0.0 462.6 jit_solution(10153845088855459613)
XLA Ops:
  6.8 18.5 %collective-permute-done.refs_1_ = bf16[18,64,384]{2,1,0:T(8,128)(2,1)S(1)} collective-permute-done((bf16[18,64,384]{2,1,0:T(8,128)(2,1)S(1)}, bf16[18,64,384]{2,1,0:T(8,128)(2,1)S(1)}, u32[]{:S(2)}, u32[]{:S(2)}) %collective-permute-start) | collective-permute-done | bytes 884768 | tf_op jit(solution)/shard_map/ppermute | solution.py:1246
  27.4 11.0 %collective-permute-done.2.refs_3_ = bf16[18,64,384]{2,1,0:T(8,128)(2,1)S(1)} collective-permute-done((bf16[18,64,384]{2,1,0:T(8,128)(2,1)S(1)}, bf16[18,64,384]{2,1,0:T(8,128)(2,1)S(1)}, u32[]{:S(2)}, u32[]{:S(2)}) %collective-permute-start.2) | collective-permute-done | bytes 884768 | tf_op jit(solution)/shard_map/ppermute | solution.py:1248
  54.2 4.4 shard_map.188
  97.7 5.7 %collective-permute-done.15 = bf16[4,48,384]{2,1,0:T(8,128)(2,1)S(1)} collective-permute-done((bf16[4,48,384]{2,1,0:T(8,128)(2,1)S(1)}, bf16[4,48,384]{2,1,0:T(8,128)(2,1)S(1)}, u32[]{:S(2)}, u32[]{:S(2)}) %collective-permute-start.15) | collective-permute-done | bytes 147488 | tf_op jit(solution)/shard_map/ppermute | solution.py:225
  117.2 5.2 %collective-permute-done.20 = bf16[4,48,384]{2,1,0:T(8,128)(2,1)S(1)} collective-permute-done((bf16[4,48,384]{2,1,0:T(8,128)(2,1)}, bf16[4,48,384]{2,1,0:T(8,128)(2,1)S(1)}, u32[]{:S(2)}, u32[]{:S(2)}) %collective-permute-start.20) | collective-permute-done | bytes 147488 | tf_op jit(solution)/shard_map/ppermute | solution.py:225
  132.2 14.4 %shard_map.190 = (bf16[1024,768]{1,0:T(8,128)(2,1)}, bf16[1024,768]{1,0:T(8,128)(2,1)}, bf16[1024,768]{1,0:T(8,128)(2,1)}, bf16[1024,768]{1,0:T(8,128)(2,1)}, f3...) custom-call(s32[4]{0:T(128)} %pad_add_fusion.1.info_ref.refs_0_, bf16[2048,768]{1,0:T(8,128)(2,1)} %refs_1_.1, ...), custom_call_target="tpu_custom_call" | custom-call | flops 193273528320 | bytes 12582912 | tf_op jit(solution)/shard_map/pallas_call | solution.py:463
  150.4 14.3 %shard_map.191 = (bf16[1024,768]{1,0:T(8,128)(2,1)}, bf16[1024,768]{1,0:T(8,128)(2,1)}, bf16[1024,768]{1,0:T(8,128)(2,1)}, bf16[1024,768]{1,0:T(8,128)(2,1)}, f3...) custom-call(s32[4]{0:T(128)} %pad_add_fusion.1.info_ref.refs_0_, ...), custom_call_target="tpu_custom_call", output_to_operand_aliasing={{0}: (7, {}), {1}: (8, {}), {2}: (9, {}), {3}: (10, {}), {4... | custom-call | flops 193273528320 | bytes 12582912 | tf_op jit(solution)/shard_map/pallas_call | solution.py:463
  167.6 18.3 %shard_map.192 = (bf16[1024,3072]{1,0:T(8,128)(2,1)}, bf16[1024,3072]{1,0:T(8,128)(2,1)}, bf16[768,1024]{1,0:T(8,128)(2,1)}, f32[1024,768]{1,0:T(8,128)}) custom-call(s32[4]{0:T(128)} %pad_add_fusion.1.info_ref.refs_0_, f32[1024,768]{1,0:T(8,128)} %get-tuple-element.370.z_ref, f32[8,768]{1,0:T(8,128)} %pad_maximum_fusion.17.rows_ref.refs_2_, ...), custom_call_target="tpu_custom_call" | custom-call | flops 144955146240 | bytes 20971520 | tf_op jit(solution)/shard_map/pallas_call | solution.py:523
  190.1 19.7 %shard_map.193 = (bf16[1024,768]{1,0:T(8,128)(2,1)}, f32[1024,768]{1,0:T(8,128)}, bf16[4,768,384]{2,1,0:T(8,128)(2,1)}, bf16[768,1024]{1,0:T(8,128)(2,1)}, f32[8,768]{1,0:T(8,128)}) custom-call(s32[4]{0:T(128)} %pad_add_fusion.1.info_ref.refs_0_, f32[1024,768]{1,0:T(8,128)} %get-tuple-element.377.h_ref, ...), custom_call_target="tpu_custom_call" | custom-call | flops 217432719360 | bytes 31457280 | tf_op jit(solution)/shard_map/pallas_call | solution.py:606
  210.2 6.0 %shard_map.194 = bf16[4,768,384]{2,1,0:T(8,128)(2,1)} custom-call(bf16[768,1024]{1,0:T(8,128)(2,1)} %get-tuple-element.383.left_ref, bf16[1024,3072]{1,0:T(8,128)(2,1)} %get-tuple-element.378.act_ref.right_ref), custom_call_target="tpu_custom_call" | custom-call | flops 72477573120 | bytes 10485760 | tf_op jit(solution)/shard_map/pallas_call | solution.py:749
  222.0 24.3 %shard_map.195 = (f32[1024,768]{1,0:T(8,128)}, bf16[1024,768]{1,0:T(8,128)(2,1)}, bf16[768,1024]{1,0:T(8,128)(2,1)}, bf16[1024,3072]{1,0:T(8,128)(2,1)}, f32[8,768]{1,0:T(8,128)}) custom-call(s32[4]{0:T(128)} %pad_add_fusion.1.info_ref.refs_0_, f32[1024,768]{1,0:T(8,128)} %get-tuple-element.370.z_ref, f32[1024,768]{1,0:T(8,128)} %get-tuple-element.390.dz2_ref, ...), custom_call_target="tpu_custom_call" | custom-call | flops 289910292480 | bytes 31457280 | tf_op jit(solution)/shard_map/pallas_call | solution.py:703
  249.5 9.8 %shard_map.196 = (bf16[5,768,384]{2,1,0:T(8,128)(2,1)}, bf16[5,768,384]{2,1,0:T(8,128)(2,1)}) custom-call(bf16[768,1024]{1,0:T(8,128)(2,1)} %get-tuple-element.401.left_ref, bf16[1024,3072]{1,0:T(8,128)(2,1)} %get-tuple-element.402.right_ref), custom_call_target="tpu_custom_call" | custom-call | flops 144955146240 | bytes 20971520 | tf_op jit(solution)/shard_map/pallas_call | solution.py:749
  269.7 16.7 %shard_map.198 = (bf16[1024,2304]{1,0:T(8,128)(2,1)}, bf16[1024,768]{1,0:T(8,128)(2,1)}, f32[8,768]{1,0:T(8,128)}) custom-call(s32[4]{0:T(128)} %pad_add_fusion.1.info_ref.refs_0_, bf16[1024,768]{1,0:T(8,128)(2,1)} %get-tuple-element.414.q_ref.refs_1_, bf16[1024,768]{1,0:T(8,128)(2,1)} %get-tuple-element.415.k_ref.refs_2_, ...), custom_call_target="tpu_custom_call" | custom-call | flops 175154135040 | bytes 15728640 | tf_op jit(solution)/shard_map/pallas_call | solution.py:909
  286.4 5.0 %add_convert_fusion = (bf16[5,384,384]{2,1,0:T(8,128)(2,1)}, bf16[5,384,384]{2,1,0:T(8,128)(2,1)}) fusion(bf16[5,768,384]{2,1,0:T(8,128)(2,1)} %collective-permute-done.40, s32[]{:T(128)S(6)} %select_n.1065, bf16[5,768,384]{2,1,0:T(8,128)(2,1)} %get-tuple-element.426, s32[]{:T(128)S(6)} %select_n.1067), kind=kLoop, calls=%fused_computation.2 | loop fusion | flops 5898240 | bytes 8847368 | tf_op jit(solution)/shard_map/convert_element_type | solution.py:221
  299.0 16.6 %shard_map.199 = (bf16[1024,2304]{1,0:T(8,128)(2,1)}, bf16[1024,768]{1,0:T(8,128)(2,1)}, f32[8,768]{1,0:T(8,128)}) custom-call(s32[4]{0:T(128)} %pad_add_fusion.1.info_ref.refs_0_, bf16[1024,768]{1,0:T(8,128)(2,1)} %get-tuple-element.414.q_ref.refs_1_, ...), custom_call_target="tpu_custom_call", output_to_operand_aliasing={{0}: (11, {}), {1}: (12, {})} | custom-call | flops 175154135040 | bytes 15728640 | tf_op jit(solution)/shard_map/pallas_call | solution.py:909
  321.9 5.5 %shard_map.200 = bf16[3,768,384]{2,1,0:T(8,128)(2,1)} custom-call(bf16[768,1024]{1,0:T(8,128)(2,1)} %get-tuple-element.462.left_ref, bf16[1024,2304]{1,0:T(8,128)(2,1)} %get-tuple-element.451.right_ref), custom_call_target="tpu_custom_call" | custom-call | flops 54358179840 | bytes 6291456 | tf_op jit(solution)/shard_map/pallas_call | solution.py:780
  327.4 10.3 %collective-permute-done.45 = bf16[4,192,384]{2,1,0:T(8,128)(2,1)} collective-permute-done((bf16[4,192,384]{2,1,0:T(8,128)(2,1)}, bf16[4,192,384]{2,1,0:T(8,128)(2,1)}, u32[]{:S(2)}, u32[]{:S(2)}) %collective-permute-start.45) | collective-permute-done | bytes 589856 | tf_op jit(solution)/shard_map/ppermute | solution.py:225
  347.8 5.5 %shard_map.201 = bf16[3,768,384]{2,1,0:T(8,128)(2,1)} custom-call(bf16[768,1024]{1,0:T(8,128)(2,1)} %get-tuple-element.462.left_ref, bf16[1024,2304]{1,0:T(8,128)(2,1)} %get-tuple-element.451.right_ref), custom_call_target="tpu_custom_call" | custom-call | flops 54358179840 | bytes 6291456 | tf_op jit(solution)/shard_map/pallas_call | solution.py:780
  353.4 6.7 %collective-permute-done.50 = bf16[5,48,384]{2,1,0:T(8,128)(2,1)S(1)} collective-permute-done((bf16[5,48,384]{2,1,0:T(8,128)(2,1)}, bf16[5,48,384]{2,1,0:T(8,128)(2,1)S(1)}, u32[]{:S(2)}, u32[]{:S(2)}) %collective-permute-start.50) | collective-permute-done | bytes 184352 | tf_op jit(solution)/shard_map/ppermute | solution.py:225
  377.9 8.0 %collective-permute-done.58 = bf16[5,48,384]{2,1,0:T(8,128)(2,1)S(1)} collective-permute-done((bf16[5,48,384]{2,1,0:T(8,128)(2,1)}, bf16[5,48,384]{2,1,0:T(8,128)(2,1)S(1)}, u32[]{:S(2)}, u32[]{:S(2)}) %collective-permute-start.58) | collective-permute-done | bytes 184352 | tf_op jit(solution)/shard_map/ppermute | solution.py:225
  420.7 10.3 %collective-permute-done.71 = f32[24,768]{1,0:T(8,128)S(1)} collective-permute-done((f32[24,768]{1,0:T(8,128)S(1)}, f32[24,768]{1,0:T(8,128)S(1)}, u32[]{:S(2)}, u32[]{:S(2)}) %collective-permute-start.71) | collective-permute-done | bytes 73760 | tf_op jit(solution)/shard_map/ppermute | solution.py:225
  434.8 9.4 %shard_map.202 = (f32[18,64,384]{2,1,0:T(8,128)}, f32[18,64,384]{2,1,0:T(8,128)}, f32[18,64,384]{2,1,0:T(8,128)}, f32[18,64,384]{2,1,0:T(8,128)}) custom-call(s32[3,18]{1,0:T(4,128)} %pad_add_fusion.table_ref.refs_0_, f32[44]{0:T(128)} %concatenate.109.scale_ref.refs_1_, f32[18,64,384]{2,1,0:T(8,128)} %refs_2_.1, f32[18,64,384]{2,1,0:T(8,128)} %refs_3_.1, ...), custom_call_target="tpu_custom_call" | custom-call | flops 265420800 | bytes 17694720 | tf_op jit(solution)/shard_map/pallas_call | solution.py:995
  448.2 5.3 %collective-permute-done.74.refs_9_ = bf16[3,192,384]{2,1,0:T(8,128)(2,1)S(1)} collective-permute-done((bf16[3,192,384]{2,1,0:T(8,128)(2,1)S(1)}, bf16[3,192,384]{2,1,0:T(8,128)(2,1)S(1)}, u32[]{:S(2)}, u32[]{:S(2)}) %collective-permute-start.74) | collective-permute-done | bytes 442400 | tf_op jit(solution)/shard_map/ppermute | solution.py:225
  454.9 7.2 %shard_map.203 = (f32[18,64,384]{2,1,0:T(8,128)}, f32[18,64,384]{2,1,0:T(8,128)}, f32[18,64,384]{2,1,0:T(8,128)}, f32[18,64,384]{2,1,0:T(8,128)}) custom-call(s32[3,18]{1,0:T(4,128)} %pad_add_fusion.table_ref.refs_0_, f32[44]{0:T(128)} %concatenate.109.scale_ref.refs_1_, ...), custom_call_target="tpu_custom_call", output_to_operand_aliasing={{0}: (10, {}), {1}: (11, {}), {2}: (12, {}), {3}: (13, {})} | custom-call | flops 265420800 | bytes 17694720 | tf_op jit(solution)/shard_map/pallas_call | solution.py:1065
  (305 shorter events, 197.3 us)
Async XLA Ops:
  2.3 23.0 %collective-permute-start = (bf16[18,64,384]{2,1,0:T(8,128)(2,1)S(1)}, bf16[18,64,384]{2,1,0:T(8,128)(2,1)S(1)}, u32[]{:S(2)}, u32[]{:S(2)}) collective-permute-start(bf16[18,64,384]{2,1,0:T(8,128)(2,1)S(1)} %convert_element_type.376.refs_0_), channel_id=1, source_target_pairs={{0,4},{1,3},{2,6},{3,1},{4,0},{5,7},{6,2},{7,5},{8,12},{9,11},{10,... | collective-permute-start | bytes 2654216 | tf_op jit(solution)/shard_map/ppermute | solution.py:1246
  5.3 22.0 %collective-permute-start.1 = (bf16[18,64,384]{2,1,0:T(8,128)(2,1)S(1)}, bf16[18,64,384]{2,1,0:T(8,128)(2,1)S(1)}, u32[]{:S(2)}, u32[]{:S(2)}) collective-permute-start(bf16[18,64,384]{2,1,0:T(8,128)(2,1)S(1)} %convert_element_type.376.refs_0_), channel_id=1, source_target_pairs={{0,2},{1,5},{2,0},{3,7},{4,6},{5,1},{6,4},{7,3},{8,10},{9,13},{10,... | collective-permute-start | bytes 2654216 | tf_op jit(solution)/shard_map/ppermute | solution.py:1247
  103.5 18.9 %collective-permute-start.22 = (bf16[4,384,384]{2,1,0:T(8,128)(2,1)S(1)}, bf16[4,384,384]{2,1,0:T(8,128)(2,1)}, u32[]{:S(2)}, u32[]{:S(2)}) collective-permute-start(bf16[4,384,384]{2,1,0:T(8,128)(2,1)S(1)} %collective-permute-done.13.w1_ref.refs_4_.refs_9_.refs_8_), channel_id=1, source_target_pairs={{0,1},{1,0},{2,3},{3,2},{4,5},{5,4},{6,7},{7,6},{8,9},{9,8},{10,11... | collective-permute-start | bytes 3538952 | tf_op jit(solution)/shard_map/ppermute | solution.py:359
  124.6 22.0 %collective-permute-start.23 = (bf16[4,384,384]{2,1,0:T(8,128)(2,1)}, bf16[4,384,384]{2,1,0:T(8,128)(2,1)}, u32[]{:S(2)}, u32[]{:S(2)}) collective-permute-start(bf16[4,384,384]{2,1,0:T(8,128)(2,1)} %pad_maximum_fusion.3.w0_ref.refs_4_), channel_id=1, source_target_pairs={{0,4},{1,3},{2,6},{3,1},{4,0},{5,7},{6,2},{7,5},{8,12},{9,11},{10,... | collective-permute-start | bytes 3538952 | tf_op jit(solution)/shard_map/ppermute | solution.py:225
  125.8 20.8 %collective-permute-start.27 = (bf16[4,384,384]{2,1,0:T(8,128)(2,1)}, bf16[4,384,384]{2,1,0:T(8,128)(2,1)}, u32[]{:S(2)}, u32[]{:S(2)}) collective-permute-start(bf16[4,384,384]{2,1,0:T(8,128)(2,1)} %pad_maximum_fusion.3.w0_ref.refs_4_), channel_id=1, source_target_pairs={{0,1},{1,0},{2,3},{3,2},{4,5},{5,4},{6,7},{7,6},{8,9},{9,8},{10,11... | collective-permute-start | bytes 3538952 | tf_op jit(solution)/shard_map/ppermute | solution.py:359
  126.1 20.5 %collective-permute-start.24 = (bf16[4,48,384]{2,1,0:T(8,128)(2,1)}, bf16[4,48,384]{2,1,0:T(8,128)(2,1)}, u32[]{:S(2)}, u32[]{:S(2)}) collective-permute-start(bf16[4,48,384]{2,1,0:T(8,128)(2,1)} %add_convert_fusion.20), channel_id=1, source_target_pairs={{0,8},{1,9},{2,10},{3,11},{4,12},{5,13},{6,14},{7,15},{8,16},{9,17... | collective-permute-start | bytes 442376 | tf_op jit(solution)/shard_map/ppermute | solution.py:225
  167.3 18.6 %collective-permute-start.30 = (bf16[4,384,384]{2,1,0:T(8,128)(2,1)}, bf16[4,384,384]{2,1,0:T(8,128)(2,1)}, u32[]{:S(2)}, u32[]{:S(2)}) collective-permute-start(bf16[4,384,384]{2,1,0:T(8,128)(2,1)} %pad_maximum_fusion.4.w0_ref.refs_0_), channel_id=1, source_target_pairs={{0,4},{1,3},{2,6},{3,1},{4,0},{5,7},{6,2},{7,5},{8,12},{9,11},{10,... | collective-permute-start | bytes 3538952 | tf_op jit(solution)/shard_map/ppermute | solution.py:225
  167.3 18.6 %collective-permute-start.31 = (bf16[4,384,384]{2,1,0:T(8,128)(2,1)}, bf16[4,384,384]{2,1,0:T(8,128)(2,1)}, u32[]{:S(2)}, u32[]{:S(2)}) collective-permute-start(bf16[4,384,384]{2,1,0:T(8,128)(2,1)} %pad_maximum_fusion.4.w0_ref.refs_0_), channel_id=1, source_target_pairs={{0,1},{1,0},{2,3},{3,2},{4,5},{5,4},{6,7},{7,6},{8,9},{9,8},{10,11... | collective-permute-start | bytes 3538952 | tf_op jit(solution)/shard_map/ppermute | solution.py:359
  219.8 26.5 %collective-permute-start.35 = (bf16[1024,768]{1,0:T(8,128)(2,1)}, bf16[1024,768]{1,0:T(8,128)(2,1)}, u32[]{:S(2)}, u32[]{:S(2)}) collective-permute-start(bf16[1024,768]{1,0:T(8,128)(2,1)} %get-tuple-element.478), channel_id=1, source_target_pairs={{0,1},{1,0},{2,3},{3,2},{4,5},{5,4},{6,7},{7,6},{8,9},{9,8},{10,11... | collective-permute-start | bytes 4718600 | tf_op jit(solution)/shard_map/ppermute | solution.py:359
  220.0 26.2 %collective-permute-start.34 = (bf16[4,384,384]{2,1,0:T(8,128)(2,1)}, bf16[4,384,384]{2,1,0:T(8,128)(2,1)}, u32[]{:S(2)}, u32[]{:S(2)}) collective-permute-start(bf16[4,384,384]{2,1,0:T(8,128)(2,1)} %get-tuple-element.387), channel_id=1, source_target_pairs={{0,4},{1,3},{2,6},{3,1},{4,0},{5,7},{6,2},{7,5},{8,12},{9,11},{10,... | collective-permute-start | bytes 3538952 | tf_op jit(solution)/shard_map/ppermute | solution.py:225
  265.9 20.6 %collective-permute-start.40 = (bf16[5,768,384]{2,1,0:T(8,128)(2,1)}, bf16[5,768,384]{2,1,0:T(8,128)(2,1)}, u32[]{:S(2)}, u32[]{:S(2)}) collective-permute-start(bf16[5,768,384]{2,1,0:T(8,128)(2,1)} %get-tuple-element.412), channel_id=1, source_target_pairs={{0,1},{1,0},{2,3},{3,2},{4,5},{5,4},{6,7},{7,6},{8,9},{9,8},{10,11... | collective-permute-start | bytes 8847368 | tf_op jit(solution)/shard_map/ppermute | solution.py:359
  265.9 20.5 %collective-permute-start.37 = (bf16[4,48,384]{2,1,0:T(8,128)(2,1)}, bf16[4,48,384]{2,1,0:T(8,128)(2,1)}, u32[]{:S(2)}, u32[]{:S(2)}) collective-permute-start(bf16[4,48,384]{2,1,0:T(8,128)(2,1)} %get-tuple-element.409), channel_id=1, source_target_pairs={{0,8},{1,9},{2,10},{3,11},{4,12},{5,13},{6,14},{7,15},{8,16},{9,17... | collective-permute-start | bytes 442376 | tf_op jit(solution)/shard_map/ppermute | solution.py:225
  266.3 20.2 %collective-permute-start.38 = (bf16[4,48,384]{2,1,0:T(8,128)(2,1)}, bf16[4,48,384]{2,1,0:T(8,128)(2,1)}, u32[]{:S(2)}, u32[]{:S(2)}) collective-permute-start(bf16[4,48,384]{2,1,0:T(8,128)(2,1)} %get-tuple-element.410), channel_id=1, source_target_pairs={{0,16},{1,17},{2,18},{3,19},{4,20},{5,21},{6,22},{7,23},{8,24},{9,... | collective-permute-start | bytes 442376 | tf_op jit(solution)/shard_map/ppermute | solution.py:225
  267.1 19.3 %collective-permute-start.39 = (bf16[4,48,384]{2,1,0:T(8,128)(2,1)}, bf16[4,48,384]{2,1,0:T(8,128)(2,1)}, u32[]{:S(2)}, u32[]{:S(2)}) collective-permute-start(bf16[4,48,384]{2,1,0:T(8,128)(2,1)} %get-tuple-element.411), channel_id=1, source_target_pairs={{0,24},{1,25},{2,26},{3,27},{4,28},{5,29},{6,30},{7,31},{8,0},{9,1... | collective-permute-start | bytes 442376 | tf_op jit(solution)/shard_map/ppermute | solution.py:225
  293.5 22.1 %collective-permute-start.44 = (bf16[5,384,384]{2,1,0:T(8,128)(2,1)}, bf16[5,384,384]{2,1,0:T(8,128)(2,1)}, u32[]{:S(2)}, u32[]{:S(2)}) collective-permute-start(bf16[5,384,384]{2,1,0:T(8,128)(2,1)} %get-tuple-element.431), channel_id=1, source_target_pairs={{0,4},{1,3},{2,6},{3,1},{4,0},{5,7},{6,2},{7,5},{8,12},{9,11},{10,... | collective-permute-start | bytes 4423688 | tf_op jit(solution)/shard_map/ppermute | solution.py:225
  294.0 21.6 %collective-permute-start.41 = (bf16[4,48,384]{2,1,0:T(8,128)(2,1)}, bf16[4,48,384]{2,1,0:T(8,128)(2,1)}, u32[]{:S(2)}, u32[]{:S(2)}) collective-permute-start(bf16[4,48,384]{2,1,0:T(8,128)(2,1)} %add_convert_fusion.15), channel_id=1, source_target_pairs={{0,8},{1,9},{2,10},{3,11},{4,12},{5,13},{6,14},{7,15},{8,16},{9,17... | collective-permute-start | bytes 442376 | tf_op jit(solution)/shard_map/ppermute | solution.py:225
  294.5 21.1 %collective-permute-start.42 = (bf16[4,48,384]{2,1,0:T(8,128)(2,1)}, bf16[4,48,384]{2,1,0:T(8,128)(2,1)}, u32[]{:S(2)}, u32[]{:S(2)}) collective-permute-start(bf16[4,48,384]{2,1,0:T(8,128)(2,1)} %add_convert_fusion.15), channel_id=1, source_target_pairs={{0,16},{1,17},{2,18},{3,19},{4,20},{5,21},{6,22},{7,23},{8,24},{9,... | collective-permute-start | bytes 442376 | tf_op jit(solution)/shard_map/ppermute | solution.py:225
  296.0 19.6 %collective-permute-start.43 = (bf16[4,48,384]{2,1,0:T(8,128)(2,1)}, bf16[4,48,384]{2,1,0:T(8,128)(2,1)}, u32[]{:S(2)}, u32[]{:S(2)}) collective-permute-start(bf16[4,48,384]{2,1,0:T(8,128)(2,1)} %add_convert_fusion.15), channel_id=1, source_target_pairs={{0,24},{1,25},{2,26},{3,27},{4,28},{5,29},{6,30},{7,31},{8,0},{9,1... | collective-permute-start | bytes 442376 | tf_op jit(solution)/shard_map/ppermute | solution.py:225
  365.0 27.7 %collective-permute-start.61 = (bf16[1024,768]{1,0:T(8,128)(2,1)}, bf16[1024,768]{1,0:T(8,128)(2,1)S(1)}, u32[]{:S(2)}, u32[]{:S(2)}) collective-permute-start(bf16[1024,768]{1,0:T(8,128)(2,1)} %get-tuple-element.493), channel_id=1, source_target_pairs={{0,1},{1,0},{2,3},{3,2},{4,5},{5,4},{6,7},{7,6},{8,9},{9,8},{10,11... | collective-permute-start | bytes 4718600 | tf_op jit(solution)/shard_map/ppermute | solution.py:359
  370.7 21.2 %collective-permute-start.54 = (bf16[3,192,384]{2,1,0:T(8,128)(2,1)S(1)}, bf16[3,192,384]{2,1,0:T(8,128)(2,1)S(1)}, u32[]{:S(2)}, u32[]{:S(2)}) collective-permute-start(bf16[3,192,384]{2,1,0:T(8,128)(2,1)S(1)} %get-tuple-element.470), channel_id=1, source_target_pairs={{0,2},{1,3},{2,0},{3,1},{4,6},{5,7},{6,4},{7,5},{8,10},{9,11},{10,... | collective-permute-start | bytes 1327112 | tf_op jit(solution)/shard_map/ppermute | solution.py:225
  371.5 21.2 %collective-permute-start.55 = (bf16[3,192,384]{2,1,0:T(8,128)(2,1)S(1)}, bf16[3,192,384]{2,1,0:T(8,128)(2,1)S(1)}, u32[]{:S(2)}, u32[]{:S(2)}) collective-permute-start(bf16[3,192,384]{2,1,0:T(8,128)(2,1)S(1)} %get-tuple-element.471), channel_id=1, source_target_pairs={{0,4},{1,5},{2,6},{3,7},{4,0},{5,1},{6,2},{7,3},{8,12},{9,13},{10,... | collective-permute-start | bytes 1327112 | tf_op jit(solution)/shard_map/ppermute | solution.py:225
  373.1 19.6 %collective-permute-start.56 = (bf16[3,192,384]{2,1,0:T(8,128)(2,1)S(1)}, bf16[3,192,384]{2,1,0:T(8,128)(2,1)S(1)}, u32[]{:S(2)}, u32[]{:S(2)}) collective-permute-start(bf16[3,192,384]{2,1,0:T(8,128)(2,1)S(1)} %get-tuple-element.472), channel_id=1, source_target_pairs={{0,6},{1,7},{2,4},{3,5},{4,2},{5,3},{6,0},{7,1},{8,14},{9,15},{10,... | collective-permute-start | bytes 1327112 | tf_op jit(solution)/shard_map/ppermute | solution.py:225
  407.8 23.2 %collective-permute-start.70 = (bf16[5,384,384]{2,1,0:T(8,128)(2,1)S(1)}, bf16[5,384,384]{2,1,0:T(8,128)(2,1)S(1)}, u32[]{:S(2)}, u32[]{:S(2)}) collective-permute-start(bf16[5,384,384]{2,1,0:T(8,128)(2,1)S(1)} %pad_maximum_fusion.1.refs_0_), channel_id=1, source_target_pairs={{0,4},{1,3},{2,6},{3,1},{4,0},{5,7},{6,2},{7,5},{8,12},{9,11},{10,... | collective-permute-start | bytes 4423688 | tf_op jit(solution)/shard_map/ppermute | solution.py:225
  432.8 20.7 %collective-permute-start.74 = (bf16[3,192,384]{2,1,0:T(8,128)(2,1)S(1)}, bf16[3,192,384]{2,1,0:T(8,128)(2,1)S(1)}, u32[]{:S(2)}, u32[]{:S(2)}) collective-permute-start(bf16[3,192,384]{2,1,0:T(8,128)(2,1)S(1)} %pad_maximum_fusion.11.refs_6_), channel_id=1, source_target_pairs={{0,6},{1,7},{2,4},{3,5},{4,2},{5,3},{6,0},{7,1},{8,14},{9,15},{10,... | collective-permute-start | bytes 1327112 | tf_op jit(solution)/shard_map/ppermute | solution.py:225
  (89 other events, 988.9 us)

commit v3 on v2

--- a/solution.py
+++ b/solution.py
@@ -43,6 +43,11 @@
     mean_grad = jnp.mean(grad_scaled, axis=-1, keepdims=True)
     mean_both = jnp.mean(grad_scaled * normal, axis=-1, keepdims=True)
     return inverse * (grad_scaled - mean_grad - normal * mean_both)
+
+
+def fold_rows(array_in):
+    rows, cols = array_in.shape
+    return jnp.sum(array_in.reshape(rows // 8, 8, cols), axis=0)
 
 
 def row_sum(array_in):
@@ -229,33 +234,27 @@
     return lax.dynamic_slice_in_dim(array_in, start, size, 1)
 
 
-def first_split(info, mine, other):
-    half = mine.shape[1] // 2
-    return [
-        total(cut(mine, at * half, half), cut(other, at * half, half))
-        for at in (1 - info[0], info[0])
-    ]
-
-
-def second_split(info, kept, got):
-    half = kept.shape[1] // 2
+def first_split(info, terms):
+    half = terms[0].shape[1] // 2
+    return total(*[cut(term, (1 - info[0]) * half, half) for term in terms])
+
+
+def second_split(info, terms, got):
+    half = got.shape[1] // 2
     start = (1 - info[1]) * half
-    return total(cut(kept, start, half), cut(got, start, half))
-
-
-def third_split(info, kept, one, two):
+    kept = [cut(term, info[0] * got.shape[1] + start, half) for term in terms]
+    return total(*kept, cut(got, start, half))
+
+
+def third_split(info, terms, one, two):
     half = two.shape[1]
     size = half // PLANES
     pieces = []
     for ahead in range(PLANES):
         start = (info[2] + ahead) % PLANES * size
-        pieces.append(
-            total(
-                cut(kept, info[1] * half + start, size),
-                cut(one, info[1] * half + start, size),
-                cut(two, start, size),
-            )
-        )
+        first = info[1] * half + start
+        kept = [cut(term, info[0] * one.shape[1] + first, size) for term in terms]
+        pieces.append(total(*kept, cut(one, first, size), cut(two, start, size)))
     return pieces
 
 
@@ -272,11 +271,10 @@
     )
 
 
-def exchange(going, kept, orient, info):
-    (one,) = yield [(going, swap_pairs(orient, 1))]
-    outgoing = second_split(info, kept, one)
-    (two,) = yield [(outgoing, swap_pairs(orient, 2))]
-    own, *pieces = third_split(info, kept, one, two)
+def exchange(terms, orient, info):
+    (one,) = yield [(first_split(info, terms), swap_pairs(orient, 1))]
+    (two,) = yield [(second_split(info, terms, one), swap_pairs(orient, 2))]
+    own, *pieces = third_split(info, terms, one, two)
     return (yield from spreading([own] + pieces, orient, info))
 
 
@@ -291,23 +289,19 @@
     return level, there
 
 
-def quarters(info, mine, other):
-    size = mine.shape[1] // 4
-    at = info[0]
-    return [
-        total(cut(mine, (at ^ away) * size, size), cut(other, (at ^ away) * size, size))
-        for away in range(4)
+def plane_exchange(terms, info):
+    quarter = terms[0].shape[1] // 4
+    size = quarter // PLANES
+    going = [
+        total(*[cut(term, (info[0] ^ away) * quarter, quarter) for term in terms])
+        for away in (1, 2, 3)
     ]
-
-
-def plane_exchange(pieces, info):
-    own, *going = pieces
     got = yield [(piece, flip_pairs(away)) for away, piece in zip((1, 2, 3), going)]
-    size = own.shape[1] // PLANES
     parts = []
     for ahead in range(PLANES):
         start = (info[2] + ahead) % PLANES * size
-        parts.append(total(*[cut(piece, start, size) for piece in [own] + got]))
+        kept = [cut(term, info[0] * quarter + start, size) for term in terms]
+        parts.append(total(*kept, *[cut(piece, start, size) for piece in got]))
     arrived = yield [(parts[step], plane_pairs(step)) for step in range(1, PLANES)]
     owned = total(parts[0], *arrived)
     others = yield [(owned, plane_pairs(step)) for step in range(1, PLANES)]
@@ -512,8 +506,7 @@
         slope_ref[:, spot] = (phi_sum + upper * density).astype(BF)
 
 
-TILE = 512
-ROWS, COLUMNS, NORM_ROWS = 256, 256, 64
+ROWS, COLUMNS, NORM_ROWS = 256, 256, 128
 UP_TILE = 256
 
 
@@ -544,33 +537,54 @@
     )(info, first, rows, bias, *weights)
 
 
-def down_kernel(
-    info_ref, h_ref, act_ref, cot_ref, rows_ref, w0_ref, w1_ref, w2_ref, w3_ref,
-    out_ref, dz_ref, gt_ref, dyt_ref, sum_ref, w_ref, branch_ref, low_ref, sem_ref,
-):
+PARTS = 4
+
+
+def wait_pairs(copies):
+    for pair in copies:
+        for copy in pair:
+            copy.wait()
+
+
+def down_kernel(info_ref, h_in_ref, act_ref, cot_in_ref, rows_ref, *refs):
+    parts, outs, gt_ref, sum_ref = refs[:4], refs[4:7], refs[7], refs[8]
+    w_ref, h_ref, cot_ref, branch_ref = refs[9:13]
+    out_ref, dz_ref, dyt_ref, low_ref, sem_ref, own_sem_ref = refs[13:]
     step = pl.program_id(0)
-    width = h_ref.shape[1]
-    tiles = act_ref.shape[0] // TILE
-
-    parts = (w0_ref, w1_ref, w2_ref, w3_ref)
+    tok, width = h_ref.shape
     copies = load_blocks(info_ref, parts, HALVED, w_ref, sem_ref)
+    start = pl.multiple_of(info_ref[1] * tok, tok)
+    h_copy = pltpu.make_async_copy(h_in_ref, h_ref, own_sem_ref.at[0])
+    cot_copy = pltpu.make_async_copy(
+        cot_in_ref.at[pl.ds(start, tok)], cot_ref, own_sem_ref.at[1]
+    )
+    out_copies = [
+        pltpu.make_async_copy(source, target, own_sem_ref.at[2 + at])
+        for at, (source, target) in enumerate(zip((out_ref, dz_ref, dyt_ref), outs))
+    ]
     start_first(copies)
 
     @pl.when(step == 0)
     def _():
+        h_copy.start()
+        cot_copy.start()
         sum_ref[...] = jnp.zeros_like(sum_ref)
 
-    first_time(copies)
-
-    @pl.when(step < tiles)
+    for part in range(PARTS):
+        @pl.when(step == part)
+        def _():
+            wait_pairs(copies[2 * part : 2 * part + 2])
+            lanes = slice(part * width, (part + 1) * width)
+            branch = dot_nt(act_ref[...], w_ref[:, lanes])
+            branch_ref[...] = branch if part == 0 else branch_ref[...] + branch
+
+    @pl.when(step == PARTS - 1)
     def _():
-        base = pl.multiple_of(step * TILE, TILE)
-        for row in range(0, TILE, ROWS):
-            spot = slice(row, row + ROWS)
-            branch_ref[spot, :] = dot_nt(act_ref[pl.ds(base + row, ROWS), :], w_ref[...])
+        h_copy.wait()
+        cot_copy.wait()
         gains = rows_ref[6:7]
         sums = [0.0, 0.0, 0.0]
-        for row in range(0, TILE, NORM_ROWS):
+        for row in range(0, tok, NORM_ROWS):
             spot = slice(row, row + NORM_ROWS)
             normal, inverse = normalized(h_ref[spot, :] + branch_ref[spot, :] + rows_ref[5:6])
             out_ref[spot, :] = (normal * gains + rows_ref[7:8]).astype(BF)
@@ -579,16 +593,21 @@
             dz_ref[spot, :] = grad
             low_ref[spot, :] = grad.astype(BF)
             for at, value in enumerate((grad, cot * normal, cot)):
-                sums[at] = sums[at] + row_sum(value)
-        dyt_ref[:, pl.ds(base, TILE)] = low_ref[...].T
+                sums[at] = sums[at] + fold_rows(value)
+        dyt_ref[...] = low_ref[...].T
         for at in range(3):
-            sum_ref[at : at + 1] += sums[at]
-
-    for part in range(2):
-        @pl.when(step == tiles + part)
-        def _():
-            grad = dot(dyt_ref[...], act_ref[:, (part + 2) * width : (part + 3) * width])
-            put_blocks(gt_ref, grad)
+            sum_ref[at : at + 1] += row_sum(sums[at])
+        for copy in out_copies:
+            copy.start()
+
+    @pl.when(step >= PARTS)
+    def _():
+        put_blocks(gt_ref, dot(dyt_ref[...], act_ref[...]))
+
+    @pl.when(step == PARTS + 1)
+    def _():
+        for copy in out_copies:
+            copy.wait()
 
 
 def put_blocks(ref, grad):
@@ -599,41 +618,42 @@
 
 def feed_down(info, hidden, act, cot, rows, weights):
     tok, width = hidden.shape
-    tiles = tok // TILE
-    last = tiles - 1
-    row_tile = pl.BlockSpec((TILE, width), lambda i, *_: (jnp.minimum(i, last), 0))
-    grads = struct((4, width, width // 2), BF)
+    wide = (tok, width)
     return call(
         down_kernel,
-        (tiles + 2,),
-        [
-            row_tile,
-            pl.BlockSpec((tok, FF), lambda i, *_: (0, 0)),
-            pl.BlockSpec(
-                (TILE, width), lambda i, info: (info[1] * tiles + jnp.minimum(i, last), 0)
-            ),
+        (PARTS + 2,),
+        [
+            ANY,
+            pl.BlockSpec(wide, lambda i, *_: (0, jnp.where(i < PARTS, i, i - 2))),
+            ANY,
             pl.BlockSpec((8, width), lambda i, *_: (0, 0)),
         ]
         + [ANY] * 4,
         [
-            row_tile,
-            row_tile,
-            pl.BlockSpec((2, width, width // 2), lambda i, *_: (jnp.clip(i - tiles, 0, 1), 0, 0)),
-            pl.BlockSpec((width, tok), lambda i, *_: (0, 0)),
+            ANY,
+            ANY,
+            ANY,
+            pl.BlockSpec((2, width, width // 2), lambda i, *_: (jnp.clip(i - PARTS, 0, 1), 0, 0)),
             pl.BlockSpec((8, width), lambda i, *_: (0, 0)),
         ],
         [
-            struct((tok, width), BF),
-            struct((tok, width), F32),
-            grads,
+            struct(wide, BF),
+            struct(wide, F32),
             struct((width, tok), BF),
+            struct((4, width, width // 2), BF),
             struct((8, width), F32),
         ],
         [
             pltpu.VMEM((width, FF), BF),
-            pltpu.VMEM((TILE, width), F32),
-            pltpu.VMEM((TILE, width), BF),
+            pltpu.VMEM(wide, F32),
+            pltpu.VMEM(wide, BF),
+            pltpu.VMEM(wide, F32),
+            pltpu.VMEM(wide, BF),
+            pltpu.VMEM(wide, F32),
+            pltpu.VMEM((width, tok), BF),
+            pltpu.VMEM(wide, BF),
             pltpu.SemaphoreType.DMA((16,)),
+            pltpu.SemaphoreType.DMA((5,)),
         ],
         1,
         3 * tok * width * FF,
@@ -641,73 +661,100 @@
     )(info, hidden, act, cot, rows, *weights)
 
 
-def back_kernel(info_ref, z_ref, dz2_ref, slope_ref, rows_ref, *refs):
+def back_kernel(info_ref, z_in_ref, dz2_ref, slope_ref, rows_ref, *refs):
     down, upper, other = refs[:4], refs[4:8], refs[8:12]
-    dz1_ref, dctx_ref, dtt_ref, da_ref, sum_ref = refs[12:17]
-    wd_ref, wu_ref, wo_ref, hidden_ref, low_ref, dsem_ref, usem_ref, osem_ref = refs[17:]
-    width = z_ref.shape[1]
+    outs, da_ref, sum_ref = refs[12:15], refs[15], refs[16]
+    wd_ref, wu_ref, wo_ref, z_ref, hidden_ref, low_ref, held_ref = refs[17:24]
+    dz1_ref, dctx_ref, dtt_ref, dsem_ref, usem_ref, osem_ref, own_sem_ref = refs[24:]
+    step = pl.program_id(0)
+    tok, width = z_ref.shape
     downs = load_blocks(info_ref, down, HALVED, wd_ref, dsem_ref)
     ups = load_blocks(info_ref, upper, HALVED, wu_ref, usem_ref)
-    outs = load_blocks(info_ref, other, [(0, 3), (1, 3)], wo_ref, osem_ref)
+    others = load_blocks(info_ref, other, [(0, 3), (1, 3)], wo_ref, osem_ref)
+    z_copy = pltpu.make_async_copy(z_in_ref, z_ref, own_sem_ref.at[0])
     for at in range(0, 8, 2):
         start_first(downs[at : at + 2] + ups[at : at + 2])
-    start_first(outs)
-
-    @pl.when(pl.program_id(0) == 0)
+    start_first(others + [[z_copy]])
+
+    @pl.when(step == 0)
     def _():
         sum_ref[...] = jnp.zeros_like(sum_ref)
-
-    tile = z_ref.shape[0]
-    low_two = dz2_ref[...].astype(BF)
-    for part in range(FF // width):
-        first_time(downs[2 * part : 2 * part + 2])
-        place = 4 + (part ^ (2 * info_ref[1]))
-        for start in range(0, width, COLUMNS):
-            lanes = slice(part * width + start, part * width + start + COLUMNS)
-            grad_sum = 0.0
-            for row in range(0, tile, ROWS):
-                spot = slice(row, row + ROWS)
-                grad_act = dot(low_two[spot], wd_ref[:, lanes])
-                grad_up = (grad_act * slope_ref[spot, lanes].astype(F32)).astype(BF)
-                da_ref[spot, lanes] = grad_up
-                grad_sum = grad_sum + row_sum(grad_up.astype(F32))
-            sum_ref[pl.ds(place, 1), start : start + COLUMNS] += grad_sum
-    first_time(ups)
-    for row in range(0, tile, ROWS):
-        spot = slice(row, row + ROWS)
-        hidden_ref[spot, :] = dz2_ref[spot, :] + dot_nt(da_ref[spot, :], wu_ref[...])
-    gains = rows_ref[3:4]
-    sums = [0.0, 0.0, 0.0]
-    for row in range(0, tile, NORM_ROWS):
-        spot = slice(row, row + NORM_ROWS)
-        grad_hidden = hidden_ref[spot, :]
-        normal, inverse = normalized(z_ref[spot, :])
-        grad_one = norm_back(grad_hidden * gains, normal, inverse)
-        sums[0] = sums[0] + row_sum(grad_one)
-        sums[1] = sums[1] + row_sum(grad_hidden * normal)
-        sums[2] = sums[2] + row_sum(grad_hidden)
-        dz1_ref[spot, :] = grad_one
-        low_ref[spot, :] = grad_one.astype(BF)
-    for at in range(3):
-        sum_ref[at : at + 1] += sums[at]
-    dtt_ref[...] = low_ref[...].T
-    first_time(outs)
-    dctx_ref[...] = dot(low_ref[...], wo_ref[...]).astype(BF)
+        hidden_ref[...] = dz2_ref[...]
+        low_ref[...] = dz2_ref[...].astype(BF)
+
+    for part in range(PARTS + 1):
+        @pl.when(step == part)
+        def _():
+            if part < PARTS:
+                wait_pairs(downs[2 * part : 2 * part + 2])
+            if part > 0:
+                wait_pairs(ups[2 * part - 2 : 2 * part])
+            place = 4 + (part ^ (2 * info_ref[1]))
+            for column in range(0, width, COLUMNS):
+                spot = slice(column, column + COLUMNS)
+                lanes = slice(part * width + column, part * width + column + COLUMNS)
+                if part < PARTS:
+                    grad_act = dot(low_ref[...], wd_ref[:, lanes])
+                if part > 0:
+                    before = slice((part - 1) * width, part * width)
+                    hidden_ref[:, spot] += dot_nt(held_ref[(part - 1) % 2], wu_ref[spot, before])
+                if part < PARTS:
+                    grad_up = (grad_act * slope_ref[:, spot].astype(F32)).astype(BF)
+                    da_ref[:, spot] = grad_up
+                    held_ref[part % 2, :, spot] = grad_up
+                    sum_ref[pl.ds(place, 1), spot] = row_sum(fold_rows(grad_up.astype(F32)))
+
+    @pl.when(step == PARTS)
+    def _():
+        z_copy.wait()
+        gains = rows_ref[3:4]
+        sums = [0.0, 0.0, 0.0]
+        out_copies = []
+        for half in range(2):
+            rows = slice(half * (tok // 2), (half + 1) * (tok // 2))
+            for row in range(rows.start, rows.stop, NORM_ROWS):
+                spot = slice(row, row + NORM_ROWS)
+                grad_hidden = hidden_ref[spot, :]
+                normal, inverse = normalized(z_ref[spot, :])
+                grad_one = norm_back(grad_hidden * gains, normal, inverse)
+                dz1_ref[spot, :] = grad_one
+                low_ref[spot, :] = grad_one.astype(BF)
+                for at, value in enumerate((grad_one, grad_hidden * normal, grad_hidden)):
+                    sums[at] = sums[at] + fold_rows(value)
+            if half == 0:
+                wait_pairs(others)
+            dctx_ref[rows, :] = dot(low_ref[rows, :], wo_ref[...]).astype(BF)
+            dtt_ref[:, rows] = low_ref[rows, :].T
+            spot = pl.ds(rows.start, tok // 2)
+            for at, (source, target) in enumerate(zip((dz1_ref, dctx_ref, dtt_ref), outs)):
+                source, target = (
+                    (source.at[:, spot], target.at[:, spot])
+                    if at == 2
+                    else (source.at[spot], target.at[spot])
+                )
+                out_copies.append(
+                    pltpu.make_async_copy(source, target, own_sem_ref.at[1 + 3 * half + at])
+                )
+                out_copies[-1].start()
+        for at in range(3):
+            sum_ref[at : at + 1] = row_sum(sums[at])
+        for copy in out_copies:
+            copy.wait()
 
 
 def feed_back(info, first, dz2, slope, rows, down, upper, other):
     tok, width = first.shape
-    row_tile = pl.BlockSpec((TILE, width), lambda i, *_: (i, 0))
-    wide_tile = pl.BlockSpec((TILE, FF), lambda i, *_: (i, 0))
+    wide = (tok, width)
     fixed = pl.BlockSpec((8, width), lambda i, *_: (0, 0))
+    part = pl.BlockSpec(wide, lambda i, *_: (0, jnp.minimum(i, PARTS - 1)))
     return call(
         back_kernel,
-        (tok // TILE,),
-        [row_tile, row_tile, wide_tile, fixed] + [ANY] * 12,
-        [row_tile, row_tile, pl.BlockSpec((width, TILE), lambda i, *_: (0, i)), wide_tile, fixed],
-        [
-            struct((tok, width), F32),
-            struct((tok, width), BF),
+        (PARTS + 1,),
+        [ANY, pl.BlockSpec(wide, lambda i, *_: (0, 0)), part, fixed] + [ANY] * 12,
+        [ANY, ANY, ANY, part, fixed],
+        [
+            struct(wide, F32),
+            struct(wide, BF),
             struct((width, tok), BF),
             struct((tok, FF), BF),
             struct((8, width), F32),
@@ -716,11 +763,17 @@
             pltpu.VMEM((width, FF), BF),
             pltpu.VMEM((width, FF), BF),
             pltpu.VMEM((width, width), BF),
-            pltpu.VMEM((TILE, width), F32),
-            pltpu.VMEM((TILE, width), BF),
+            pltpu.VMEM(wide, F32),
+            pltpu.VMEM(wide, F32),
+            pltpu.VMEM(wide, BF),
+            pltpu.VMEM((2, *wide), BF),
+            pltpu.VMEM(wide, F32),
+            pltpu.VMEM(wide, BF),
+            pltpu.VMEM((width, tok), BF),
             pltpu.SemaphoreType.DMA((16,)),
             pltpu.SemaphoreType.DMA((16,)),
             pltpu.SemaphoreType.DMA((4,)),
+            pltpu.SemaphoreType.DMA((7,)),
         ],
         1,
         4 * tok * width * FF,
@@ -762,13 +815,6 @@
     )(left_t, right)
 
 
-def square_kernel(left_ref, right_ref, gm_ref, gt_ref):
-    grad = dot(left_ref[...], right_ref[...])
-    cols = gm_ref.shape[2]
-    gm_ref[0] = grad[:, :cols].astype(BF)
-    gt_ref[0] = grad[:, cols:].astype(BF)
-
-
 def share_kernel(left_ref, right_ref, out_ref):
     put_blocks(out_ref, dot(left_ref[...], right_ref[...]))
 
@@ -793,26 +839,60 @@
     )(left_t, right)[0]
 
 
-def square_grad(left_t, right, first=0, kept=None):
-    width, tok = left_t.shape
-    count = right.shape[1] // width
-    block = pl.BlockSpec((1, width, width // 2), lambda i: (first + i, 0, 0))
+def up_grad_kernel(ht_ref, dtt_ref, da_ref, ctx_ref, gm_ref, gt_ref, held_ref, sem_ref):
+    step = pl.program_id(0)
+    cols = held_ref.shape[3]
+
+    def copies(at):
+        targets = (
+            [(ref, PARTS) for ref in (gm_ref, gt_ref)]
+            if at == PARTS
+            else [((gm_ref, gt_ref)[at // 2], at % 2 * 2 + block) for block in range(2)]
+        )
+        return [
+            pltpu.make_async_copy(
+                held_ref.at[at % 2, block], ref.at[target], sem_ref.at[at % 2, block]
+            )
+            for block, (ref, target) in enumerate(targets)
+        ]
+
+    for at in range(PARTS + 1):
+        @pl.when(step == at)
+        def _():
+            left, right = (dtt_ref, ctx_ref) if at == PARTS else (ht_ref, da_ref)
+            grad = dot(left[...], right[...])
+            if at >= 2:
+                for copy in copies(at - 2):
+                    copy.wait()
+            for block in range(2):
+                held_ref[at % 2, block] = grad[:, block * cols : (block + 1) * cols].astype(BF)
+            for copy in copies(at):
+                copy.start()
+            if at == PARTS:
+                for copy in copies(at - 1) + copies(at):
+                    copy.wait()
+
+
+def up_grad(hidden_t, dt_t, grad_up, ctx):
+    width, tok = hidden_t.shape
+    cols = width // 2
+    whole = pl.BlockSpec((width, tok), lambda i: (0, 0))
     return call(
-        square_kernel,
-        (count,),
-        [
-            pl.BlockSpec((width, tok), lambda i: (0, 0)),
-            pl.BlockSpec((tok, width), lambda i: (0, i)),
+        up_grad_kernel,
+        (PARTS + 1,),
+        [
+            whole,
+            whole,
+            pl.BlockSpec((tok, width), lambda i: (0, jnp.minimum(i, PARTS - 1))),
+            pl.BlockSpec((tok, width), lambda i: (0, 0)),
         ],
-        [block, block],
-        [struct((first + count, width, width // 2), BF)] * 2,
-        [],
+        [ANY, ANY],
+        [struct((PARTS + 1, width, cols), BF)] * 2,
+        [pltpu.VMEM((2, 2, width, cols), BF), pltpu.SemaphoreType.DMA((2, 2))],
         0,
-        2 * tok * width * width * count,
-        4 * 2**20 * count,
-        0,
-        kept,
-    )(left_t, right, *(kept or ()))
+        2 * tok * width * (FF + width),
+        25 * 2**20,
+    )(hidden_t, dt_t, grad_up, ctx)
 
 
 def attend_pairs_back(first, short, q_ref, k_ref, v_ref, dctx_ref, lse_ref, dqkv_ref):
@@ -1145,9 +1225,8 @@
         blocks = jnp.where(own[..., None, None], blocks, 0.0).astype(BF)
         return lax.psum(blocks.reshape(4, width, cols), "batch")
 
-    def grads_chain(mine, other):
-        going, kept = first_split(places[0], mine, other)
-        return Chain(exchange(going, kept, 0, places[0]))
+    def grads_chain(terms, orient):
+        return Chain(exchange(terms, orient, places[orient]))
 
     def shared(array_in):
         half = array_in.shape[1] // 2
@@ -1215,7 +1294,8 @@
         jnp.where(kind[:, None] == jnp.arange(4)[None, :], learn_rates[None, :4], 0.0), axis=1
     )
     quarter_rows, half_rows = row_blocks // 4, row_blocks // 2
-    first_quarter, first_half = (corner[0], places[0][0]) if fast else (0, 0)
+    first_quarter = corner[0] if fast else 0
+    first_half = jnp.where(chunk_at == 1, places[1][0], places[0][0]) if fast else 0
     array_at = jnp.where(
         chunk_at == 0,
         (row_at // quarter_rows) ^ first_quarter,
@@ -1234,9 +1314,7 @@
     firsts = [places[0][0], places[1][0]] if fast else [0, 0]
     info = jnp.stack([phase_of[0], core, *firsts]).astype(jnp.int32)
     vectors = vector_state[0]
-    rows = jnp.concatenate(
-        [swapped(vectors[0:2]), vectors[2:5], vectors[9:12]], axis=0
-    )
+    rows = jnp.concatenate([swapped(vectors[0:2]), vectors[2:5], vectors[9:12]], axis=0)
     upper = vectors[5:9].reshape(2, FF // 2)
     turned = jnp.concatenate([upper[1:], upper[:1]], axis=0)
     bias_up = jnp.where(core == 0, upper, turned).reshape(4, width)
@@ -1250,7 +1328,9 @@
         io = weights_chain(spreads(sources, (0,))[0])
         _, (up, down) = phase([io], work=lambda _: spreads(sources, (1, 2)))
         up, down = weights_chain(up), weights_chain(down)
-        phase([io])
+        _, (info, rows, bias_up, table, scales) = phase(
+            [io], work=lambda _: (info, rows, bias_up, table, scales)
+        )
         phase([io, up])
         theirs_first, _ = phase([io, up], io.ready)
         theirs_last, _ = phase([up, down], io.result[1:])
@@ -1282,7 +1362,7 @@
         q, k, v, ctx, lse, first, x_t = stage
         act, slope, hidden_t, hidden = feed_up(info, first, rows, bias_up, weights_up)
 
-    out_half, dz2, down_theirs, grad_two_t, sums_two = feed_down(
+    out_half, dz2, grad_two_t, down_theirs, sums_two = feed_down(
         info, hidden, act, cotangent, rows, weights_down
     )
     heads = (q, k, v)
@@ -1299,20 +1379,18 @@
         (other,), (down_mine,) = phase(
             swaps=[down_theirs], work=lambda late: wide_grad(after(grad_two_t, late), act, (0,))
         )
-        down = grads_chain(down_mine, other)
+        down = grads_chain([down_mine, other], 0)
         (out_other,), (dz1, dctx, dt_t, grad_up, sums_one) = phase(
             [down], [out_half], lambda late: back(after(info, late))
         )
         _, (up_mine, up_theirs) = phase(
             [down],
-            work=lambda late: square_grad(
-                dt_t, ctx, 4, wide_grad(after(hidden_t, late), grad_up, (0, 1), 5)
-            ),
+            work=lambda late: up_grad(after(hidden_t, late), dt_t, grad_up, ctx),
         )
         (other,), (kept, sums_zero) = phase(
             [down], [up_theirs], lambda late: heads_back(0, after(info, late), dctx, dz1)
         )
-        up = grads_chain(up_mine, other)
+        up = grads_chain([up_mine, other], 1)
         _, (kept, sums_extra) = phase(
             [down, up],
             work=lambda late: heads_back(1, after(info, late), dctx, dz1, kept),
@@ -1325,7 +1403,7 @@
         (other,), io_mine = phase(
             [down, up, vec], [io_theirs], lambda late: share_grad(after(x_t, late), dqkv, 0)
         )
-        io = Chain(plane_exchange(quarters(corner, io_mine, other), corner))
+        io = Chain(plane_exchange([io_mine, other], corner))
         (grad_x_other,), out = phase(
             [io, up, vec], [grad_x], lambda late: both(after(out_half, late), out_other)
         )
@@ -1349,9 +1427,7 @@
             kept, sums_extra = heads_back(group, info, dctx, dz1, kept)
             sums_zero = sums_zero + sums_extra
         dqkv, grad_x = kept
-        up_mine, up_theirs = square_grad(
-            dt_t, ctx, 4, wide_grad(hidden_t, grad_up, (0, 1), 5)
-        )
+        up_mine, up_theirs = up_grad(hidden_t, dt_t, grad_up, ctx)
         (down_mine,) = wide_grad(grad_two_t, act, (0,))
         grads = []
         for mine, theirs, parts in (

time: 470 us -> 458 us (0.974)
  waiting for transfers between devices: 112 us -> 98.8 us
  Pallas kernels: 185 us -> 180 us
  local copies, waits for them, and re-layouts: 10.2 us -> 15.1 us
    pallas_call x2 -> x1, Pallas kernels: 15.8 us -> 5.96 us  [wide_grad(): call(product_kernel, (2 * len(halves),), [pl.BlockSpec((width, tok), lamb...]
    ppermute x61, waiting for transfers between devices: 79.5 us -> 72.6 us  [send(): return lax.ppermute(array_in, BOTH, pairs)]
  transfers between devices with their start and end apart: 75 -> 75, of which waited for: 21 -> 22; matrix products, arithmetic and copies ran while one was open for 5% -> 5% of each run, Pallas kernels for 33% -> 34%
where the time goes in v3:
time: 458 us; the launch traced here: 449 us
  Pallas kernels  180 us (39%)
  waiting for transfers between devices  98.8 us (22%)
  starting transfers between devices  93.8 us (20%)
  other arithmetic  54.9 us (12%)
  local copies, waits for them, and re-layouts  15.1 us (3%)
  between operations  6.65 us (1%)
    ppermute x61, starting transfers between devices, send(): return lax.ppermute(array_in, BOTH, pairs)  86.6 us
    ppermute x61, waiting for transfers between devices, send(): return lax.ppermute(array_in, BOTH, pairs)  72.6 us
    pallas_call x2, Pallas kernels, attend_back(): call(attend_back_kernel, (1,), [tile, tile, tile, tile, pl.BlockSpec((1,...  33.3 us
    pallas_call x2, Pallas kernels, forward(): call(forward_kernel, (1,), [pl.BlockSpec((LONG, width), lambda i, info: (...  28.8 us
    convert_element_type x14, other arithmetic, total(): return result.astype(BF)  24.5 us
    pallas_call x1, Pallas kernels, feed_back(): call(back_kernel, (PARTS + 1,), [ANY, pl.BlockSpec(wide, lambda i, *_: (0...  23.4 us
    pallas_call x1, Pallas kernels, feed_up(): call(up_kernel, (tok // UP_TILE,), [pl.BlockSpec((UP_TILE, width), lambda...  18.5 us
    pallas_call x1, Pallas kernels, feed_down(): call(down_kernel, (PARTS + 2,), [ANY, pl.BlockSpec(wide, lambda i, *_: (0...  17.7 us
  transfers between devices with their start and end apart: 75, of which 22 were waited for; matrix products, arithmetic and copies ran while one was open for 5% of the time, Pallas kernels for 34%

profile of v3, /device:TPU:0, one launch (start us, length us, event | category | flops | bytes accessed | tf_op | source)
XLA Modules:
  0.0 449.3 jit_solution(18105725009146188583)
XLA Ops:
  11.5 13.9 %collective-permute-done.refs_1_ = bf16[18,64,384]{2,1,0:T(8,128)(2,1)S(1)} collective-permute-done((bf16[18,64,384]{2,1,0:T(8,128)(2,1)S(1)}, bf16[18,64,384]{2,1,0:T(8,128)(2,1)S(1)}, u32[]{:S(2)}, u32[]{:S(2)}) %collective-permute-start) | collective-permute-done | bytes 884768 | tf_op jit(solution)/shard_map/ppermute | solution.py:1324
  28.8 9.6 %collective-permute-done.2.refs_3_ = bf16[18,64,384]{2,1,0:T(8,128)(2,1)S(1)} collective-permute-done((bf16[18,64,384]{2,1,0:T(8,128)(2,1)S(1)}, bf16[18,64,384]{2,1,0:T(8,128)(2,1)S(1)}, u32[]{:S(2)}, u32[]{:S(2)}) %collective-permute-start.2) | collective-permute-done | bytes 884768 | tf_op jit(solution)/shard_map/ppermute | solution.py:1326
  55.6 4.4 shard_map.188
  68.3 4.7 %collective-permute-done.7 = bf16[4,48,384]{2,1,0:T(8,128)(2,1)S(1)} collective-permute-done((bf16[4,48,384]{2,1,0:T(8,128)(2,1)S(1)}, bf16[4,48,384]{2,1,0:T(8,128)(2,1)S(1)}, u32[]{:S(2)}, u32[]{:S(2)}) %collective-permute-start.7) | collective-permute-done | bytes 147488 | tf_op jit(solution)/shard_map/ppermute | solution.py:230
  97.2 6.0 %collective-permute-done.15 = bf16[4,48,384]{2,1,0:T(8,128)(2,1)S(1)} collective-permute-done((bf16[4,48,384]{2,1,0:T(8,128)(2,1)S(1)}, bf16[4,48,384]{2,1,0:T(8,128)(2,1)S(1)}, u32[]{:S(2)}, u32[]{:S(2)}) %collective-permute-start.15) | collective-permute-done | bytes 147488 | tf_op jit(solution)/shard_map/ppermute | solution.py:230
  114.2 5.7 %collective-permute-done.20 = bf16[4,48,384]{2,1,0:T(8,128)(2,1)S(1)} collective-permute-done((bf16[4,48,384]{2,1,0:T(8,128)(2,1)S(1)}, bf16[4,48,384]{2,1,0:T(8,128)(2,1)S(1)}, u32[]{:S(2)}, u32[]{:S(2)}) %collective-permute-start.20) | collective-permute-done | bytes 147488 | tf_op jit(solution)/shard_map/ppermute | solution.py:230
  129.1 14.4 %shard_map.190 = (bf16[1024,768]{1,0:T(8,128)(2,1)}, bf16[1024,768]{1,0:T(8,128)(2,1)}, bf16[1024,768]{1,0:T(8,128)(2,1)}, bf16[1024,768]{1,0:T(8,128)(2,1)}, f3...) custom-call(s32[4]{0:T(128)} %pad_add_fusion.1.info_ref.refs_0_, bf16[2048,768]{1,0:T(8,128)(2,1)} %refs_1_.1, ...), custom_call_target="tpu_custom_call" | custom-call | flops 193273528320 | bytes 12582912 | tf_op jit(solution)/shard_map/pallas_call | solution.py:457
  146.5 14.3 %shard_map.191 = (bf16[1024,768]{1,0:T(8,128)(2,1)}, bf16[1024,768]{1,0:T(8,128)(2,1)}, bf16[1024,768]{1,0:T(8,128)(2,1)}, bf16[1024,768]{1,0:T(8,128)(2,1)}, f3...) custom-call(s32[4]{0:T(128)} %pad_add_fusion.1.info_ref.refs_0_, ...), custom_call_target="tpu_custom_call", output_to_operand_aliasing={{0}: (7, {}), {1}: (8, {}), {2}: (9, {}), {3}: (10, {}), {4... | custom-call | flops 193273528320 | bytes 12582912 | tf_op jit(solution)/shard_map/pallas_call | solution.py:457
  165.1 18.5 %shard_map.192 = (bf16[1024,3072]{1,0:T(8,128)(2,1)}, bf16[1024,3072]{1,0:T(8,128)(2,1)}, bf16[768,1024]{1,0:T(8,128)(2,1)}, f32[1024,768]{1,0:T(8,128)}) custom-call(s32[4]{0:T(128)} %pad_add_fusion.1.info_ref.refs_0_, f32[1024,768]{1,0:T(8,128)} %get-tuple-element.375.z_ref.z_in_ref, f32[8,768]{1,0:T(8,128)} %pad_maximum_fusion.17.rows_ref.refs_2_, ...), custom_call_target="tpu_custom_call" | custom-call | flops 144955146240 | bytes 20971520 | tf_op jit(solution)/shard_map/pallas_call | solution.py:516
  187.9 17.7 %shard_map.193 = (bf16[1024,768]{1,0:T(8,128)(2,1)}, f32[1024,768]{1,0:T(8,128)}, bf16[768,1024]{1,0:T(8,128)(2,1)}, bf16[4,768,384]{2,1,0:T(8,128)(2,1)}, f32[8,768]{1,0:T(8,128)}) custom-call(s32[4]{0:T(128)} %pad_add_fusion.1.info_ref.refs_0_, f32[1024,768]{1,0:T(8,128)} %get-tuple-element.383.h_in_ref, ...), custom_call_target="tpu_custom_call" | custom-call | flops 217432719360 | bytes 31457280 | tf_op jit(solution)/shard_map/pallas_call | solution.py:622
  206.1 6.0 %shard_map.194 = bf16[4,768,384]{2,1,0:T(8,128)(2,1)} custom-call(bf16[768,1024]{1,0:T(8,128)(2,1)} %get-tuple-element.389.left_ref, bf16[1024,3072]{1,0:T(8,128)(2,1)} %get-tuple-element.384.act_ref.right_ref), custom_call_target="tpu_custom_call" | custom-call | flops 72477573120 | bytes 10485760 | tf_op jit(solution)/shard_map/pallas_call | solution.py:802
  216.0 23.4 %shard_map.195 = (f32[1024,768]{1,0:T(8,128)}, bf16[1024,768]{1,0:T(8,128)(2,1)}, bf16[768,1024]{1,0:T(8,128)(2,1)}, bf16[1024,3072]{1,0:T(8,128)(2,1)}, f32[8,768]{1,0:T(8,128)}) custom-call(s32[4]{0:T(128)} %pad_add_fusion.1.info_ref.refs_0_, f32[1024,768]{1,0:T(8,128)} %get-tuple-element.375.z_ref.z_in_ref, f32[1024,768]{1,0:T(8,128)} %get-tuple-element.396.dz2_ref, ...), custom_call_target="tpu_custom_call" | custom-call | flops 289910292480 | bytes 31457280 | tf_op jit(solution)/shard_map/pallas_call | solution.py:750
  243.7 11.8 %shard_map.196 = (bf16[5,768,384]{2,1,0:T(8,128)(2,1)}, bf16[5,768,384]{2,1,0:T(8,128)(2,1)}) custom-call(bf16[768,1024]{1,0:T(8,128)(2,1)} %get-tuple-element.405.ht_ref, bf16[768,1024]{1,0:T(8,128)(2,1)} %get-tuple-element.406.dtt_ref, bf16[1024,3072]{1,0:T(8,128)(2,1)} %get-tuple-element.407.da_ref, bf16[1024,768]{1,0:T(8,128)(2,1)} %get-tuple-element.408.ctx_ref), custom_call_target="tpu_custom_call" | custom-call | flops 181193932800 | bytes 26214400 | tf_op jit(solution)/shard_map/pallas_call | solution.py:880
  261.9 16.7 %shard_map.197 = (bf16[1024,2304]{1,0:T(8,128)(2,1)}, bf16[1024,768]{1,0:T(8,128)(2,1)}, f32[8,768]{1,0:T(8,128)}) custom-call(s32[4]{0:T(128)} %pad_add_fusion.1.info_ref.refs_0_, bf16[1024,768]{1,0:T(8,128)(2,1)} %get-tuple-element.418.q_ref.refs_1_, bf16[1024,768]{1,0:T(8,128)(2,1)} %get-tuple-element.419.k_ref.refs_2_, ...), custom_call_target="tpu_custom_call" | custom-call | flops 175154135040 | bytes 15728640 | tf_op jit(solution)/shard_map/pallas_call | solution.py:989
  289.1 16.6 %shard_map.198 = (bf16[1024,2304]{1,0:T(8,128)(2,1)}, bf16[1024,768]{1,0:T(8,128)(2,1)}, f32[8,768]{1,0:T(8,128)}) custom-call(s32[4]{0:T(128)} %pad_add_fusion.1.info_ref.refs_0_, bf16[1024,768]{1,0:T(8,128)(2,1)} %get-tuple-element.418.q_ref.refs_1_, ...), custom_call_target="tpu_custom_call", output_to_operand_aliasing={{0}: (11, {}), {1}: (12, {})} | custom-call | flops 175154135040 | bytes 15728640 | tf_op jit(solution)/shard_map/pallas_call | solution.py:989
  312.7 5.5 %shard_map.199 = bf16[3,768,384]{2,1,0:T(8,128)(2,1)} custom-call(bf16[768,1024]{1,0:T(8,128)(2,1)} %get-tuple-element.466.left_ref, bf16[1024,2304]{1,0:T(8,128)(2,1)} %get-tuple-element.455.right_ref), custom_call_target="tpu_custom_call" | custom-call | flops 54358179840 | bytes 6291456 | tf_op jit(solution)/shard_map/pallas_call | solution.py:826
  318.2 7.7 %collective-permute-done.45 = bf16[4,192,384]{2,1,0:T(8,128)(2,1)S(1)} collective-permute-done((bf16[4,192,384]{2,1,0:T(8,128)(2,1)S(1)}, bf16[4,192,384]{2,1,0:T(8,128)(2,1)S(1)}, u32[]{:S(2)}, u32[]{:S(2)}) %collective-permute-start.45) | collective-permute-done | bytes 589856 | tf_op jit(solution)/shard_map/ppermute | solution.py:230
  337.8 5.5 %shard_map.200 = bf16[3,768,384]{2,1,0:T(8,128)(2,1)} custom-call(bf16[768,1024]{1,0:T(8,128)(2,1)} %get-tuple-element.466.left_ref, bf16[1024,2304]{1,0:T(8,128)(2,1)} %get-tuple-element.455.right_ref), custom_call_target="tpu_custom_call" | custom-call | flops 54358179840 | bytes 6291456 | tf_op jit(solution)/shard_map/pallas_call | solution.py:826
  343.4 6.9 %collective-permute-done.50 = bf16[5,48,384]{2,1,0:T(8,128)(2,1)S(1)} collective-permute-done((bf16[5,48,384]{2,1,0:T(8,128)(2,1)}, bf16[5,48,384]{2,1,0:T(8,128)(2,1)S(1)}, u32[]{:S(2)}, u32[]{:S(2)}) %collective-permute-start.50) | collective-permute-done | bytes 184352 | tf_op jit(solution)/shard_map/ppermute | solution.py:230
  366.7 7.6 %collective-permute-done.58 = bf16[5,48,384]{2,1,0:T(8,128)(2,1)S(1)} collective-permute-done((bf16[5,48,384]{2,1,0:T(8,128)(2,1)S(1)}, bf16[5,48,384]{2,1,0:T(8,128)(2,1)S(1)}, u32[]{:S(2)}, u32[]{:S(2)}) %collective-permute-start.58) | collective-permute-done | bytes 184352 | tf_op jit(solution)/shard_map/ppermute | solution.py:230
  408.2 6.3 %collective-permute-done.71 = f32[24,768]{1,0:T(8,128)S(1)} collective-permute-done((f32[24,768]{1,0:T(8,128)S(1)}, f32[24,768]{1,0:T(8,128)S(1)}, u32[]{:S(2)}, u32[]{:S(2)}) %collective-permute-start.71) | collective-permute-done | bytes 73760 | tf_op jit(solution)/shard_map/ppermute | solution.py:230
  422.4 9.4 %shard_map.201 = (f32[18,64,384]{2,1,0:T(8,128)}, f32[18,64,384]{2,1,0:T(8,128)}, f32[18,64,384]{2,1,0:T(8,128)}, f32[18,64,384]{2,1,0:T(8,128)}) custom-call(s32[3,18]{1,0:T(4,128)} %pad_add_fusion.table_ref.refs_0_, f32[44]{0:T(128)} %concatenate.98.scale_ref.refs_1_, f32[18,64,384]{2,1,0:T(8,128)} %refs_2_.1, f32[18,64,384]{2,1,0:T(8,128)} %refs_3_.1, ...), custom_call_target="tpu_custom_call" | custom-call | flops 265420800 | bytes 17694720 | tf_op jit(solution)/shard_map/pallas_call | solution.py:1075
  435.8 4.6 %collective-permute-done.73.refs_8_ = bf16[3,192,384]{2,1,0:T(8,128)(2,1)S(1)} collective-permute-done((bf16[3,192,384]{2,1,0:T(8,128)(2,1)S(1)}, bf16[3,192,384]{2,1,0:T(8,128)(2,1)S(1)}, u32[]{:S(2)}, u32[]{:S(2)}) %collective-permute-start.73) | collective-permute-done | bytes 442400 | tf_op jit(solution)/shard_map/ppermute | solution.py:230
  441.9 7.2 %shard_map.202 = (f32[18,64,384]{2,1,0:T(8,128)}, f32[18,64,384]{2,1,0:T(8,128)}, f32[18,64,384]{2,1,0:T(8,128)}, f32[18,64,384]{2,1,0:T(8,128)}) custom-call(s32[3,18]{1,0:T(4,128)} %pad_add_fusion.table_ref.refs_0_, f32[44]{0:T(128)} %concatenate.98.scale_ref.refs_1_, ...), custom_call_target="tpu_custom_call", output_to_operand_aliasing={{0}: (10, {}), {1}: (11, {}), {2}: (12, {}), {3}: (13, {})} | custom-call | flops 265420800 | bytes 17694720 | tf_op jit(solution)/shard_map/pallas_call | solution.py:1145
  (332 shorter events, 198.1 us)
Async XLA Ops:
  2.3 23.0 %collective-permute-start = (bf16[18,64,384]{2,1,0:T(8,128)(2,1)S(1)}, bf16[18,64,384]{2,1,0:T(8,128)(2,1)S(1)}, u32[]{:S(2)}, u32[]{:S(2)}) collective-permute-start(bf16[18,64,384]{2,1,0:T(8,128)(2,1)S(1)} %convert_element_type.391.refs_0_), channel_id=1, source_target_pairs={{0,4},{1,3},{2,6},{3,1},{4,0},{5,7},{6,2},{7,5},{8,12},{9,11},{10,... | collective-permute-start | bytes 2654216 | tf_op jit(solution)/shard_map/ppermute | solution.py:1324
  5.3 23.5 %collective-permute-start.1 = (bf16[18,64,384]{2,1,0:T(8,128)(2,1)S(1)}, bf16[18,64,384]{2,1,0:T(8,128)(2,1)S(1)}, u32[]{:S(2)}, u32[]{:S(2)}) collective-permute-start(bf16[18,64,384]{2,1,0:T(8,128)(2,1)S(1)} %convert_element_type.391.refs_0_), channel_id=1, source_target_pairs={{0,2},{1,5},{2,0},{3,7},{4,6},{5,1},{6,4},{7,3},{8,10},{9,13},{10,... | collective-permute-start | bytes 2654216 | tf_op jit(solution)/shard_map/ppermute | solution.py:1325
  122.0 21.6 %collective-permute-start.23 = (bf16[4,384,384]{2,1,0:T(8,128)(2,1)}, bf16[4,384,384]{2,1,0:T(8,128)(2,1)}, u32[]{:S(2)}, u32[]{:S(2)}) collective-permute-start(bf16[4,384,384]{2,1,0:T(8,128)(2,1)} %pad_maximum_fusion.3.w0_ref.refs_4_), channel_id=1, source_target_pairs={{0,4},{1,3},{2,6},{3,1},{4,0},{5,7},{6,2},{7,5},{8,12},{9,11},{10,... | collective-permute-start | bytes 3538952 | tf_op jit(solution)/shard_map/ppermute | solution.py:230
  123.1 20.5 %collective-permute-start.27 = (bf16[4,384,384]{2,1,0:T(8,128)(2,1)}, bf16[4,384,384]{2,1,0:T(8,128)(2,1)}, u32[]{:S(2)}, u32[]{:S(2)}) collective-permute-start(bf16[4,384,384]{2,1,0:T(8,128)(2,1)} %pad_maximum_fusion.3.w0_ref.refs_4_), channel_id=1, source_target_pairs={{0,1},{1,0},{2,3},{3,2},{4,5},{5,4},{6,7},{7,6},{8,9},{9,8},{10,11... | collective-permute-start | bytes 3538952 | tf_op jit(solution)/shard_map/ppermute | solution.py:353
  123.1 20.5 %collective-permute-start.24 = (bf16[4,48,384]{2,1,0:T(8,128)(2,1)}, bf16[4,48,384]{2,1,0:T(8,128)(2,1)}, u32[]{:S(2)}, u32[]{:S(2)}) collective-permute-start(bf16[4,48,384]{2,1,0:T(8,128)(2,1)} %add_convert_fusion.17), channel_id=1, source_target_pairs={{0,8},{1,9},{2,10},{3,11},{4,12},{5,13},{6,14},{7,15},{8,16},{9,17... | collective-permute-start | bytes 442376 | tf_op jit(solution)/shard_map/ppermute | solution.py:230
  163.4 20.3 %collective-permute-start.30 = (bf16[4,384,384]{2,1,0:T(8,128)(2,1)}, bf16[4,384,384]{2,1,0:T(8,128)(2,1)}, u32[]{:S(2)}, u32[]{:S(2)}) collective-permute-start(bf16[4,384,384]{2,1,0:T(8,128)(2,1)} %pad_maximum_fusion.4.refs_0_), channel_id=1, source_target_pairs={{0,4},{1,3},{2,6},{3,1},{4,0},{5,7},{6,2},{7,5},{8,12},{9,11},{10,... | collective-permute-start | bytes 3538952 | tf_op jit(solution)/shard_map/ppermute | solution.py:230
  165.1 18.6 %collective-permute-start.31 = (bf16[4,384,384]{2,1,0:T(8,128)(2,1)}, bf16[4,384,384]{2,1,0:T(8,128)(2,1)}, u32[]{:S(2)}, u32[]{:S(2)}) collective-permute-start(bf16[4,384,384]{2,1,0:T(8,128)(2,1)} %pad_maximum_fusion.4.refs_0_), channel_id=1, source_target_pairs={{0,1},{1,0},{2,3},{3,2},{4,5},{5,4},{6,7},{7,6},{8,9},{9,8},{10,11... | collective-permute-start | bytes 3538952 | tf_op jit(solution)/shard_map/ppermute | solution.py:353
  215.5 23.9 %collective-permute-start.35 = (bf16[1024,768]{1,0:T(8,128)(2,1)}, bf16[1024,768]{1,0:T(8,128)(2,1)}, u32[]{:S(2)}, u32[]{:S(2)}) collective-permute-start(bf16[1024,768]{1,0:T(8,128)(2,1)} %get-tuple-element.482), channel_id=1, source_target_pairs={{0,1},{1,0},{2,3},{3,2},{4,5},{5,4},{6,7},{7,6},{8,9},{9,8},{10,11... | collective-permute-start | bytes 4718600 | tf_op jit(solution)/shard_map/ppermute | solution.py:353
  215.6 23.8 %collective-permute-start.34 = (bf16[4,384,384]{2,1,0:T(8,128)(2,1)}, bf16[4,384,384]{2,1,0:T(8,128)(2,1)}, u32[]{:S(2)}, u32[]{:S(2)}) collective-permute-start(bf16[4,384,384]{2,1,0:T(8,128)(2,1)} %add_convert_fusion.1), channel_id=1, source_target_pairs={{0,4},{1,3},{2,6},{3,1},{4,0},{5,7},{6,2},{7,5},{8,12},{9,11},{10,... | collective-permute-start | bytes 3538952 | tf_op jit(solution)/shard_map/ppermute | solution.py:230
  258.0 20.6 %collective-permute-start.40 = (bf16[5,768,384]{2,1,0:T(8,128)(2,1)}, bf16[5,768,384]{2,1,0:T(8,128)(2,1)}, u32[]{:S(2)}, u32[]{:S(2)}) collective-permute-start(bf16[5,768,384]{2,1,0:T(8,128)(2,1)} %get-tuple-element.416), channel_id=1, source_target_pairs={{0,1},{1,0},{2,3},{3,2},{4,5},{5,4},{6,7},{7,6},{8,9},{9,8},{10,11... | collective-permute-start | bytes 8847368 | tf_op jit(solution)/shard_map/ppermute | solution.py:353
  258.0 20.6 %collective-permute-start.37 = (bf16[4,48,384]{2,1,0:T(8,128)(2,1)}, bf16[4,48,384]{2,1,0:T(8,128)(2,1)}, u32[]{:S(2)}, u32[]{:S(2)}) collective-permute-start(bf16[4,48,384]{2,1,0:T(8,128)(2,1)} %get-tuple-element.413), channel_id=1, source_target_pairs={{0,8},{1,9},{2,10},{3,11},{4,12},{5,13},{6,14},{7,15},{8,16},{9,17... | collective-permute-start | bytes 442376 | tf_op jit(solution)/shard_map/ppermute | solution.py:230
  258.1 20.5 %collective-permute-start.38 = (bf16[4,48,384]{2,1,0:T(8,128)(2,1)}, bf16[4,48,384]{2,1,0:T(8,128)(2,1)}, u32[]{:S(2)}, u32[]{:S(2)}) collective-permute-start(bf16[4,48,384]{2,1,0:T(8,128)(2,1)} %get-tuple-element.414), channel_id=1, source_target_pairs={{0,16},{1,17},{2,18},{3,19},{4,20},{5,21},{6,22},{7,23},{8,24},{9,... | collective-permute-start | bytes 442376 | tf_op jit(solution)/shard_map/ppermute | solution.py:230
  259.7 18.9 %collective-permute-start.39 = (bf16[4,48,384]{2,1,0:T(8,128)(2,1)}, bf16[4,48,384]{2,1,0:T(8,128)(2,1)}, u32[]{:S(2)}, u32[]{:S(2)}) collective-permute-start(bf16[4,48,384]{2,1,0:T(8,128)(2,1)} %get-tuple-element.415), channel_id=1, source_target_pairs={{0,24},{1,25},{2,26},{3,27},{4,28},{5,29},{6,30},{7,31},{8,0},{9,1... | collective-permute-start | bytes 442376 | tf_op jit(solution)/shard_map/ppermute | solution.py:230
  283.6 22.1 %collective-permute-start.44 = (bf16[5,384,384]{2,1,0:T(8,128)(2,1)}, bf16[5,384,384]{2,1,0:T(8,128)(2,1)}, u32[]{:S(2)}, u32[]{:S(2)}) collective-permute-start(bf16[5,384,384]{2,1,0:T(8,128)(2,1)} %add_convert_fusion), channel_id=1, source_target_pairs={{0,2},{1,5},{2,0},{3,7},{4,6},{5,1},{6,4},{7,3},{8,10},{9,13},{10,... | collective-permute-start | bytes 4423688 | tf_op jit(solution)/shard_map/ppermute | solution.py:230
  283.7 22.0 %collective-permute-start.41 = (bf16[4,48,384]{2,1,0:T(8,128)(2,1)}, bf16[4,48,384]{2,1,0:T(8,128)(2,1)}, u32[]{:S(2)}, u32[]{:S(2)}) collective-permute-start(bf16[4,48,384]{2,1,0:T(8,128)(2,1)} %add_convert_fusion.12), channel_id=1, source_target_pairs={{0,8},{1,9},{2,10},{3,11},{4,12},{5,13},{6,14},{7,15},{8,16},{9,17... | collective-permute-start | bytes 442376 | tf_op jit(solution)/shard_map/ppermute | solution.py:230
  285.1 20.6 %collective-permute-start.42 = (bf16[4,48,384]{2,1,0:T(8,128)(2,1)}, bf16[4,48,384]{2,1,0:T(8,128)(2,1)}, u32[]{:S(2)}, u32[]{:S(2)}) collective-permute-start(bf16[4,48,384]{2,1,0:T(8,128)(2,1)} %add_convert_fusion.12), channel_id=1, source_target_pairs={{0,16},{1,17},{2,18},{3,19},{4,20},{5,21},{6,22},{7,23},{8,24},{9,... | collective-permute-start | bytes 442376 | tf_op jit(solution)/shard_map/ppermute | solution.py:230
  286.2 19.4 %collective-permute-start.43 = (bf16[4,48,384]{2,1,0:T(8,128)(2,1)}, bf16[4,48,384]{2,1,0:T(8,128)(2,1)}, u32[]{:S(2)}, u32[]{:S(2)}) collective-permute-start(bf16[4,48,384]{2,1,0:T(8,128)(2,1)} %add_convert_fusion.12), channel_id=1, source_target_pairs={{0,24},{1,25},{2,26},{3,27},{4,28},{5,29},{6,30},{7,31},{8,0},{9,1... | collective-permute-start | bytes 442376 | tf_op jit(solution)/shard_map/ppermute | solution.py:230
  353.4 27.2 %collective-permute-start.61 = (bf16[1024,768]{1,0:T(8,128)(2,1)}, bf16[1024,768]{1,0:T(8,128)(2,1)}, u32[]{:S(2)}, u32[]{:S(2)}) collective-permute-start(bf16[1024,768]{1,0:T(8,128)(2,1)} %get-tuple-element.497), channel_id=1, source_target_pairs={{0,1},{1,0},{2,3},{3,2},{4,5},{5,4},{6,7},{7,6},{8,9},{9,8},{10,11... | collective-permute-start | bytes 4718600 | tf_op jit(solution)/shard_map/ppermute | solution.py:353
  357.7 22.9 %collective-permute-start.54 = (bf16[3,192,384]{2,1,0:T(8,128)(2,1)S(1)}, bf16[3,192,384]{2,1,0:T(8,128)(2,1)S(1)}, u32[]{:S(2)}, u32[]{:S(2)}) collective-permute-start(bf16[3,192,384]{2,1,0:T(8,128)(2,1)S(1)} %get-tuple-element.474), channel_id=1, source_target_pairs={{0,2},{1,3},{2,0},{3,1},{4,6},{5,7},{6,4},{7,5},{8,10},{9,11},{10,... | collective-permute-start | bytes 1327112 | tf_op jit(solution)/shard_map/ppermute | solution.py:230
  359.4 21.2 %collective-permute-start.55 = (bf16[3,192,384]{2,1,0:T(8,128)(2,1)S(1)}, bf16[3,192,384]{2,1,0:T(8,128)(2,1)S(1)}, u32[]{:S(2)}, u32[]{:S(2)}) collective-permute-start(bf16[3,192,384]{2,1,0:T(8,128)(2,1)S(1)} %get-tuple-element.475), channel_id=1, source_target_pairs={{0,4},{1,5},{2,6},{3,7},{4,0},{5,1},{6,2},{7,3},{8,12},{9,13},{10,... | collective-permute-start | bytes 1327112 | tf_op jit(solution)/shard_map/ppermute | solution.py:230
  361.5 19.1 %collective-permute-start.56 = (bf16[3,192,384]{2,1,0:T(8,128)(2,1)S(1)}, bf16[3,192,384]{2,1,0:T(8,128)(2,1)S(1)}, u32[]{:S(2)}, u32[]{:S(2)}) collective-permute-start(bf16[3,192,384]{2,1,0:T(8,128)(2,1)S(1)} %get-tuple-element.476), channel_id=1, source_target_pairs={{0,6},{1,7},{2,4},{3,5},{4,2},{5,3},{6,0},{7,1},{8,14},{9,15},{10,... | collective-permute-start | bytes 1327112 | tf_op jit(solution)/shard_map/ppermute | solution.py:230
  397.2 19.4 %collective-permute-start.70 = (bf16[5,384,384]{2,1,0:T(8,128)(2,1)S(1)}, bf16[5,384,384]{2,1,0:T(8,128)(2,1)S(1)}, u32[]{:S(2)}, u32[]{:S(2)}) collective-permute-start(bf16[5,384,384]{2,1,0:T(8,128)(2,1)S(1)} %pad_maximum_fusion.1.refs_0_), channel_id=1, source_target_pairs={{0,2},{1,5},{2,0},{3,7},{4,6},{5,1},{6,4},{7,3},{8,10},{9,13},{10,... | collective-permute-start | bytes 4423688 | tf_op jit(solution)/shard_map/ppermute | solution.py:230
  420.7 19.6 %collective-permute-start.73 = (bf16[3,192,384]{2,1,0:T(8,128)(2,1)S(1)}, bf16[3,192,384]{2,1,0:T(8,128)(2,1)S(1)}, u32[]{:S(2)}, u32[]{:S(2)}) collective-permute-start(bf16[3,192,384]{2,1,0:T(8,128)(2,1)S(1)} %pad_maximum_fusion.11.refs_6_), channel_id=1, source_target_pairs={{0,4},{1,5},{2,6},{3,7},{4,0},{5,1},{6,2},{7,3},{8,12},{9,13},{10,... | collective-permute-start | bytes 1327112 | tf_op jit(solution)/shard_map/ppermute | solution.py:230
  420.7 19.6 %collective-permute-start.74 = (bf16[3,192,384]{2,1,0:T(8,128)(2,1)S(1)}, bf16[3,192,384]{2,1,0:T(8,128)(2,1)S(1)}, u32[]{:S(2)}, u32[]{:S(2)}) collective-permute-start(bf16[3,192,384]{2,1,0:T(8,128)(2,1)S(1)} %pad_maximum_fusion.11.refs_6_), channel_id=1, source_target_pairs={{0,6},{1,7},{2,4},{3,5},{4,2},{5,3},{6,0},{7,1},{8,14},{9,15},{10,... | collective-permute-start | bytes 1327112 | tf_op jit(solution)/shard_map/ppermute | solution.py:230
  (103 other events, 1147.3 us)
